TPU v7x, 32 devices: a whole 2x2x4 slice. The times are simulated.
32 devices in a mesh: ia: 4 (over y, core), ja: 8 (over z, x).
Axes of the slice: x: 2, y: 2, z: 4, core: 2. Of those that a mesh axis runs over, the one named last changes fastest.
Arguments:
- positions: float32 [3, 65536], P(None, 'ja')
- velocities: float32 [3, 65536], P(None, 'ja'), may hold values from -4 to 4
- accels: float32 [3, 65536], P(None, 'ja'), may hold values from -6 to 6
- jerks: float32 [3, 65536], P(None, 'ja'), may hold values from -6 to 6
- masses: float32 [65536], P('ja'), may hold values from 3.0517579e-06 to 7.6293945e-05
- levels: int32 [65536], P('ja'), may hold values from 0 to 7
- active: int32 [512], P('ia'), may hold values from 0 to 65535, as said below
Outputs:
- targets_new: float32 [12, 512], P(None, 'ia')
- stars_new: float32 [12, 65536], P(None, 'ja')
Inputs may be any that keep to these rules, and one draw needn't show every extreme that they name: `active`: 512 distinct star indices.
All inputs are finite; a program needn't handle non-finite values.
Results may differ from a plain program's by a relative error of at most 0.0001.
Values sent between devices are 32-bit elements; how exact they have to be, the bound alone decides.
No kernel may reach another device: no remote copies, remote signals or barrier semaphores. Data moves between devices by JAX's collectives and lax.ppermute only.
A program may use at most 64 MiB of HBM per device.

v0:
```python
import math

import jax
import jax.numpy as jnp
from jax import lax
from jax.sharding import PartitionSpec as P

softening_length = 0.01
base_step = 0.0625


def predict(state, elapsed):
    pos, vel, acc, jrk = (state[0:3], state[3:6], state[6:9], state[9:12])
    half = elapsed * elapsed * 0.5
    sixth = half * elapsed / 3.0
    pred_pos = pos + elapsed * vel + half * acc + sixth * jrk
    pred_vel = vel + elapsed * acc + half * jrk
    return (pred_pos, pred_vel)


def pair_terms(carry, source, tpos, tvel):
    spos, svel, smass = source
    position_offset = spos[:, None, :] - tpos[:, :, None]
    delta_v = svel[:, None, :] - tvel[:, :, None]
    radius_squared = jnp.sum(position_offset * position_offset, axis=0) + softening_length
    reciprocal_distance = lax.rsqrt(radius_squared)
    inv_sq = reciprocal_distance * reciprocal_distance
    weight = smass[None, :] * reciprocal_distance * inv_sq
    radial = 3.0 * jnp.sum(position_offset * delta_v, axis=0) * inv_sq
    acc_part = jnp.sum(weight[None] * position_offset, axis=-1)
    jerk_part = jnp.sum(weight[None] * (delta_v - radial[None] * position_offset), axis=-1)
    return carry + jnp.concatenate([acc_part, jerk_part], axis=0)


def correct(old, forces):
    x0, v0, a0, j0, step = (old[0:3], old[3:6], old[6:9], old[9:12], old[12:13])
    a1, j1 = (forces[0:3], forces[3:6])
    quad = step * step / 12.0
    v1 = v0 + 0.5 * step * (a0 + a1) + quad * (j0 - j1)
    x1 = x0 + 0.5 * step * (v0 + v1) + quad * (a0 - a1)
    return jnp.concatenate([x1, v1, a1, j1], axis=0)


def local(positions, velocities, accels, jerks, masses, levels, active):
    state = jnp.concatenate([positions, velocities, accels, jerks], axis=0)
    nlocal = state.shape[1]
    leading_entry = lax.axis_index("ja") * nlocal
    elapsed = base_step * jnp.exp2(-levels.astype(jnp.float32))
    pred_pos, pred_vel = predict(state, elapsed[None, :])
    offset = active - leading_entry
    inside = (offset >= 0) & (offset < nlocal)
    clipped = jnp.clip(offset, 0, nlocal - 1)
    mine_pred = jnp.where(
        inside[None, :], jnp.concatenate([pred_pos, pred_vel], axis=0)[:, clipped], 0.0
    )
    mine_old = jnp.where(
        inside[None, :], jnp.concatenate([state, elapsed[None, :]], axis=0)[:, clipped], 0.0
    )
    row_pred, row_old = lax.psum((mine_pred, mine_old), "ja")
    tpos, tvel = (row_pred[0:3], row_pred[3:6])
    width = math.gcd(nlocal, 2048)
    count = nlocal // width
    blocks = (
        jnp.moveaxis(pred_pos.reshape(3, count, width), 1, 0),
        jnp.moveaxis(pred_vel.reshape(3, count, width), 1, 0),
        masses.reshape(count, width),
    )

    def step_fn(carry, source):
        return (pair_terms(carry, source, tpos, tvel), None)

    init = jnp.zeros((6, active.shape[0]), jnp.float32)
    partial_forces, unused = lax.scan(step_fn, init, blocks)
    forces = lax.psum(partial_forces, "ja")
    targets_new = correct(row_old, forces)
    target_col = jnp.where(inside, offset, nlocal)
    placed = jnp.zeros_like(state).at[:, target_col].add(targets_new, mode="drop")
    marks = jnp.zeros((nlocal,), jnp.float32).at[target_col].add(1.0, mode="drop")
    placed_sum, marks_sum = lax.psum((placed, marks), "ia")
    stars_new = jnp.where(marks_sum[None, :] > 0.5, placed_sum, state)
    return (targets_new, stars_new)


def solution(mesh):
    return jax.shard_map(
        local,
        mesh=mesh,
        in_specs=(
            P(None, "ja"),
            P(None, "ja"),
            P(None, "ja"),
            P(None, "ja"),
            P("ja"),
            P("ja"),
            P("ia"),
        ),
        out_specs=(P(None, "ia"), P(None, "ja")),
        check_vma=False,
    )
```

profile of v0, /device:TPU:0, one launch (start us, length us, event | category | flops | bytes accessed | tf_op | source)
XLA Modules:
  0.0 208.8 jit_solution(13220002902892262794)
XLA Ops:
  7.2 0.7 compare_select_fusion
  7.9 0.7 compare_and_fusion
  8.5 0.8 reshape.58
  9.3 0.8 exponential_multiply_fusion
  10.1 1.2 multiply_add_fusion
  11.4 2.6 %copy.97 = f32[6,8192]{0,1:T(8,128)} copy(f32[6,8192]{1,0:T(8,128)S(1)} %pad_maximum_fusion.1) | data formatting | bytes 393216 | tf_op jit(solution)/shard_map/concatenate | solution.py:54
  14.0 2.8 %gather_fusion.1 = f32[128,6]{1,0:T(8,128)S(1)} fusion(f32[6,8192]{0,1:T(8,128)} %copy.97, s32[1024]{0:T(1024)S(1)} %pad_clamp_fusion), kind=kCustom, calls=%fused_computation.1 | custom fusion | bytes 6656 | tf_op jit(solution)/shard_map/gather | solution.py:54
  16.9 39.3 %psum.36 = f32[6,128]{0,1:T(8,128)S(1)} all-reduce(f32[6,128]{0,1:T(8,128)S(1)} %select_bitcast_fusion), channel_id=1, replica_groups=mesh['ia'=4,'ja'=8] {'ja'}, use_global_device_ids=true, to_apply=%region_1.2 | all-reduce | flops 768 | bytes 6144 | tf_op jit(solution)/shard_map/psum | solution.py:59
  56.5 9.8 %while.11 = (s32[]{:T(128)}, f32[6,128]{1,0:T(8,128)S(1)}, f32[4,2048]{1,0:T(4,128)S(1)}, f32[4,3,2048]{2,1,0:T(4,128)S(1)}, f32[3,128]{1,0:T(4,128)S(1)}, /*ind...) while((s32[]{:T(128)}, f32[6,128]{1,0:T(8,128)S(1)}, ...), condition=%wide.region_7.8_spmd.clone, body=%wide.region_2.7_spmd.clone.sunk | while | flops 12060163 | bytes 8628343 | solution.py:73
  56.5 0.9 fusion.17
  57.7 1.2 fusion.18
  58.9 0.9 fusion.17
  59.8 0.3 multiply_multiply_fusion.5
  60.1 1.2 fusion.18
  61.4 0.9 fusion.17
  62.3 0.3 multiply_multiply_fusion.5
  62.6 1.2 fusion.18
  63.8 0.9 fusion.17
  64.7 0.3 multiply_multiply_fusion.5
  65.0 1.2 fusion.18
  66.3 0.7 concatenate.17
  66.9 2.6 %copy.94 = f32[13,8192]{0,1:T(8,128)} copy(f32[13,8192]{1,0:T(8,128)S(1)} %concatenate.17) | data formatting | bytes 851968 | tf_op jit(solution)/shard_map/concatenate | solution.py:57
  69.6 2.8 %gather_fusion = f32[128,13]{1,0:T(8,128)S(1)} fusion(f32[13,8192]{0,1:T(8,128)} %copy.94, s32[1024]{0:T(1024)S(1)} %pad_clamp_fusion), kind=kCustom, calls=%fused_computation | custom fusion | bytes 13824 | tf_op jit(solution)/shard_map/gather | solution.py:57
  72.5 33.0 %all-reduce = (f32[6,128]{1,0:T(8,128)S(1)}, f32[13,128]{1,0:T(8,128)S(1)}) all-reduce(f32[6,128]{1,0:T(8,128)S(1)} %get-tuple-element.39, f32[13,128]{1,0:T(8,128)S(1)} %select_bitcast_fusion.1), channel_id=1, replica_groups=mesh['ia'=4,'ja'=8] {'ja'}, use_global_device_ids=true, to_apply=%region_8.9 | all-reduce | flops 2432 | bytes 19456 | tf_op jit(solution)/shard_map/psum | solution.py:74
  105.6 3.2 %scatter_custom_fusion.1 = f32[12,8192]{0,1:T(8,128)} fusion(s32[128]{0:T(128)S(1)} %get-tuple-element.144, f32[128,12]{1,0:T(8,128)S(1)} %copy.101, f32[]{:T(128)} %constant.11.clone.1), kind=kCustom, calls=%fused_computation.21 | custom fusion | flops 1536 | bytes 393220 | tf_op jit(solution)/shard_map/scatter-add | solution.py:77
  108.8 0.6 pad_maximum_fusion.2
  109.6 2.9 %copy.102 = f32[12,8192]{0,1:T(8,128)} copy(f32[12,8192]{1,0:T(8,128)S(1)} %pad_maximum_fusion) | data formatting | bytes 786432 | tf_op jit(solution)/shard_map/concatenate | solution.py:45
  112.5 1.3 scatter_custom_fusion
  113.7 11.6 %psum.38 = f32[8192]{0:T(1024)S(1)} all-reduce(f32[8192]{0:T(1024)S(1)} %scatter_custom_fusion), channel_id=1, replica_groups=mesh['ia'=4,'ja'=8] {'ia'}, use_global_device_ids=true, to_apply=%region_10.11 | all-reduce | flops 8192 | bytes 65536 | tf_op jit(solution)/shard_map/psum | solution.py:79
  125.3 66.9 %all-reduce.3.cloned.1.call-done = f32[12,8192]{0,1:T(8,128)} async-done(((f32[12,8192]{0,1:T(8,128)}), f32[12,8192]{0,1:T(8,128)}) %all-reduce.3.cloned.1.call-update) | async-done | bytes 393232 | tf_op jit(solution)/shard_map/psum | solution.py:79
  192.2 6.2 %broadcast_select_fusion = f32[12,8192]{0,1:T(8,128)} fusion(f32[12,8192]{0,1:T(8,128)} %all-reduce.3.cloned.1.call-done, f32[12,8192]{0,1:T(8,128)} %copy.102, pred[8192]{0:T(1024)(128)(4,1)S(1)} %broadcast_compare_fusion), kind=kLoop, calls=%fused_computation.23 | loop fusion | flops 98304 | bytes 1187840 | tf_op jit(solution)/shard_map/jit(_where)/select_n | solution.py:80
  198.4 3.5 %copy.103 = f32[12,8192]{1,0:T(8,128)} copy(f32[12,8192]{0,1:T(8,128)} %broadcast_select_fusion) | data formatting | bytes 786432
  (39 shorter events, 1.3 us)
Async XLA Ops:
  7.2 185.0 %all-reduce.3.cloned.1.call-start = ((), (), s32[]{:S(2)}) async-start(), calls=%async_computation | async-start | bytes 8388608 | tf_op jit(solution)/shard_map/psum | solution.py:79
  56.4 9.8 %copy-start = (f32[3,8192]{1,0:T(4,128)S(1)}, f32[3,8192]{1,0:T(4,128)}, u32[]{:S(2)}) copy-start(f32[3,8192]{1,0:T(4,128)} %param.12) | copy-start | bytes 294916
  56.4 9.8 %copy-start.1 = (f32[3,8192]{1,0:T(4,128)S(1)}, f32[3,8192]{1,0:T(4,128)}, u32[]{:S(2)}) copy-start(f32[3,8192]{1,0:T(4,128)} %param.10) | copy-start | bytes 294916
  56.4 9.8 %copy-start.2 = (f32[3,8192]{1,0:T(4,128)S(1)}, f32[3,8192]{1,0:T(4,128)}, u32[]{:S(2)}) copy-start(f32[3,8192]{1,0:T(4,128)} %param.11) | copy-start | bytes 294916
  56.4 9.8 %copy-start.3 = (f32[3,8192]{1,0:T(4,128)S(1)}, f32[3,8192]{1,0:T(4,128)}, u32[]{:S(2)}) copy-start(f32[3,8192]{1,0:T(4,128)} %param.9) | copy-start | bytes 294916
Sparse Core Ops, SparseCore 0:
  108.9 83.1 all-reduce.2
where the time goes:
time: 209 us
  blocking collectives  83.8 us (40%)
  waiting for transfers between devices  66.9 us (32%)
  other arithmetic  24.4 us (12%)
  local copies, waits for them, and re-layouts  19.3 us (9%)
  between operations  14.2 us (7%)
    psum x1, waiting for transfers between devices, local(): placed_sum, marks_sum = lax.psum((placed, marks), 'ia')  66.9 us
    psum x1, blocking collectives, local(): row_pred, row_old = lax.psum((mine_pred, mine_old), 'ja')  39.3 us
    psum x1, blocking collectives, local(): forces = lax.psum(partial_forces, 'ja')  33 us
    psum x1, blocking collectives, local(): placed_sum, marks_sum = lax.psum((placed, marks), 'ia')  11.6 us
    select_n x1, other arithmetic, local(): stars_new = jnp.where(marks_sum[None, :] > 0.5, placed_sum, state)  6.2 us
    reduce_sum x4, other arithmetic, pair_terms(): acc_part = jnp.sum(weight[None] * position_offset, axis=-1)  4.7 us
  transfers between devices with their start and end apart: 1, of which 1 were waited for; matrix products, arithmetic and copies ran while one was open for 2% of the time, Pallas kernels for 0%

commit v1 on v0

v1 whole, which is shorter than its diff:
```python
import functools

import jax
import jax.numpy as jnp
from jax import lax
from jax.experimental import pallas as pl
from jax.experimental.pallas import tpu as pltpu
from jax.sharding import PartitionSpec as P

softening_length = 0.01
base_step = 0.0625
LANES = 128
f32 = jnp.float32
VMEM = pl.BlockSpec(memory_space=pltpu.VMEM)
HBM = pl.BlockSpec(memory_space=pltpu.HBM)
PARAMS = pltpu.CompilerParams(vmem_limit_bytes=24 * 1024 * 1024)


def elapsed_of(levels):
    return (128 >> levels).astype(f32) * (base_step / 128.0)


def predict(pos, vel, acc, jrk, elapsed):
    half = elapsed * elapsed * 0.5
    sixth = half * elapsed / 3.0
    pred_pos = pos + elapsed * vel + half * acc + sixth * jrk
    pred_vel = vel + elapsed * acc + half * jrk
    return (pred_pos, pred_vel)


def correct(x0, v0, a0, j0, step, a1, j1):
    quad = step * step / 12.0
    v1 = v0 + 0.5 * step * (a0 + a1) + quad * (j0 - j1)
    x1 = x0 + 0.5 * step * (v0 + v1) + quad * (a0 - a1)
    return (x1, v1)


def tile(t):
    return slice(t * LANES, (t + 1) * LANES)


def gather_kernel(*refs):
    given, out, held, sems, kept = (refs[:6], refs[6], refs[7], refs[8], refs[9:])
    copies = [
        pltpu.make_async_copy(a, b, sems.at[n]) for n, (a, b) in enumerate(zip(given, kept))
    ]
    for copy in copies:
        copy.start()
    for copy in copies:
        copy.wait()
    pos, vel, acc, jrk, levels, active = kept
    groups = levels.shape[0]
    offset = active[...] - lax.axis_index("ja") * (groups * LANES)
    group = jnp.broadcast_to(offset >> 7, (8, LANES))
    lane = jnp.broadcast_to(offset & (LANES - 1), (8, LANES))
    held[0:3, :] = pos[...]
    held[3:6, :] = vel[...]
    held[6:9, :] = acc[...]
    held[9:12, :] = jrk[...]
    elapsed = elapsed_of(levels[...])
    for t in range(groups):
        held[12:16, tile(t)] = jnp.broadcast_to(elapsed[t : t + 1], (4, LANES))
    low = jnp.zeros((8, LANES), f32)
    high = jnp.zeros((8, LANES), f32)
    for t in range(groups):
        here = group == t
        low = jnp.where(here, jnp.take_along_axis(held[0:8, tile(t)], lane, axis=1), low)
        high = jnp.where(here, jnp.take_along_axis(held[8:16, tile(t)], lane, axis=1), high)
    out[0:8, :] = low
    out[8:16, :] = high


def force_kernel(columns, *refs):
    gathered, refs = (refs[:columns], refs[columns:])
    pos, vel, acc, jrk, levels, masses, active, packed, old, sources, targets, sums = refs
    groups = levels.shape[0]
    ntarget = active.shape[1]
    state = gathered[0][...]
    for block in gathered[1:]:
        state = state + block[...]
    old[...] = state
    tpos, tvel = predict(state[0:3], state[3:6], state[6:9], state[9:12], state[12:13])
    columns = jnp.transpose(
        jnp.concatenate([tpos, tvel, jnp.zeros((LANES - 6, ntarget), f32)], axis=0)
    )
    for c in range(6):
        targets[c] = jnp.broadcast_to(columns[:, c : c + 1], (ntarget, LANES))
    elapsed = elapsed_of(levels[...])
    for t in range(groups):
        spos, svel = predict(
            pos[:, tile(t)], vel[:, tile(t)], acc[:, tile(t)], jrk[:, tile(t)], elapsed[t : t + 1]
        )
        for c in range(3):
            sources[t, c] = jnp.broadcast_to(spos[c : c + 1], (8, LANES))
            sources[t, 3 + c] = jnp.broadcast_to(svel[c : c + 1], (8, LANES))
        sources[t, 6] = jnp.broadcast_to(masses[t : t + 1, :], (8, LANES))

    def one_group(g, unused):
        rows = pl.ds(pl.multiple_of(g * 8, 8), 8)
        tx, ty, tz, tu, tv, tw = (targets[c, rows, :] for c in range(6))

        def one_tile(t, carry):
            dx, dy, dz = (sources[t, 0] - tx, sources[t, 1] - ty, sources[t, 2] - tz)
            du, dv, dw = (sources[t, 3] - tu, sources[t, 4] - tv, sources[t, 5] - tw)
            r2 = dx * dx + dy * dy + dz * dz + softening_length
            inv = lax.rsqrt(r2)
            inv_sq = inv * inv
            weight = sources[t, 6] * inv * inv_sq
            radial = (dx * du + dy * dv + dz * dw) * inv_sq
            px, py, pz = (weight * dx, weight * dy, weight * dz)
            ax, ay, az, jx, jy, jz, kx, ky, kz = carry
            return (
                ax + px,
                ay + py,
                az + pz,
                jx + weight * du,
                jy + weight * dv,
                jz + weight * dw,
                kx + radial * px,
                ky + radial * py,
                kz + radial * pz,
            )

        zero = jnp.zeros((8, LANES), f32)
        ax, ay, az, jx, jy, jz, kx, ky, kz = lax.fori_loop(
            0, groups, one_tile, (zero,) * 9, unroll=16
        )
        for c, value in enumerate((ax, ay, az, jx - 3.0 * kx, jy - 3.0 * ky, jz - 3.0 * kz)):
            sums[c, rows, :] = value
        return unused

    lax.fori_loop(0, ntarget // 8, one_group, 0)
    lane = lax.broadcasted_iota(jnp.int32, (ntarget, LANES), 1)
    table = jnp.zeros((ntarget, LANES), f32)
    for c in range(6):
        table = jnp.where(lane == c, jnp.sum(sums[c], axis=1, keepdims=True), table)
    table = jnp.transpose(table)[0:8]
    row = lax.broadcasted_iota(jnp.int32, (8, ntarget), 0)
    table = jnp.where(row == 6, active[...].astype(f32), table)
    for k in range(packed.shape[0]):
        packed[k] = table


def finish_kernel(
    rows, columns, everyone, old, pos, vel, acc, jrk, levels, targets_new, stars_new
):
    groups = levels.shape[0]
    ntarget = everyone.shape[-1]
    me = lax.axis_index("ia")
    base = lax.axis_index("ja") * (groups * LANES)

    forces, where_hi, where_lo = ([], [], [])
    mine = jnp.zeros((8, ntarget), f32)
    for r in range(rows):
        total = everyone[r * columns]
        for c in range(1, columns):
            total = total + everyone[r * columns + c]
        forces.append(total)
        mine = jnp.where(me == r, total, mine)
        offset = everyone[r * columns][6:7].astype(jnp.int32) - base
        where_hi.append(offset >> 7)
        where_lo.append(offset & (LANES - 1))

    o = old[...]
    x1, v1 = correct(o[0:3], o[3:6], o[6:9], o[9:12], o[12:13], mine[0:3], mine[3:6])
    targets_new[0:3, :] = x1
    targets_new[3:6, :] = v1
    targets_new[6:12, :] = mine[0:6]

    group = lax.broadcasted_iota(jnp.int32, (groups, ntarget), 0)
    lane = lax.broadcasted_iota(jnp.int32, (LANES, ntarget), 0)
    number = lax.broadcasted_iota(jnp.int32, (groups, ntarget), 1).astype(f32) + 1.0
    spot = jnp.zeros((groups, LANES), f32)
    part = jnp.zeros((groups, LANES), f32)
    for r in range(rows):
        hit = group == where_hi[r]
        side = (lane == where_lo[r]).astype(jnp.bfloat16)
        found = lax.dot_general(
            jnp.where(hit, number, 0.0).astype(jnp.bfloat16),
            side,
            (((1,), (1,)), ((), ())),
            preferred_element_type=f32,
        )
        part = jnp.where(found > 0.5, float(r), part)
        spot = spot + found
    present = spot > 0.5
    slot = jnp.where(present, spot - 1.0, 0.0).astype(jnp.int32)
    part = jnp.where(present, part, -1.0)
    elapsed = elapsed_of(levels[...])
    for t in range(groups):
        lanes = jnp.broadcast_to(slot[t : t + 1], (8, LANES))
        holder = jnp.broadcast_to(part[t : t + 1], (8, LANES))
        new = jnp.zeros((8, LANES), f32)
        for r in range(rows):
            new = jnp.where(holder == float(r), jnp.take_along_axis(forces[r], lanes, axis=1), new)
        there = holder[0:3] > -0.5
        x0, v0, a0, j0 = (pos[:, tile(t)], vel[:, tile(t)], acc[:, tile(t)], jrk[:, tile(t)])
        a1, j1 = (new[0:3], new[3:6])
        x1, v1 = correct(x0, v0, a0, j0, elapsed[t : t + 1], a1, j1)
        stars_new[0:3, tile(t)] = jnp.where(there, x1, x0)
        stars_new[3:6, tile(t)] = jnp.where(there, v1, v0)
        stars_new[6:9, tile(t)] = jnp.where(there, a1, a0)
        stars_new[9:12, tile(t)] = jnp.where(there, j1, j0)


def local(rows, columns, positions, velocities, accels, jerks, masses, levels, active):
    nlocal = positions.shape[1]
    ntarget = active.shape[0]
    groups = nlocal // LANES
    levels = levels.reshape(groups, LANES)
    masses = masses.reshape(groups, LANES)
    active = active.reshape(1, ntarget)
    state = (positions, velocities, accels, jerks)

    mine = pl.pallas_call(
        gather_kernel,
        out_shape=jax.ShapeDtypeStruct((16, ntarget), f32),
        in_specs=[HBM] * 6,
        out_specs=VMEM,
        scratch_shapes=[
            pltpu.VMEM((16, nlocal), f32),
            pltpu.SemaphoreType.DMA((6,)),
            *(pltpu.VMEM(x.shape, x.dtype) for x in (*state, levels, active)),
        ],
        compiler_params=pltpu.CompilerParams(vmem_limit_bytes=60 * 1024 * 1024),
        name="gather",
    )(*state, levels, active)
    gathered = [mine]
    for k in range(1, columns):
        ring = [(c, (c + k) % columns) for c in range(columns)]
        gathered.append(lax.ppermute(mine, "ja", ring))
    packed, old = pl.pallas_call(
        functools.partial(force_kernel, columns),
        out_shape=(
            jax.ShapeDtypeStruct((rows * columns, 8, ntarget), f32),
            jax.ShapeDtypeStruct((16, ntarget), f32),
        ),
        in_specs=[VMEM] * (columns + 7),
        out_specs=(VMEM, VMEM),
        scratch_shapes=[
            pltpu.VMEM((groups, 7, 8, LANES), f32),
            pltpu.VMEM((6, ntarget, LANES), f32),
            pltpu.VMEM((6, ntarget, LANES), f32),
        ],
        compiler_params=PARAMS,
        name="forces",
    )(*gathered, *state, levels, masses, active)
    everyone = lax.all_to_all(packed, ("ia", "ja"), 0, 0)
    return pl.pallas_call(
        functools.partial(finish_kernel, rows, columns),
        out_shape=(
            jax.ShapeDtypeStruct((12, ntarget), f32),
            jax.ShapeDtypeStruct((12, nlocal), f32),
        ),
        in_specs=[VMEM] * 7,
        out_specs=(VMEM, VMEM),
        compiler_params=PARAMS,
        name="finish",
    )(everyone, old, *state, levels)


def solution(mesh):
    rows, columns = mesh.shape["ia"], mesh.shape["ja"]

    def body(*args):
        return local(rows, columns, *args)

    return jax.shard_map(
        body,
        mesh=mesh,
        in_specs=(
            P(None, "ja"),
            P(None, "ja"),
            P(None, "ja"),
            P(None, "ja"),
            P("ja"),
            P("ja"),
            P("ia"),
        ),
        out_specs=(P(None, "ia"), P(None, "ja")),
        check_vma=False,
    )
```

time: 209 us -> 41.1 us (0.20)
  blocking collectives: 83.8 us -> 10.6 us
  waiting for transfers between devices: 66.9 us -> 5.43 us
  other arithmetic: 24.4 us -> 0 us
  local copies, waits for them, and re-layouts: 19.3 us -> 1.48 us
  between operations: 14.2 us -> 0.74 us
  starting transfers between devices: 0.04 us -> 12.4 us
  Pallas kernels: 0 us -> 10.2 us
    psum x3 -> x0, blocking collectives: 83.8 us -> none  [the longest x1 39.3 us: local(): row_pred, row_old = lax.psum((mine_pred, mine_old), 'ja')]
    psum x1 -> x0, waiting for transfers between devices: 66.9 us -> none  [local(): placed_sum, marks_sum = lax.psum((placed, marks), 'ia')]
    ppermute x0 -> x7, starting transfers between devices: none -> 12.4 us  [local(): gathered.append(lax.ppermute(mine, 'ja', ring))]
    all_to_all x0 -> x1, blocking collectives: none -> 10.6 us  [local(): everyone = lax.all_to_all(packed, ('ia', 'ja'), 0, 0)]
    pallas_call x0 -> x3, Pallas kernels: none -> 10.2 us  [the longest x1 6.54 us: local(): pl.pallas_call(functools.partial(force_kernel, columns), out_shape=(jax.S...]
    concatenate x5 -> x0, local copies, waits for them, and re-layouts: 8.88 us -> none  [the longest x2 3.27 us: local(): jnp.concatenate([state, elapsed[None, :]], axis=0)[:, clipped]]
    reduce_sum x8 -> x0, other arithmetic: 8.11 us -> none  [the longest x4 4.7 us: pair_terms(): acc_part = jnp.sum(weight[None] * position_offset, axis=-1)]
    select_n x4 -> x0, other arithmetic: 6.96 us -> none  [the longest x1 6.2 us: local(): stars_new = jnp.where(marks_sum[None, :] > 0.5, placed_sum, state)]
  transfers between devices with their start and end apart: 1 -> 7, of which waited for: 1 -> 3; matrix products, arithmetic and copies ran while one was open for 2% -> 0% of each run, Pallas kernels for 0% -> 0%
where the time goes in v1:
time: 41.1 us; the launch traced here: 40.8 us
  starting transfers between devices  12.4 us (30%)
  blocking collectives  10.6 us (26%)
  Pallas kernels  10.2 us (25%)
  waiting for transfers between devices  5.43 us (13%)
  local copies, waits for them, and re-layouts  1.48 us (4%)
  between operations  0.74 us (2%)
    ppermute x7, starting transfers between devices, local(): gathered.append(lax.ppermute(mine, 'ja', ring))  12.4 us
    all_to_all x1, blocking collectives, local(): everyone = lax.all_to_all(packed, ('ia', 'ja'), 0, 0)  10.6 us
    pallas_call x1, Pallas kernels, local(): pl.pallas_call(functools.partial(force_kernel, columns), out_shape=(jax.S...  6.54 us
    ppermute x7, waiting for transfers between devices, local(): gathered.append(lax.ppermute(mine, 'ja', ring))  5.43 us
    pallas_call x1, Pallas kernels, local(): pl.pallas_call(gather_kernel, out_shape=jax.ShapeDtypeStruct((16, ntarget...  2.07 us
    pallas_call x1, Pallas kernels, local(): pl.pallas_call(functools.partial(finish_kernel, rows, columns), out_shape...  1.58 us
    unnamed x16, local copies, waits for them, and re-layouts  1.48 us
  transfers between devices with their start and end apart: 7, of which 3 were waited for; matrix products, arithmetic and copies ran while one was open for 0% of the time, Pallas kernels for 0%

profile of v1, /device:TPU:0, one launch (start us, length us, event | category | flops | bytes accessed | tf_op | source)
XLA Modules:
  0.0 40.8 jit_solution(6106106234803479012)
XLA Ops:
  0.6 0.0 copy-start
  0.6 0.0 copy-start.1
  0.7 0.0 copy-start.2
  0.7 0.0 copy-start.3
  0.7 0.0 copy-start.4
  0.7 2.1 %gather.1.refs_0_ = f32[16,128]{1,0:T(8,128)} custom-call(f32[3,8192]{1,0:T(4,128)} %pos.1, f32[3,8192]{1,0:T(4,128)} %vel.1, f32[3,8192]{1,0:T(4,128)} %acc.1, f32[3,8192]{1,0:T(4,128)} %jrk.1, s32[64,128]{1,0:T(8,128)} %bitcast.3, s32[1,128]{1,0:T(1,128)} %bitcast.7), custom_call_target="tpu_custom_call" | custom-call | tf_op jit(solution)/shard_map/gather/pallas_call | solution.py:215
  2.8 0.0 copy-start.7
  2.8 6.0 %collective-permute-start.6 = (f32[16,128]{1,0:T(8,128)}, f32[16,128]{1,0:T(8,128)S(1)}, u32[]{:S(2)}, u32[]{:S(2)}) collective-permute-start(f32[16,128]{1,0:T(8,128)} %gather.1.refs_0_), channel_id=1, source_target_pairs={{0,7},{1,0},{2,1},{3,2},{4,3},{5,4},{6,5},{7,6},{8,15},{9,8},{10,9... | collective-permute-start | bytes 24584 | tf_op jit(solution)/shard_map/ppermute | solution.py:231
  8.8 0.4 %collective-permute-start.5 = (f32[16,128]{1,0:T(8,128)}, f32[16,128]{1,0:T(8,128)S(1)}, u32[]{:S(2)}, u32[]{:S(2)}) collective-permute-start(f32[16,128]{1,0:T(8,128)} %gather.1.refs_0_), channel_id=1, source_target_pairs={{0,6},{1,7},{2,0},{3,1},{4,2},{5,3},{6,4},{7,5},{8,14},{9,15},{10,... | collective-permute-start | bytes 24584 | tf_op jit(solution)/shard_map/ppermute | solution.py:231
  9.3 0.0 collective-permute-start.4
  9.3 3.0 %collective-permute-start.3 = (f32[16,128]{1,0:T(8,128)}, f32[16,128]{1,0:T(8,128)S(1)}, u32[]{:S(2)}, u32[]{:S(2)}) collective-permute-start(f32[16,128]{1,0:T(8,128)} %gather.1.refs_0_), channel_id=1, source_target_pairs={{0,4},{1,5},{2,6},{3,7},{4,0},{5,1},{6,2},{7,3},{8,12},{9,13},{10,... | collective-permute-start | bytes 24584 | tf_op jit(solution)/shard_map/ppermute | solution.py:231
  12.3 0.0 collective-permute-start.2
  12.3 0.0 collective-permute-done.6.refs_7_
  12.3 1.8 %collective-permute-start.1 = (f32[16,128]{1,0:T(8,128)}, f32[16,128]{1,0:T(8,128)S(1)}, u32[]{:S(2)}, u32[]{:S(2)}) collective-permute-start(f32[16,128]{1,0:T(8,128)} %gather.1.refs_0_), channel_id=1, source_target_pairs={{0,2},{1,3},{2,4},{3,5},{4,6},{5,7},{6,0},{7,1},{8,10},{9,11},{10,... | collective-permute-start | bytes 24584 | tf_op jit(solution)/shard_map/ppermute | solution.py:231
  14.1 0.0 collective-permute-done.5.refs_6_
  14.1 1.1 %collective-permute-start = (f32[16,128]{1,0:T(8,128)}, f32[16,128]{1,0:T(8,128)S(1)}, u32[]{:S(2)}, u32[]{:S(2)}) collective-permute-start(f32[16,128]{1,0:T(8,128)} %gather.1.refs_0_), channel_id=1, source_target_pairs={{0,1},{1,2},{2,3},{3,4},{4,5},{5,6},{6,7},{7,0},{8,9},{9,10},{10,1... | collective-permute-start | bytes 24584 | tf_op jit(solution)/shard_map/ppermute | solution.py:231
  15.2 0.0 collective-permute-done.4.refs_5_
  15.2 0.0 collective-permute-done.3.refs_4_
  15.2 2.7 %collective-permute-done.2.refs_3_ = f32[16,128]{1,0:T(8,128)S(1)} collective-permute-done((f32[16,128]{1,0:T(8,128)}, f32[16,128]{1,0:T(8,128)S(1)}, u32[]{:S(2)}, u32[]{:S(2)}) %collective-permute-start.2) | collective-permute-done | bytes 8224 | tf_op jit(solution)/shard_map/ppermute | solution.py:231
  17.9 1.0 %collective-permute-done.1.refs_2_ = f32[16,128]{1,0:T(8,128)S(1)} collective-permute-done((f32[16,128]{1,0:T(8,128)}, f32[16,128]{1,0:T(8,128)S(1)}, u32[]{:S(2)}, u32[]{:S(2)}) %collective-permute-start.1) | collective-permute-done | bytes 8224 | tf_op jit(solution)/shard_map/ppermute | solution.py:231
  18.9 1.7 %collective-permute-done.refs_1_ = f32[16,128]{1,0:T(8,128)S(1)} collective-permute-done((f32[16,128]{1,0:T(8,128)}, f32[16,128]{1,0:T(8,128)S(1)}, u32[]{:S(2)}, u32[]{:S(2)}) %collective-permute-start) | collective-permute-done | bytes 8224 | tf_op jit(solution)/shard_map/ppermute | solution.py:231
  20.7 0.0 copy-done
  20.7 0.0 copy-done.1
  20.7 0.0 copy-done.2
  20.7 0.0 copy-done.3
  20.7 0.0 copy-done.4
  20.7 0.0 copy-start.5
  20.7 0.7 %copy-done.5 = f32[16,128]{1,0:T(8,128)S(1)} copy-done((f32[16,128]{1,0:T(8,128)S(1)}, f32[16,128]{1,0:T(8,128)}, u32[]{:S(2)}) %copy-start.5) | copy-done | bytes 8216
  21.4 0.8 %copy-done.6 = f32[8192]{0:T(1024)S(1)} copy-done((f32[8192]{0:T(1024)S(1)}, f32[8192]{0:T(1024)}, u32[]{:S(2)}) %copy-start.6) | copy-done | bytes 32792
  22.2 6.5 %forces.1 = (f32[32,8,128]{2,1,0:T(8,128)S(1)}, f32[16,128]{1,0:T(8,128)S(1)}) custom-call(f32[16,128]{1,0:T(8,128)S(1)} %copy-done.5, f32[16,128]{1,0:T(8,128)S(1)} %collective-permute-done.refs_1_, f32[16,128]{1,0:T(8,128)S(1)} %collective-permute-done.1.refs_2_, f32[16,128]{1,0:T(8,128)S(1)} %collective-permute-done.2.refs_3_, ...), custom_call_target="tpu_custom_call" | custom-call | tf_op jit(solution)/shard_map/forces/pallas_call | solution.py:232
  28.7 10.6 %all_to_all.5.everyone = f32[32,8,128]{2,1,0:T(8,128)S(1)} all-to-all(f32[32,8,128]{2,1,0:T(8,128)S(1)} %get-tuple-element.4), channel_id=1, replica_groups=mesh['ia'=4,'ja'=8] {'ia','ja'}, dimensions={0} | all-to-all | bytes 262144 | tf_op jit(solution)/shard_map/all_to_all | solution.py:248
  39.3 1.6 %finish.1 = (f32[12,128]{1,0:T(8,128)}, f32[12,8192]{1,0:T(8,128)}) custom-call(f32[32,8,128]{2,1,0:T(8,128)S(1)} %all_to_all.5.everyone, f32[16,128]{1,0:T(8,128)S(1)} %get-tuple-element.5.old, f32[3,8192]{1,0:T(4,128)S(1)} %copy-done, f32[3,8192]{1,0:T(4,128)S(1)} %copy-done.1, f32[3,8192]{1,0:T(4,128)S(1)} %copy-done.2, f32[3,8192]{1,0:T(4,128)S(1)} %copy-done.3, ...), custom_call_target="tpu_custom_call" | custom-call | tf_op jit(solution)/shard_map/finish/pallas_call | solution.py:249
  (2 shorter events, 0.0 us)
Async XLA Ops:
  0.6 20.0 %copy-start = (f32[3,8192]{1,0:T(4,128)S(1)}, f32[3,8192]{1,0:T(4,128)}, u32[]{:S(2)}) copy-start(f32[3,8192]{1,0:T(4,128)} %pos.1) | copy-start | bytes 294916
  0.6 20.0 %copy-start.1 = (f32[3,8192]{1,0:T(4,128)S(1)}, f32[3,8192]{1,0:T(4,128)}, u32[]{:S(2)}) copy-start(f32[3,8192]{1,0:T(4,128)} %vel.1) | copy-start | bytes 294916
  0.7 20.0 %copy-start.2 = (f32[3,8192]{1,0:T(4,128)S(1)}, f32[3,8192]{1,0:T(4,128)}, u32[]{:S(2)}) copy-start(f32[3,8192]{1,0:T(4,128)} %acc.1) | copy-start | bytes 294916
  0.7 20.0 %copy-start.3 = (f32[3,8192]{1,0:T(4,128)S(1)}, f32[3,8192]{1,0:T(4,128)}, u32[]{:S(2)}) copy-start(f32[3,8192]{1,0:T(4,128)} %jrk.1) | copy-start | bytes 294916
  0.7 20.0 %copy-start.4 = (s32[8192]{0:T(1024)S(1)}, s32[8192]{0:T(1024)}, u32[]{:S(2)}) copy-start(s32[8192]{0:T(1024)} %param.12) | copy-start | bytes 98308
  2.8 17.9 %copy-start.7 = (s32[128]{0:T(128)S(1)}, s32[128]{0:T(128)}, u32[]{:S(2)}) copy-start(s32[128]{0:T(128)} %param.13) | copy-start | bytes 1540
  2.8 9.5 %collective-permute-start.6 = (f32[16,128]{1,0:T(8,128)}, f32[16,128]{1,0:T(8,128)S(1)}, u32[]{:S(2)}, u32[]{:S(2)}) collective-permute-start(f32[16,128]{1,0:T(8,128)} %gather.1.refs_0_), channel_id=1, source_target_pairs={{0,7},{1,0},{2,1},{3,2},{4,3},{5,4},{6,5},{7,6},{8,15},{9,8},{10,9... | collective-permute-start | bytes 24584 | tf_op jit(solution)/shard_map/ppermute | solution.py:231
  8.8 5.3 %collective-permute-start.5 = (f32[16,128]{1,0:T(8,128)}, f32[16,128]{1,0:T(8,128)S(1)}, u32[]{:S(2)}, u32[]{:S(2)}) collective-permute-start(f32[16,128]{1,0:T(8,128)} %gather.1.refs_0_), channel_id=1, source_target_pairs={{0,6},{1,7},{2,0},{3,1},{4,2},{5,3},{6,4},{7,5},{8,14},{9,15},{10,... | collective-permute-start | bytes 24584 | tf_op jit(solution)/shard_map/ppermute | solution.py:231
  9.3 6.0 %collective-permute-start.4 = (f32[16,128]{1,0:T(8,128)}, f32[16,128]{1,0:T(8,128)S(1)}, u32[]{:S(2)}, u32[]{:S(2)}) collective-permute-start(f32[16,128]{1,0:T(8,128)} %gather.1.refs_0_), channel_id=1, source_target_pairs={{0,5},{1,6},{2,7},{3,0},{4,1},{5,2},{6,3},{7,4},{8,13},{9,14},{10,... | collective-permute-start | bytes 24584 | tf_op jit(solution)/shard_map/ppermute | solution.py:231
  9.3 6.0 %collective-permute-start.3 = (f32[16,128]{1,0:T(8,128)}, f32[16,128]{1,0:T(8,128)S(1)}, u32[]{:S(2)}, u32[]{:S(2)}) collective-permute-start(f32[16,128]{1,0:T(8,128)} %gather.1.refs_0_), channel_id=1, source_target_pairs={{0,4},{1,5},{2,6},{3,7},{4,0},{5,1},{6,2},{7,3},{8,12},{9,13},{10,... | collective-permute-start | bytes 24584 | tf_op jit(solution)/shard_map/ppermute | solution.py:231
  12.3 5.7 %collective-permute-start.2 = (f32[16,128]{1,0:T(8,128)}, f32[16,128]{1,0:T(8,128)S(1)}, u32[]{:S(2)}, u32[]{:S(2)}) collective-permute-start(f32[16,128]{1,0:T(8,128)} %gather.1.refs_0_), channel_id=1, source_target_pairs={{0,3},{1,4},{2,5},{3,6},{4,7},{5,0},{6,1},{7,2},{8,11},{9,12},{10,... | collective-permute-start | bytes 24584 | tf_op jit(solution)/shard_map/ppermute | solution.py:231
  12.3 6.7 %collective-permute-start.1 = (f32[16,128]{1,0:T(8,128)}, f32[16,128]{1,0:T(8,128)S(1)}, u32[]{:S(2)}, u32[]{:S(2)}) collective-permute-start(f32[16,128]{1,0:T(8,128)} %gather.1.refs_0_), channel_id=1, source_target_pairs={{0,2},{1,3},{2,4},{3,5},{4,6},{5,7},{6,0},{7,1},{8,10},{9,11},{10,... | collective-permute-start | bytes 24584 | tf_op jit(solution)/shard_map/ppermute | solution.py:231
  14.1 6.6 %collective-permute-start = (f32[16,128]{1,0:T(8,128)}, f32[16,128]{1,0:T(8,128)S(1)}, u32[]{:S(2)}, u32[]{:S(2)}) collective-permute-start(f32[16,128]{1,0:T(8,128)} %gather.1.refs_0_), channel_id=1, source_target_pairs={{0,1},{1,2},{2,3},{3,4},{4,5},{5,6},{6,7},{7,0},{8,9},{9,10},{10,1... | collective-permute-start | bytes 24584 | tf_op jit(solution)/shard_map/ppermute | solution.py:231
  20.7 0.7 %copy-start.5 = (f32[16,128]{1,0:T(8,128)S(1)}, f32[16,128]{1,0:T(8,128)}, u32[]{:S(2)}) copy-start(f32[16,128]{1,0:T(8,128)} %gather.1.refs_0_) | copy-start | bytes 24580
  21.4 0.8 %copy-start.6 = (f32[8192]{0:T(1024)S(1)}, f32[8192]{0:T(1024)}, u32[]{:S(2)}) copy-start(f32[8192]{0:T(1024)} %param.11) | copy-start | bytes 98308

commit v2 on v1

--- a/solution.py
+++ b/solution.py
@@ -10,6 +10,7 @@
 softening_length = 0.01
 base_step = 0.0625
 LANES = 128
+PIECES = 4
 f32 = jnp.float32
 VMEM = pl.BlockSpec(memory_space=pltpu.VMEM)
 HBM = pl.BlockSpec(memory_space=pltpu.HBM)
@@ -40,7 +41,7 @@
 
 
 def gather_kernel(*refs):
-    given, out, held, sems, kept = (refs[:6], refs[6], refs[7], refs[8], refs[9:])
+    given, out, kept, held, sems = (refs[:7], refs[7], refs[8:15], refs[15], refs[16])
     copies = [
         pltpu.make_async_copy(a, b, sems.at[n]) for n, (a, b) in enumerate(zip(given, kept))
     ]
@@ -48,7 +49,7 @@
         copy.start()
     for copy in copies:
         copy.wait()
-    pos, vel, acc, jrk, levels, active = kept
+    pos, vel, acc, jrk, levels, masses, active = kept
     groups = levels.shape[0]
     offset = active[...] - lax.axis_index("ja") * (groups * LANES)
     group = jnp.broadcast_to(offset >> 7, (8, LANES))
@@ -66,18 +67,19 @@
         here = group == t
         low = jnp.where(here, jnp.take_along_axis(held[0:8, tile(t)], lane, axis=1), low)
         high = jnp.where(here, jnp.take_along_axis(held[8:16, tile(t)], lane, axis=1), high)
-    out[0:8, :] = low
-    out[8:16, :] = high
-
-
-def force_kernel(columns, *refs):
-    gathered, refs = (refs[:columns], refs[columns:])
-    pos, vel, acc, jrk, levels, masses, active, packed, old, sources, targets, sums = refs
+    for k in range(out.shape[0]):
+        out[k, 0:8, :] = low
+        out[k, 8:16, :] = high
+
+
+def force_kernel(
+    gathered, pos, vel, acc, jrk, levels, masses, active, packed, old, sources, targets, sums
+):
     groups = levels.shape[0]
     ntarget = active.shape[1]
-    state = gathered[0][...]
-    for block in gathered[1:]:
-        state = state + block[...]
+    state = gathered[0]
+    for k in range(1, gathered.shape[0]):
+        state = state + gathered[k]
     old[...] = state
     tpos, tvel = predict(state[0:3], state[3:6], state[6:9], state[9:12], state[12:13])
     columns = jnp.transpose(
@@ -142,7 +144,8 @@
 
 
 def finish_kernel(
-    rows, columns, everyone, old, pos, vel, acc, jrk, levels, targets_new, stars_new
+    rows, columns, everyone, old, pos, vel, acc, jrk, levels, targets_out, stars_out,
+    targets_new, stars_new, sems
 ):
     groups = levels.shape[0]
     ntarget = everyone.shape[-1]
@@ -166,6 +169,9 @@
     targets_new[0:3, :] = x1
     targets_new[3:6, :] = v1
     targets_new[6:12, :] = mine[0:6]
+    copies = [pltpu.make_async_copy(targets_new, targets_out, sems.at[0])]
+    copies[0].start()
+    piece = groups // PIECES
 
     group = lax.broadcasted_iota(jnp.int32, (groups, ntarget), 0)
     lane = lax.broadcasted_iota(jnp.int32, (LANES, ntarget), 0)
@@ -201,41 +207,51 @@
         stars_new[3:6, tile(t)] = jnp.where(there, v1, v0)
         stars_new[6:9, tile(t)] = jnp.where(there, a1, a0)
         stars_new[9:12, tile(t)] = jnp.where(there, j1, j0)
+        if (t + 1) % piece == 0:
+            part_of = (slice(None), slice((t + 1 - piece) * LANES, (t + 1) * LANES))
+            copies.append(
+                pltpu.make_async_copy(
+                    stars_new.at[part_of], stars_out.at[part_of], sems.at[len(copies)]
+                )
+            )
+            copies[-1].start()
+    for copy in copies:
+        copy.wait()
 
 
 def local(rows, columns, positions, velocities, accels, jerks, masses, levels, active):
     nlocal = positions.shape[1]
     ntarget = active.shape[0]
     groups = nlocal // LANES
-    levels = levels.reshape(groups, LANES)
-    masses = masses.reshape(groups, LANES)
-    active = active.reshape(1, ntarget)
-    state = (positions, velocities, accels, jerks)
-
-    mine = pl.pallas_call(
+    given = (
+        positions,
+        velocities,
+        accels,
+        jerks,
+        levels.reshape(groups, LANES),
+        masses.reshape(groups, LANES),
+        active.reshape(1, ntarget),
+    )
+    mine, *kept = pl.pallas_call(
         gather_kernel,
-        out_shape=jax.ShapeDtypeStruct((16, ntarget), f32),
-        in_specs=[HBM] * 6,
-        out_specs=VMEM,
-        scratch_shapes=[
-            pltpu.VMEM((16, nlocal), f32),
-            pltpu.SemaphoreType.DMA((6,)),
-            *(pltpu.VMEM(x.shape, x.dtype) for x in (*state, levels, active)),
-        ],
-        compiler_params=pltpu.CompilerParams(vmem_limit_bytes=60 * 1024 * 1024),
+        out_shape=(
+            pltpu.VMEM((columns, 16, ntarget), f32),
+            *(pltpu.VMEM(x.shape, x.dtype) for x in given),
+        ),
+        in_specs=[HBM] * 7,
+        out_specs=(VMEM,) * 8,
+        scratch_shapes=[pltpu.VMEM((16, nlocal), f32), pltpu.SemaphoreType.DMA((7,))],
+        compiler_params=PARAMS,
         name="gather",
-    )(*state, levels, active)
-    gathered = [mine]
-    for k in range(1, columns):
-        ring = [(c, (c + k) % columns) for c in range(columns)]
-        gathered.append(lax.ppermute(mine, "ja", ring))
+    )(*(pltpu.with_memory_space_constraint(x, pltpu.HBM) for x in given))
+    gathered = lax.all_to_all(mine, "ja", 0, 0)
     packed, old = pl.pallas_call(
-        functools.partial(force_kernel, columns),
+        force_kernel,
         out_shape=(
-            jax.ShapeDtypeStruct((rows * columns, 8, ntarget), f32),
-            jax.ShapeDtypeStruct((16, ntarget), f32),
+            pltpu.VMEM((rows * columns, 8, ntarget), f32),
+            pltpu.VMEM((16, ntarget), f32),
         ),
-        in_specs=[VMEM] * (columns + 7),
+        in_specs=[VMEM] * 8,
         out_specs=(VMEM, VMEM),
         scratch_shapes=[
             pltpu.VMEM((groups, 7, 8, LANES), f32),
@@ -244,7 +260,7 @@
         ],
         compiler_params=PARAMS,
         name="forces",
-    )(*gathered, *state, levels, masses, active)
+    )(gathered, *kept)
     everyone = lax.all_to_all(packed, ("ia", "ja"), 0, 0)
     return pl.pallas_call(
         functools.partial(finish_kernel, rows, columns),
@@ -253,10 +269,15 @@
             jax.ShapeDtypeStruct((12, nlocal), f32),
         ),
         in_specs=[VMEM] * 7,
-        out_specs=(VMEM, VMEM),
+        out_specs=(HBM, HBM),
+        scratch_shapes=[
+            pltpu.VMEM((12, ntarget), f32),
+            pltpu.VMEM((12, nlocal), f32),
+            pltpu.SemaphoreType.DMA((1 + PIECES,)),
+        ],
         compiler_params=PARAMS,
         name="finish",
-    )(everyone, old, *state, levels)
+    )(everyone, old, *kept[:5])
 
 
 def solution(mesh):

time: 41.1 us -> 34 us (0.83)
  blocking collectives: 10.6 us -> 23.6 us
  starting transfers between devices: 12.4 us -> 0 us
  waiting for transfers between devices: 5.43 us -> 0 us
  local copies, waits for them, and re-layouts: 1.48 us -> 0 us
  Pallas kernels: 10.2 us -> 9.49 us
    all_to_all x0 -> x1, blocking collectives: none -> 14 us  [local(): gathered = lax.all_to_all(mine, 'ja', 0, 0)]
    ppermute x7 -> x0, starting transfers between devices: 12.4 us -> none  [local(): gathered.append(lax.ppermute(mine, 'ja', ring))]
    ppermute x7 -> x0, waiting for transfers between devices: 5.43 us -> none  [local(): gathered.append(lax.ppermute(mine, 'ja', ring))]
    unnamed x16 -> x0, local copies, waits for them, and re-layouts: 1.48 us -> none
    all_to_all x1, blocking collectives: 10.6 us -> 9.69 us  [local(): everyone = lax.all_to_all(packed, ('ia', 'ja'), 0, 0)]
    pallas_call x2, Pallas kernels: 8.62 us -> 7.97 us  [the longest x1 6.54 us: local(): pl.pallas_call(force_kernel, out_shape=(pltpu.VMEM((rows * columns, 8, nt...]
  transfers between devices with their start and end apart: 7 -> 0, of which waited for: 3 -> 0; matrix products, arithmetic and copies ran while one was open for 0% -> 0% of each run, Pallas kernels for 0% -> 0%
where the time goes in v2:
time: 34 us; the launch traced here: 33.8 us
  blocking collectives  23.6 us (69%)
  Pallas kernels  9.49 us (28%)
  between operations  0.64 us (2%)
    all_to_all x1, blocking collectives, local(): gathered = lax.all_to_all(mine, 'ja', 0, 0)  14 us
    all_to_all x1, blocking collectives, local(): everyone = lax.all_to_all(packed, ('ia', 'ja'), 0, 0)  9.69 us
    pallas_call x1, Pallas kernels, local(): pl.pallas_call(force_kernel, out_shape=(pltpu.VMEM((rows * columns, 8, nt...  6.54 us
    pallas_call x1, Pallas kernels, local(): pl.pallas_call(functools.partial(finish_kernel, rows, columns), out_shape...  1.53 us
    pallas_call x1, Pallas kernels, local(): pl.pallas_call(gather_kernel, out_shape=(pltpu.VMEM((columns, 16, ntarget...  1.43 us

profile of v2, /device:TPU:0, one launch (start us, length us, event | category | flops | bytes accessed | tf_op | source)
XLA Modules:
  0.0 33.8 jit_solution(13165521547254780079)
XLA Ops:
  0.6 1.4 %gather.1 = (f32[8,16,128]{2,1,0:T(8,128)S(1)}, f32[3,8192]{1,0:T(4,128)S(1)}, f32[3,8192]{1,0:T(4,128)S(1)}, f32[3,8192]{1,0:T(4,128)S(1)}, f32[3,8192]{1,0:T(4...) custom-call(f32[3,8192]{1,0:T(4,128)} %refs_0_.1, f32[3,8192]{1,0:T(4,128)} %refs_1_.1, ...), custom_call_target="tpu_custom_call" | custom-call | tf_op jit(solution)/shard_map/gather/pallas_call | solution.py:235
  2.1 14.0 %all_to_all.10.gathered = f32[8,16,128]{2,1,0:T(8,128)S(1)} all-to-all(f32[8,16,128]{2,1,0:T(8,128)S(1)} %get-tuple-element.12), channel_id=1, replica_groups=mesh['ia'=4,'ja'=8] {'ja'}, dimensions={0} | all-to-all | bytes 131072 | tf_op jit(solution)/shard_map/all_to_all | solution.py:247
  16.0 6.5 %forces.1 = (f32[32,8,128]{2,1,0:T(8,128)S(1)}, f32[16,128]{1,0:T(8,128)S(1)}) custom-call(f32[8,16,128]{2,1,0:T(8,128)S(1)} %all_to_all.10.gathered, f32[3,8192]{1,0:T(4,128)S(1)} %get-tuple-element.13.pos, f32[3,8192]{1,0:T(4,128)S(1)} %get-tuple-element.14.vel, f32[3,8192]{1,0:T(4,128)S(1)} %get-tuple-element.15.acc, ...), custom_call_target="tpu_custom_call" | custom-call | tf_op jit(solution)/shard_map/forces/pallas_call | solution.py:248
  22.6 9.7 %all_to_all.11.everyone = f32[32,8,128]{2,1,0:T(8,128)S(1)} all-to-all(f32[32,8,128]{2,1,0:T(8,128)S(1)} %get-tuple-element.20), channel_id=1, replica_groups=mesh['ia'=4,'ja'=8] {'ia','ja'}, dimensions={0} | all-to-all | bytes 262144 | tf_op jit(solution)/shard_map/all_to_all | solution.py:264
  32.3 1.5 %finish.1 = (f32[12,128]{1,0:T(8,128)}, f32[12,8192]{1,0:T(8,128)}) custom-call(f32[32,8,128]{2,1,0:T(8,128)S(1)} %all_to_all.11.everyone, f32[16,128]{1,0:T(8,128)S(1)} %get-tuple-element.21.old, f32[3,8192]{1,0:T(4,128)S(1)} %get-tuple-element.13.pos, f32[3,8192]{1,0:T(4,128)S(1)} %get-tuple-element.14.vel, f32[3,8192]{1,0:T(4,128)S(1)} %get-tuple-element.15.acc, ...), custom_call_target="tpu_custom_call" | custom-call | tf_op jit(solution)/shard_map/finish/pallas_call | solution.py:265

commit v3 on v2

--- a/solution.py
+++ b/solution.py
@@ -11,6 +11,7 @@
 base_step = 0.0625
 LANES = 128
 PIECES = 4
+CHUNK = 16
 f32 = jnp.float32
 VMEM = pl.BlockSpec(memory_space=pltpu.VMEM)
 HBM = pl.BlockSpec(memory_space=pltpu.HBM)
@@ -73,7 +74,8 @@
 
 
 def force_kernel(
-    gathered, pos, vel, acc, jrk, levels, masses, active, packed, old, sources, targets, sums
+    gathered, pos, vel, acc, jrk, levels, masses, active, packed, old, sources, targets, sums,
+    even, odd
 ):
     groups = levels.shape[0]
     ntarget = active.shape[1]
@@ -97,41 +99,62 @@
             sources[t, 3 + c] = jnp.broadcast_to(svel[c : c + 1], (8, LANES))
         sources[t, 6] = jnp.broadcast_to(masses[t : t + 1, :], (8, LANES))
 
-    def one_group(g, unused):
-        rows = pl.ds(pl.multiple_of(g * 8, 8), 8)
-        tx, ty, tz, tu, tv, tw = (targets[c, rows, :] for c in range(6))
-
-        def one_tile(t, carry):
-            dx, dy, dz = (sources[t, 0] - tx, sources[t, 1] - ty, sources[t, 2] - tz)
-            du, dv, dw = (sources[t, 3] - tu, sources[t, 4] - tv, sources[t, 5] - tw)
-            r2 = dx * dx + dy * dy + dz * dz + softening_length
-            inv = lax.rsqrt(r2)
-            inv_sq = inv * inv
-            weight = sources[t, 6] * inv * inv_sq
-            radial = (dx * du + dy * dv + dz * dw) * inv_sq
-            px, py, pz = (weight * dx, weight * dy, weight * dz)
-            ax, ay, az, jx, jy, jz, kx, ky, kz = carry
-            return (
-                ax + px,
-                ay + py,
-                az + pz,
-                jx + weight * du,
-                jy + weight * dv,
-                jz + weight * dw,
-                kx + radial * px,
-                ky + radial * py,
-                kz + radial * pz,
-            )
+    def rows_of(g):
+        return pl.ds(pl.multiple_of(g * 8, 8), 8)
+
+    def first_stage(t, place, held):
+        dx, dy, dz = (sources[t, c] - place[c] for c in range(3))
+        held[t, 0], held[t, 1], held[t, 2] = (dx, dy, dz)
+        held[t, 3] = lax.rsqrt(dx * dx + dy * dy + dz * dz + softening_length)
+
+    def second_stage(t, speed, held, carry):
+        dx, dy, dz, inv = (held[t, c] for c in range(4))
+        du, dv, dw = (sources[t, 3 + c] - speed[c] for c in range(3))
+        inv_sq = inv * inv
+        weight = sources[t, 6] * inv * inv_sq
+        radial = (dx * du + dy * dv + dz * dw) * inv_sq
+        px, py, pz = (weight * dx, weight * dy, weight * dz)
+        terms = (
+            *(px, py, pz),
+            *(weight * du, weight * dv, weight * dw),
+            *(radial * px, radial * py, radial * pz),
+        )
+        return tuple(total + term for total, term in zip(carry, terms))
+
+    def stages(g, later, earlier):
+        if later is not None:
+            place = [targets[c, rows_of(g), :] for c in range(3)]
+        if earlier is not None:
+            speed = [targets[3 + c, rows_of(g - 1), :] for c in range(3)]
+
+        def some_tiles(n, carry):
+            for k in range(CHUNK):
+                t = n * CHUNK + k
+                if earlier is not None:
+                    carry = second_stage(t, speed, earlier, carry)
+                if later is not None:
+                    first_stage(t, place, later)
+            return carry
 
         zero = jnp.zeros((8, LANES), f32)
         ax, ay, az, jx, jy, jz, kx, ky, kz = lax.fori_loop(
-            0, groups, one_tile, (zero,) * 9, unroll=16
+            0, groups // CHUNK, some_tiles, (zero,) * 9
         )
-        for c, value in enumerate((ax, ay, az, jx - 3.0 * kx, jy - 3.0 * ky, jz - 3.0 * kz)):
-            sums[c, rows, :] = value
+        if earlier is not None:
+            forces = (ax, ay, az, jx - 3.0 * kx, jy - 3.0 * ky, jz - 3.0 * kz)
+            for c, value in enumerate(forces):
+                sums[c, rows_of(g - 1), :] = value
+
+    def two_groups(n, unused):
+        stages(2 * n + 1, odd, even)
+        stages(2 * n + 2, even, odd)
         return unused
 
-    lax.fori_loop(0, ntarget // 8, one_group, 0)
+    last = ntarget // 8
+    stages(0, even, None)
+    lax.fori_loop(0, last // 2 - 1, two_groups, 0)
+    stages(last - 1, odd, even)
+    stages(last, None, odd)
     lane = lax.broadcasted_iota(jnp.int32, (ntarget, LANES), 1)
     table = jnp.zeros((ntarget, LANES), f32)
     for c in range(6):
@@ -155,12 +178,12 @@
     forces, where_hi, where_lo = ([], [], [])
     mine = jnp.zeros((8, ntarget), f32)
     for r in range(rows):
-        total = everyone[r * columns]
+        total = everyone[r]
         for c in range(1, columns):
-            total = total + everyone[r * columns + c]
+            total = total + everyone[c * rows + r]
         forces.append(total)
         mine = jnp.where(me == r, total, mine)
-        offset = everyone[r * columns][6:7].astype(jnp.int32) - base
+        offset = everyone[r][6:7].astype(jnp.int32) - base
         where_hi.append(offset >> 7)
         where_lo.append(offset & (LANES - 1))
 
@@ -257,11 +280,13 @@
             pltpu.VMEM((groups, 7, 8, LANES), f32),
             pltpu.VMEM((6, ntarget, LANES), f32),
             pltpu.VMEM((6, ntarget, LANES), f32),
+            pltpu.VMEM((groups, 4, 8, LANES), f32),
+            pltpu.VMEM((groups, 4, 8, LANES), f32),
         ],
         compiler_params=PARAMS,
         name="forces",
     )(gathered, *kept)
-    everyone = lax.all_to_all(packed, ("ia", "ja"), 0, 0)
+    everyone = lax.all_to_all(packed, ("ja", "ia"), 0, 0)
     return pl.pallas_call(
         functools.partial(finish_kernel, rows, columns),
         out_shape=(

time: 34 us -> 34.9 us (1.026)
  blocking collectives: 23.6 us -> 24.1 us
  Pallas kernels: 9.49 us -> 9.94 us
    all_to_all x1, blocking collectives: 9.69 us -> 10.2 us  [local(): everyone = lax.all_to_all(packed, ('ja', 'ia'), 0, 0)]
    pallas_call x1, Pallas kernels: 6.54 us -> 6.99 us  [local(): pl.pallas_call(force_kernel, out_shape=(pltpu.VMEM((rows * columns, 8, nt...]
where the time goes in v3:
time: 34.9 us; the launch traced here: 34.7 us
  blocking collectives  24.1 us (69%)
  Pallas kernels  9.94 us (28%)
  between operations  0.64 us (2%)
    all_to_all x1, blocking collectives, local(): gathered = lax.all_to_all(mine, 'ja', 0, 0)  14 us
    all_to_all x1, blocking collectives, local(): everyone = lax.all_to_all(packed, ('ja', 'ia'), 0, 0)  10.2 us
    pallas_call x1, Pallas kernels, local(): pl.pallas_call(force_kernel, out_shape=(pltpu.VMEM((rows * columns, 8, nt...  6.99 us
    pallas_call x1, Pallas kernels, local(): pl.pallas_call(functools.partial(finish_kernel, rows, columns), out_shape...  1.52 us
    pallas_call x1, Pallas kernels, local(): pl.pallas_call(gather_kernel, out_shape=(pltpu.VMEM((columns, 16, ntarget...  1.43 us

profile of v3, /device:TPU:0, one launch (start us, length us, event | category | flops | bytes accessed | tf_op | source)
XLA Modules:
  0.0 34.7 jit_solution(5869329069879825945)
XLA Ops:
  0.6 1.4 %gather.1 = (f32[8,16,128]{2,1,0:T(8,128)S(1)}, f32[3,8192]{1,0:T(4,128)S(1)}, f32[3,8192]{1,0:T(4,128)S(1)}, f32[3,8192]{1,0:T(4,128)S(1)}, f32[3,8192]{1,0:T(4...) custom-call(f32[3,8192]{1,0:T(4,128)} %refs_0_.1, f32[3,8192]{1,0:T(4,128)} %refs_1_.1, ...), custom_call_target="tpu_custom_call" | custom-call | tf_op jit(solution)/shard_map/gather/pallas_call | solution.py:258
  2.1 14.0 %all_to_all.10.gathered = f32[8,16,128]{2,1,0:T(8,128)S(1)} all-to-all(f32[8,16,128]{2,1,0:T(8,128)S(1)} %get-tuple-element.12), channel_id=1, replica_groups=mesh['ia'=4,'ja'=8] {'ja'}, dimensions={0} | all-to-all | bytes 131072 | tf_op jit(solution)/shard_map/all_to_all | solution.py:270
  16.0 7.0 %forces.1 = (f32[32,8,128]{2,1,0:T(8,128)S(1)}, f32[16,128]{1,0:T(8,128)S(1)}) custom-call(f32[8,16,128]{2,1,0:T(8,128)S(1)} %all_to_all.10.gathered, f32[3,8192]{1,0:T(4,128)S(1)} %get-tuple-element.13.pos, f32[3,8192]{1,0:T(4,128)S(1)} %get-tuple-element.14.vel, f32[3,8192]{1,0:T(4,128)S(1)} %get-tuple-element.15.acc, ...), custom_call_target="tpu_custom_call" | custom-call | tf_op jit(solution)/shard_map/forces/pallas_call | solution.py:271
  23.0 10.2 %all_to_all.11.everyone = f32[32,8,128]{2,1,0:T(8,128)S(1)} all-to-all(f32[32,8,128]{2,1,0:T(8,128)S(1)} %get-tuple-element.20), channel_id=1, replica_groups=mesh['ia'=4,'ja'=8] {'ja','ia'}, dimensions={0} | all-to-all | bytes 262144 | tf_op jit(solution)/shard_map/all_to_all | solution.py:289
  33.2 1.5 %finish.1 = (f32[12,128]{1,0:T(8,128)}, f32[12,8192]{1,0:T(8,128)}) custom-call(f32[32,8,128]{2,1,0:T(8,128)S(1)} %all_to_all.11.everyone, f32[16,128]{1,0:T(8,128)S(1)} %get-tuple-element.21.old, f32[3,8192]{1,0:T(4,128)S(1)} %get-tuple-element.13.pos, f32[3,8192]{1,0:T(4,128)S(1)} %get-tuple-element.14.vel, f32[3,8192]{1,0:T(4,128)S(1)} %get-tuple-element.15.acc, ...), custom_call_target="tpu_custom_call" | custom-call | tf_op jit(solution)/shard_map/finish/pallas_call | solution.py:290

commit v4 on v2

--- a/solution.py
+++ b/solution.py
@@ -11,6 +11,8 @@
 base_step = 0.0625
 LANES = 128
 PIECES = 4
+OLD_ROWS = 13
+NEW_ROWS = 7
 f32 = jnp.float32
 VMEM = pl.BlockSpec(memory_space=pltpu.VMEM)
 HBM = pl.BlockSpec(memory_space=pltpu.HBM)
@@ -68,8 +70,8 @@
         low = jnp.where(here, jnp.take_along_axis(held[0:8, tile(t)], lane, axis=1), low)
         high = jnp.where(here, jnp.take_along_axis(held[8:16, tile(t)], lane, axis=1), high)
     for k in range(out.shape[0]):
-        out[k, 0:8, :] = low
-        out[k, 8:16, :] = high
+        for c in range(OLD_ROWS):
+            out[k, :, tile(c)] = (low if c < 8 else high)[c % 8 : c % 8 + 1]
 
 
 def force_kernel(
@@ -77,10 +79,12 @@
 ):
     groups = levels.shape[0]
     ntarget = active.shape[1]
-    state = gathered[0]
+    flat = gathered[0]
     for k in range(1, gathered.shape[0]):
-        state = state + gathered[k]
-    old[...] = state
+        flat = flat + gathered[k]
+    for c in range(OLD_ROWS):
+        old[c : c + 1, :] = flat[:, tile(c)]
+    state = old[...]
     tpos, tvel = predict(state[0:3], state[3:6], state[6:9], state[9:12], state[12:13])
     columns = jnp.transpose(
         jnp.concatenate([tpos, tvel, jnp.zeros((LANES - 6, ntarget), f32)], axis=0)
@@ -125,7 +129,7 @@
 
         zero = jnp.zeros((8, LANES), f32)
         ax, ay, az, jx, jy, jz, kx, ky, kz = lax.fori_loop(
-            0, groups, one_tile, (zero,) * 9, unroll=16
+            0, groups, one_tile, (zero,) * 9, unroll=32
         )
         for c, value in enumerate((ax, ay, az, jx - 3.0 * kx, jy - 3.0 * ky, jz - 3.0 * kz)):
             sums[c, rows, :] = value
@@ -140,15 +144,16 @@
     row = lax.broadcasted_iota(jnp.int32, (8, ntarget), 0)
     table = jnp.where(row == 6, active[...].astype(f32), table)
     for k in range(packed.shape[0]):
-        packed[k] = table
+        for c in range(NEW_ROWS):
+            packed[k, :, tile(c)] = table[c : c + 1]
 
 
 def finish_kernel(
     rows, columns, everyone, old, pos, vel, acc, jrk, levels, targets_out, stars_out,
-    targets_new, stars_new, sems
+    targets_new, stars_new, rowed, sems
 ):
     groups = levels.shape[0]
-    ntarget = everyone.shape[-1]
+    ntarget = old.shape[1]
     me = lax.axis_index("ia")
     base = lax.axis_index("ja") * (groups * LANES)
 
@@ -158,9 +163,11 @@
         total = everyone[r * columns]
         for c in range(1, columns):
             total = total + everyone[r * columns + c]
-        forces.append(total)
-        mine = jnp.where(me == r, total, mine)
-        offset = everyone[r * columns][6:7].astype(jnp.int32) - base
+        for c in range(6):
+            rowed[r, c : c + 1, :] = total[:, tile(c)]
+        forces.append(rowed[r])
+        mine = jnp.where(me == r, forces[r], mine)
+        offset = everyone[r * columns][:, tile(6)].astype(jnp.int32) - base
         where_hi.append(offset >> 7)
         where_lo.append(offset & (LANES - 1))
 
@@ -235,7 +242,7 @@
     mine, *kept = pl.pallas_call(
         gather_kernel,
         out_shape=(
-            pltpu.VMEM((columns, 16, ntarget), f32),
+            pltpu.VMEM((columns, 1, OLD_ROWS * ntarget), f32),
             *(pltpu.VMEM(x.shape, x.dtype) for x in given),
         ),
         in_specs=[HBM] * 7,
@@ -248,7 +255,7 @@
     packed, old = pl.pallas_call(
         force_kernel,
         out_shape=(
-            pltpu.VMEM((rows * columns, 8, ntarget), f32),
+            pltpu.VMEM((rows * columns, 1, NEW_ROWS * ntarget), f32),
             pltpu.VMEM((16, ntarget), f32),
         ),
         in_specs=[VMEM] * 8,
@@ -273,6 +280,7 @@
         scratch_shapes=[
             pltpu.VMEM((12, ntarget), f32),
             pltpu.VMEM((12, nlocal), f32),
+            pltpu.VMEM((rows, 8, ntarget), f32),
             pltpu.SemaphoreType.DMA((1 + PIECES,)),
         ],
         compiler_params=PARAMS,

time: 34 us -> 33.7 us (level)
  no operation moved by 1% of the time
where the time goes in v4:
time: 33.7 us; the launch traced here: 33.5 us
  blocking collectives  23.4 us (69%)
  Pallas kernels  9.41 us (28%)
  between operations  0.65 us (2%)
    all_to_all x1, blocking collectives, local(): gathered = lax.all_to_all(mine, 'ja', 0, 0)  13.9 us
    all_to_all x1, blocking collectives, local(): everyone = lax.all_to_all(packed, ('ia', 'ja'), 0, 0)  9.55 us
    pallas_call x1, Pallas kernels, local(): pl.pallas_call(force_kernel, out_shape=(pltpu.VMEM((rows * columns, 1, NE...  6.44 us
    pallas_call x1, Pallas kernels, local(): pl.pallas_call(functools.partial(finish_kernel, rows, columns), out_shape...  1.52 us
    pallas_call x1, Pallas kernels, local(): pl.pallas_call(gather_kernel, out_shape=(pltpu.VMEM((columns, 1, OLD_ROWS...  1.45 us

profile of v4, /device:TPU:0, one launch (start us, length us, event | category | flops | bytes accessed | tf_op | source)
XLA Modules:
  0.0 33.5 jit_solution(8035955848895824102)
XLA Ops:
  0.6 1.4 %gather.1 = (f32[8,1,1664]{2,1,0:T(1,128)S(1)}, f32[3,8192]{1,0:T(4,128)S(1)}, f32[3,8192]{1,0:T(4,128)S(1)}, f32[3,8192]{1,0:T(4,128)S(1)}, f32[3,8192]{1,0:T(4...) custom-call(f32[3,8192]{1,0:T(4,128)} %refs_0_.1, f32[3,8192]{1,0:T(4,128)} %refs_1_.1, ...), custom_call_target="tpu_custom_call" | custom-call | tf_op jit(solution)/shard_map/gather/pallas_call | solution.py:242
  2.1 13.9 %all_to_all.10.gathered = f32[8,1,1664]{2,1,0:T(1,128)S(1)} all-to-all(f32[8,1,1664]{2,1,0:T(1,128)S(1)} %get-tuple-element.12), channel_id=1, replica_groups=mesh['ia'=4,'ja'=8] {'ja'}, dimensions={0} | all-to-all | bytes 106496 | tf_op jit(solution)/shard_map/all_to_all | solution.py:254
  16.0 6.4 %forces.1 = (f32[32,1,896]{2,1,0:T(1,128)S(1)}, f32[16,128]{1,0:T(8,128)S(1)}) custom-call(f32[8,1,1664]{2,1,0:T(1,128)S(1)} %all_to_all.10.gathered, f32[3,8192]{1,0:T(4,128)S(1)} %get-tuple-element.13.pos, f32[3,8192]{1,0:T(4,128)S(1)} %get-tuple-element.14.vel, f32[3,8192]{1,0:T(4,128)S(1)} %get-tuple-element.15.acc, ...), custom_call_target="tpu_custom_call" | custom-call | tf_op jit(solution)/shard_map/forces/pallas_call | solution.py:255
  22.4 9.5 %all_to_all.11.everyone = f32[32,1,896]{2,1,0:T(1,128)S(1)} all-to-all(f32[32,1,896]{2,1,0:T(1,128)S(1)} %get-tuple-element.20), channel_id=1, replica_groups=mesh['ia'=4,'ja'=8] {'ia','ja'}, dimensions={0} | all-to-all | bytes 229376 | tf_op jit(solution)/shard_map/all_to_all | solution.py:271
  32.0 1.5 %finish.1 = (f32[12,128]{1,0:T(8,128)}, f32[12,8192]{1,0:T(8,128)}) custom-call(f32[32,1,896]{2,1,0:T(1,128)S(1)} %all_to_all.11.everyone, f32[16,128]{1,0:T(8,128)S(1)} %get-tuple-element.21.old, f32[3,8192]{1,0:T(4,128)S(1)} %get-tuple-element.13.pos, f32[3,8192]{1,0:T(4,128)S(1)} %get-tuple-element.14.vel, f32[3,8192]{1,0:T(4,128)S(1)} %get-tuple-element.15.acc, ...), custom_call_target="tpu_custom_call" | custom-call | tf_op jit(solution)/shard_map/finish/pallas_call | solution.py:272

commit v5 on v4

--- a/solution.py
+++ b/solution.py
@@ -11,7 +11,6 @@
 base_step = 0.0625
 LANES = 128
 PIECES = 4
-OLD_ROWS = 13
 NEW_ROWS = 7
 f32 = jnp.float32
 VMEM = pl.BlockSpec(memory_space=pltpu.VMEM)
@@ -23,18 +22,26 @@
     return (128 >> levels).astype(f32) * (base_step / 128.0)
 
 
-def predict(pos, vel, acc, jrk, elapsed):
+def step_factors(elapsed):
     half = elapsed * elapsed * 0.5
-    sixth = half * elapsed / 3.0
+    return (elapsed, half, half * elapsed * (1.0 / 3.0))
+
+
+def predict(pos, vel, acc, jrk, factors):
+    elapsed, half, sixth = factors
     pred_pos = pos + elapsed * vel + half * acc + sixth * jrk
     pred_vel = vel + elapsed * acc + half * jrk
     return (pred_pos, pred_vel)
 
 
-def correct(x0, v0, a0, j0, step, a1, j1):
-    quad = step * step / 12.0
-    v1 = v0 + 0.5 * step * (a0 + a1) + quad * (j0 - j1)
-    x1 = x0 + 0.5 * step * (v0 + v1) + quad * (a0 - a1)
+def correction_factors(step):
+    return (0.5 * step, step * step * (1.0 / 12.0))
+
+
+def correct(x0, v0, a0, j0, factors, a1, j1):
+    half, quad = factors
+    v1 = v0 + half * (a0 + a1) + quad * (j0 - j1)
+    x1 = x0 + half * (v0 + v1) + quad * (a0 - a1)
     return (x1, v1)
 
 
@@ -43,35 +50,52 @@
 
 
 def gather_kernel(*refs):
-    given, out, kept, held, sems = (refs[:7], refs[7], refs[8:15], refs[15], refs[16])
-    copies = [
-        pltpu.make_async_copy(a, b, sems.at[n]) for n, (a, b) in enumerate(zip(given, kept))
-    ]
-    for copy in copies:
-        copy.start()
-    for copy in copies:
-        copy.wait()
+    given, out, kept, sems = (refs[:7], refs[7], refs[8:15], refs[15])
     pos, vel, acc, jrk, levels, masses, active = kept
     groups = levels.shape[0]
+    half = groups // 2
+
+    def copy_of(n, sem, columns=None):
+        if columns is None:
+            return pltpu.make_async_copy(given[n], kept[n], sems.at[sem])
+        part = (slice(None), columns)
+        return pltpu.make_async_copy(given[n].at[part], kept[n].at[part], sems.at[sem])
+
+    small = [copy_of(6, 0), copy_of(4, 1)]
+    parts = [
+        [copy_of(n, 2 + 4 * h + n, slice(h * half * LANES, (h + 1) * half * LANES)) for n in range(4)]
+        for h in range(2)
+    ]
+    late = copy_of(5, 10)
+    for copy in (*small, *parts[0], *parts[1], late):
+        copy.start()
+    for copy in small:
+        copy.wait()
     offset = active[...] - lax.axis_index("ja") * (groups * LANES)
     group = jnp.broadcast_to(offset >> 7, (8, LANES))
     lane = jnp.broadcast_to(offset & (LANES - 1), (8, LANES))
-    held[0:3, :] = pos[...]
-    held[3:6, :] = vel[...]
-    held[6:9, :] = acc[...]
-    held[9:12, :] = jrk[...]
+    row = lax.broadcasted_iota(jnp.int32, (8, LANES), 0)
     elapsed = elapsed_of(levels[...])
-    for t in range(groups):
-        held[12:16, tile(t)] = jnp.broadcast_to(elapsed[t : t + 1], (4, LANES))
-    low = jnp.zeros((8, LANES), f32)
-    high = jnp.zeros((8, LANES), f32)
-    for t in range(groups):
-        here = group == t
-        low = jnp.where(here, jnp.take_along_axis(held[0:8, tile(t)], lane, axis=1), low)
-        high = jnp.where(here, jnp.take_along_axis(held[8:16, tile(t)], lane, axis=1), high)
+    steps = jnp.zeros((8, LANES), f32)
+    for t in range(0, groups, 8):
+        here = group == row + t
+        steps = jnp.where(here, jnp.take_along_axis(elapsed[t : t + 8], lane, axis=1), steps)
+    found = [jnp.zeros((3, LANES), f32)] * 4
+    for h in range(2):
+        for copy in parts[h]:
+            copy.wait()
+        for t in range(h * half, (h + 1) * half):
+            here = group[0:3] == t
+            found = [
+                jnp.where(here, jnp.take_along_axis(x[:, tile(t)], lane[0:3], axis=1), old)
+                for x, old in zip((pos, vel, acc, jrk), found)
+            ]
+    steps = jnp.broadcast_to(jnp.sum(steps, axis=0, keepdims=True), (4, LANES))
     for k in range(out.shape[0]):
-        for c in range(OLD_ROWS):
-            out[k, :, tile(c)] = (low if c < 8 else high)[c % 8 : c % 8 + 1]
+        for n, value in enumerate(found):
+            out[k, 3 * n : 3 * n + 3, :] = value
+        out[k, 12:16, :] = steps
+    late.wait()
 
 
 def force_kernel(
@@ -79,22 +103,22 @@
 ):
     groups = levels.shape[0]
     ntarget = active.shape[1]
-    flat = gathered[0]
+    state = gathered[0]
     for k in range(1, gathered.shape[0]):
-        flat = flat + gathered[k]
-    for c in range(OLD_ROWS):
-        old[c : c + 1, :] = flat[:, tile(c)]
-    state = old[...]
-    tpos, tvel = predict(state[0:3], state[3:6], state[6:9], state[9:12], state[12:13])
+        state = state + gathered[k]
+    old[...] = state
+    tpos, tvel = predict(
+        state[0:3], state[3:6], state[6:9], state[9:12], step_factors(state[12:13])
+    )
     columns = jnp.transpose(
         jnp.concatenate([tpos, tvel, jnp.zeros((LANES - 6, ntarget), f32)], axis=0)
     )
     for c in range(6):
         targets[c] = jnp.broadcast_to(columns[:, c : c + 1], (ntarget, LANES))
-    elapsed = elapsed_of(levels[...])
+    factors = step_factors(elapsed_of(levels[...]))
     for t in range(groups):
         spos, svel = predict(
-            pos[:, tile(t)], vel[:, tile(t)], acc[:, tile(t)], jrk[:, tile(t)], elapsed[t : t + 1]
+            *(x[:, tile(t)] for x in (pos, vel, acc, jrk)), [f[t : t + 1] for f in factors]
         )
         for c in range(3):
             sources[t, c] = jnp.broadcast_to(spos[c : c + 1], (8, LANES))
@@ -110,7 +134,7 @@
             du, dv, dw = (sources[t, 3] - tu, sources[t, 4] - tv, sources[t, 5] - tw)
             r2 = dx * dx + dy * dy + dz * dz + softening_length
             inv = lax.rsqrt(r2)
-            inv_sq = inv * inv
+            inv_sq = pl.reciprocal(r2, approx=True)
             weight = sources[t, 6] * inv * inv_sq
             radial = (dx * du + dy * dv + dz * dw) * inv_sq
             px, py, pz = (weight * dx, weight * dy, weight * dz)
@@ -172,7 +196,8 @@
         where_lo.append(offset & (LANES - 1))
 
     o = old[...]
-    x1, v1 = correct(o[0:3], o[3:6], o[6:9], o[9:12], o[12:13], mine[0:3], mine[3:6])
+    factors = correction_factors(o[12:13])
+    x1, v1 = correct(o[0:3], o[3:6], o[6:9], o[9:12], factors, mine[0:3], mine[3:6])
     targets_new[0:3, :] = x1
     targets_new[3:6, :] = v1
     targets_new[6:12, :] = mine[0:6]
@@ -199,7 +224,7 @@
     present = spot > 0.5
     slot = jnp.where(present, spot - 1.0, 0.0).astype(jnp.int32)
     part = jnp.where(present, part, -1.0)
-    elapsed = elapsed_of(levels[...])
+    factors = correction_factors(elapsed_of(levels[...]))
     for t in range(groups):
         lanes = jnp.broadcast_to(slot[t : t + 1], (8, LANES))
         holder = jnp.broadcast_to(part[t : t + 1], (8, LANES))
@@ -209,7 +234,7 @@
         there = holder[0:3] > -0.5
         x0, v0, a0, j0 = (pos[:, tile(t)], vel[:, tile(t)], acc[:, tile(t)], jrk[:, tile(t)])
         a1, j1 = (new[0:3], new[3:6])
-        x1, v1 = correct(x0, v0, a0, j0, elapsed[t : t + 1], a1, j1)
+        x1, v1 = correct(x0, v0, a0, j0, [f[t : t + 1] for f in factors], a1, j1)
         stars_new[0:3, tile(t)] = jnp.where(there, x1, x0)
         stars_new[3:6, tile(t)] = jnp.where(there, v1, v0)
         stars_new[6:9, tile(t)] = jnp.where(there, a1, a0)
@@ -242,12 +267,12 @@
     mine, *kept = pl.pallas_call(
         gather_kernel,
         out_shape=(
-            pltpu.VMEM((columns, 1, OLD_ROWS * ntarget), f32),
+            pltpu.VMEM((columns, 16, ntarget), f32),
             *(pltpu.VMEM(x.shape, x.dtype) for x in given),
         ),
         in_specs=[HBM] * 7,
         out_specs=(VMEM,) * 8,
-        scratch_shapes=[pltpu.VMEM((16, nlocal), f32), pltpu.SemaphoreType.DMA((7,))],
+        scratch_shapes=[pltpu.SemaphoreType.DMA((11,))],
         compiler_params=PARAMS,
         name="gather",
     )(*(pltpu.with_memory_space_constraint(x, pltpu.HBM) for x in given))

time: 33.7 us -> 33.9 us (level)
  no operation moved by 1% of the time
where the time goes in v5:
time: 33.9 us; the launch traced here: 33.7 us
  blocking collectives  23.6 us (70%)
  Pallas kernels  9.46 us (28%)
  between operations  0.65 us (2%)
    all_to_all x1, blocking collectives, local(): gathered = lax.all_to_all(mine, 'ja', 0, 0)  14 us
    all_to_all x1, blocking collectives, local(): everyone = lax.all_to_all(packed, ('ia', 'ja'), 0, 0)  9.6 us
    pallas_call x1, Pallas kernels, local(): pl.pallas_call(force_kernel, out_shape=(pltpu.VMEM((rows * columns, 1, NE...  6.44 us
    pallas_call x1, Pallas kernels, local(): pl.pallas_call(functools.partial(finish_kernel, rows, columns), out_shape...  1.53 us
    pallas_call x1, Pallas kernels, local(): pl.pallas_call(gather_kernel, out_shape=(pltpu.VMEM((columns, 16, ntarget...  1.49 us

profile of v5, /device:TPU:0, one launch (start us, length us, event | category | flops | bytes accessed | tf_op | source)
XLA Modules:
  0.0 33.7 jit_solution(11798663470385023052)
XLA Ops:
  0.6 1.5 %gather.1 = (f32[8,16,128]{2,1,0:T(8,128)S(1)}, f32[3,8192]{1,0:T(4,128)S(1)}, f32[3,8192]{1,0:T(4,128)S(1)}, f32[3,8192]{1,0:T(4,128)S(1)}, f32[3,8192]{1,0:T(4...) custom-call(f32[3,8192]{1,0:T(4,128)} %refs_0_.1, f32[3,8192]{1,0:T(4,128)} %refs_1_.1, ...), custom_call_target="tpu_custom_call" | custom-call | tf_op jit(solution)/shard_map/gather/pallas_call | solution.py:267
  2.1 14.0 %all_to_all.10.gathered = f32[8,16,128]{2,1,0:T(8,128)S(1)} all-to-all(f32[8,16,128]{2,1,0:T(8,128)S(1)} %get-tuple-element.12), channel_id=1, replica_groups=mesh['ia'=4,'ja'=8] {'ja'}, dimensions={0} | all-to-all | bytes 131072 | tf_op jit(solution)/shard_map/all_to_all | solution.py:279
  16.1 6.4 %forces.1 = (f32[32,1,896]{2,1,0:T(1,128)S(1)}, f32[16,128]{1,0:T(8,128)S(1)}) custom-call(f32[8,16,128]{2,1,0:T(8,128)S(1)} %all_to_all.10.gathered, f32[3,8192]{1,0:T(4,128)S(1)} %get-tuple-element.13.pos, f32[3,8192]{1,0:T(4,128)S(1)} %get-tuple-element.14.vel, f32[3,8192]{1,0:T(4,128)S(1)} %get-tuple-element.15.acc, ...), custom_call_target="tpu_custom_call" | custom-call | tf_op jit(solution)/shard_map/forces/pallas_call | solution.py:280
  22.5 9.6 %all_to_all.11.everyone = f32[32,1,896]{2,1,0:T(1,128)S(1)} all-to-all(f32[32,1,896]{2,1,0:T(1,128)S(1)} %get-tuple-element.20), channel_id=1, replica_groups=mesh['ia'=4,'ja'=8] {'ia','ja'}, dimensions={0} | all-to-all | bytes 229376 | tf_op jit(solution)/shard_map/all_to_all | solution.py:296
  32.1 1.5 %finish.1 = (f32[12,128]{1,0:T(8,128)}, f32[12,8192]{1,0:T(8,128)}) custom-call(f32[32,1,896]{2,1,0:T(1,128)S(1)} %all_to_all.11.everyone, f32[16,128]{1,0:T(8,128)S(1)} %get-tuple-element.21.old, f32[3,8192]{1,0:T(4,128)S(1)} %get-tuple-element.13.pos, f32[3,8192]{1,0:T(4,128)S(1)} %get-tuple-element.14.vel, f32[3,8192]{1,0:T(4,128)S(1)} %get-tuple-element.15.acc, ...), custom_call_target="tpu_custom_call" | custom-call | tf_op jit(solution)/shard_map/finish/pallas_call | solution.py:297

commit v6 on v5

--- a/solution.py
+++ b/solution.py
@@ -11,6 +11,7 @@
 base_step = 0.0625
 LANES = 128
 PIECES = 4
+TILES = 2
 NEW_ROWS = 7
 f32 = jnp.float32
 VMEM = pl.BlockSpec(memory_space=pltpu.VMEM)
@@ -125,41 +126,35 @@
             sources[t, 3 + c] = jnp.broadcast_to(svel[c : c + 1], (8, LANES))
         sources[t, 6] = jnp.broadcast_to(masses[t : t + 1, :], (8, LANES))
 
-    def one_group(g, unused):
-        rows = pl.ds(pl.multiple_of(g * 8, 8), 8)
-        tx, ty, tz, tu, tv, tw = (targets[c, rows, :] for c in range(6))
-
-        def one_tile(t, carry):
-            dx, dy, dz = (sources[t, 0] - tx, sources[t, 1] - ty, sources[t, 2] - tz)
-            du, dv, dw = (sources[t, 3] - tu, sources[t, 4] - tv, sources[t, 5] - tw)
-            r2 = dx * dx + dy * dy + dz * dz + softening_length
-            inv = lax.rsqrt(r2)
-            inv_sq = pl.reciprocal(r2, approx=True)
-            weight = sources[t, 6] * inv * inv_sq
-            radial = (dx * du + dy * dv + dz * dw) * inv_sq
-            px, py, pz = (weight * dx, weight * dy, weight * dz)
-            ax, ay, az, jx, jy, jz, kx, ky, kz = carry
-            return (
-                ax + px,
-                ay + py,
-                az + pz,
-                jx + weight * du,
-                jy + weight * dv,
-                jz + weight * dw,
-                kx + radial * px,
-                ky + radial * py,
-                kz + radial * pz,
-            )
-
-        zero = jnp.zeros((8, LANES), f32)
-        ax, ay, az, jx, jy, jz, kx, ky, kz = lax.fori_loop(
-            0, groups, one_tile, (zero,) * 9, unroll=32
-        )
-        for c, value in enumerate((ax, ay, az, jx - 3.0 * kx, jy - 3.0 * ky, jz - 3.0 * kz)):
-            sums[c, rows, :] = value
+    sums[...] = jnp.zeros(sums.shape, f32)
+
+    def some_tiles(n, unused):
+        held = [[sources[n * TILES + k, c] for c in range(7)] for k in range(TILES)]
+        for g in range(ntarget // 8):
+            rows = slice(8 * g, 8 * g + 8)
+            target = [targets[c, rows, :] for c in range(6)]
+            total = [sums[c, rows, :] for c in range(9)]
+            for source in held:
+                dx, dy, dz, du, dv, dw = (source[c] - target[c] for c in range(6))
+                r2 = dx * dx + dy * dy + dz * dz + softening_length
+                weight = source[6] * lax.rsqrt(r2)
+                inv_sq = pl.reciprocal(r2, approx=True)
+                weight = weight * inv_sq
+                radial = (dx * du + dy * dv + dz * dw) * inv_sq
+                px, py, pz = (weight * dx, weight * dy, weight * dz)
+                terms = (
+                    *(px, py, pz),
+                    *(weight * du, weight * dv, weight * dw),
+                    *(radial * px, radial * py, radial * pz),
+                )
+                total = [old + new for old, new in zip(total, terms)]
+            for c in range(9):
+                sums[c, rows, :] = total[c]
         return unused
 
-    lax.fori_loop(0, ntarget // 8, one_group, 0)
+    lax.fori_loop(0, groups // TILES, some_tiles, 0)
+    for c in range(3, 6):
+        sums[c] = sums[c] - 3.0 * sums[c + 3]
     lane = lax.broadcasted_iota(jnp.int32, (ntarget, LANES), 1)
     table = jnp.zeros((ntarget, LANES), f32)
     for c in range(6):
@@ -288,7 +283,7 @@
         scratch_shapes=[
             pltpu.VMEM((groups, 7, 8, LANES), f32),
             pltpu.VMEM((6, ntarget, LANES), f32),
-            pltpu.VMEM((6, ntarget, LANES), f32),
+            pltpu.VMEM((9, ntarget, LANES), f32),
         ],
         compiler_params=PARAMS,
         name="forces",

time: 33.9 us -> 34.2 us (level)
  no operation moved by 1% of the time
where the time goes in v6:
time: 34.2 us; the launch traced here: 34 us
  blocking collectives  23.6 us (69%)
  Pallas kernels  9.78 us (29%)
  between operations  0.65 us (2%)
    all_to_all x1, blocking collectives, local(): gathered = lax.all_to_all(mine, 'ja', 0, 0)  14 us
    all_to_all x1, blocking collectives, local(): everyone = lax.all_to_all(packed, ('ia', 'ja'), 0, 0)  9.6 us
    pallas_call x1, Pallas kernels, local(): pl.pallas_call(force_kernel, out_shape=(pltpu.VMEM((rows * columns, 1, NE...  6.76 us
    pallas_call x1, Pallas kernels, local(): pl.pallas_call(functools.partial(finish_kernel, rows, columns), out_shape...  1.53 us
    pallas_call x1, Pallas kernels, local(): pl.pallas_call(gather_kernel, out_shape=(pltpu.VMEM((columns, 16, ntarget...  1.49 us

profile of v6, /device:TPU:0, one launch (start us, length us, event | category | flops | bytes accessed | tf_op | source)
XLA Modules:
  0.0 34.0 jit_solution(17875065649787534116)
XLA Ops:
  0.6 1.5 %gather.1 = (f32[8,16,128]{2,1,0:T(8,128)S(1)}, f32[3,8192]{1,0:T(4,128)S(1)}, f32[3,8192]{1,0:T(4,128)S(1)}, f32[3,8192]{1,0:T(4,128)S(1)}, f32[3,8192]{1,0:T(4...) custom-call(f32[3,8192]{1,0:T(4,128)} %refs_0_.1, f32[3,8192]{1,0:T(4,128)} %refs_1_.1, ...), custom_call_target="tpu_custom_call" | custom-call | tf_op jit(solution)/shard_map/gather/pallas_call | solution.py:262
  2.1 14.0 %all_to_all.10.gathered = f32[8,16,128]{2,1,0:T(8,128)S(1)} all-to-all(f32[8,16,128]{2,1,0:T(8,128)S(1)} %get-tuple-element.12), channel_id=1, replica_groups=mesh['ia'=4,'ja'=8] {'ja'}, dimensions={0} | all-to-all | bytes 131072 | tf_op jit(solution)/shard_map/all_to_all | solution.py:274
  16.1 6.8 %forces.1 = (f32[32,1,896]{2,1,0:T(1,128)S(1)}, f32[16,128]{1,0:T(8,128)S(1)}) custom-call(f32[8,16,128]{2,1,0:T(8,128)S(1)} %all_to_all.10.gathered, f32[3,8192]{1,0:T(4,128)S(1)} %get-tuple-element.13.pos, f32[3,8192]{1,0:T(4,128)S(1)} %get-tuple-element.14.vel, f32[3,8192]{1,0:T(4,128)S(1)} %get-tuple-element.15.acc, ...), custom_call_target="tpu_custom_call" | custom-call | tf_op jit(solution)/shard_map/forces/pallas_call | solution.py:275
  22.9 9.6 %all_to_all.11.everyone = f32[32,1,896]{2,1,0:T(1,128)S(1)} all-to-all(f32[32,1,896]{2,1,0:T(1,128)S(1)} %get-tuple-element.20), channel_id=1, replica_groups=mesh['ia'=4,'ja'=8] {'ia','ja'}, dimensions={0} | all-to-all | bytes 229376 | tf_op jit(solution)/shard_map/all_to_all | solution.py:291
  32.5 1.5 %finish.1 = (f32[12,128]{1,0:T(8,128)}, f32[12,8192]{1,0:T(8,128)}) custom-call(f32[32,1,896]{2,1,0:T(1,128)S(1)} %all_to_all.11.everyone, f32[16,128]{1,0:T(8,128)S(1)} %get-tuple-element.21.old, f32[3,8192]{1,0:T(4,128)S(1)} %get-tuple-element.13.pos, f32[3,8192]{1,0:T(4,128)S(1)} %get-tuple-element.14.vel, f32[3,8192]{1,0:T(4,128)S(1)} %get-tuple-element.15.acc, ...), custom_call_target="tpu_custom_call" | custom-call | tf_op jit(solution)/shard_map/finish/pallas_call | solution.py:292

commit v7 on v5

--- a/solution.py
+++ b/solution.py
@@ -10,7 +10,7 @@
 softening_length = 0.01
 base_step = 0.0625
 LANES = 128
-PIECES = 4
+PIECES = 8
 NEW_ROWS = 7
 f32 = jnp.float32
 VMEM = pl.BlockSpec(memory_space=pltpu.VMEM)
@@ -134,7 +134,7 @@
             du, dv, dw = (sources[t, 3] - tu, sources[t, 4] - tv, sources[t, 5] - tw)
             r2 = dx * dx + dy * dy + dz * dz + softening_length
             inv = lax.rsqrt(r2)
-            inv_sq = pl.reciprocal(r2, approx=True)
+            inv_sq = inv * inv
             weight = sources[t, 6] * inv * inv_sq
             radial = (dx * du + dy * dv + dz * dw) * inv_sq
             px, py, pz = (weight * dx, weight * dy, weight * dz)
@@ -276,7 +276,8 @@
         compiler_params=PARAMS,
         name="gather",
     )(*(pltpu.with_memory_space_constraint(x, pltpu.HBM) for x in given))
-    gathered = lax.all_to_all(mine, "ja", 0, 0)
+    backwards = [list(range(columns - 1, -1, -1))]
+    gathered = lax.all_to_all(mine, "ja", 0, 0, axis_index_groups=backwards)
     packed, old = pl.pallas_call(
         force_kernel,
         out_shape=(

time: 33.9 us -> 34.4 us (1.015)
  blocking collectives: 23.6 us -> 24 us
    all_to_all x1, blocking collectives: 9.6 us -> 12.7 us  [local(): everyone = lax.all_to_all(packed, ('ia', 'ja'), 0, 0)]
    all_to_all x1, blocking collectives: 14 us -> 11.3 us  [local(): gathered = lax.all_to_all(mine, 'ja', 0, 0, axis_index_groups=backwards)]
where the time goes in v7:
time: 34.4 us; the launch traced here: 34.1 us
  blocking collectives  24 us (70%)
  Pallas kernels  9.46 us (28%)
  between operations  0.65 us (2%)
    all_to_all x1, blocking collectives, local(): everyone = lax.all_to_all(packed, ('ia', 'ja'), 0, 0)  12.7 us
    all_to_all x1, blocking collectives, local(): gathered = lax.all_to_all(mine, 'ja', 0, 0, axis_index_groups=backwards)  11.3 us
    pallas_call x1, Pallas kernels, local(): pl.pallas_call(force_kernel, out_shape=(pltpu.VMEM((rows * columns, 1, NE...  6.43 us
    pallas_call x1, Pallas kernels, local(): pl.pallas_call(functools.partial(finish_kernel, rows, columns), out_shape...  1.54 us
    pallas_call x1, Pallas kernels, local(): pl.pallas_call(gather_kernel, out_shape=(pltpu.VMEM((columns, 16, ntarget...  1.49 us

profile of v7, /device:TPU:0, one launch (start us, length us, event | category | flops | bytes accessed | tf_op | source)
XLA Modules:
  0.0 34.1 jit_solution(17786574570807965939)
XLA Ops:
  0.6 1.5 %gather.1 = (f32[8,16,128]{2,1,0:T(8,128)S(1)}, f32[3,8192]{1,0:T(4,128)S(1)}, f32[3,8192]{1,0:T(4,128)S(1)}, f32[3,8192]{1,0:T(4,128)S(1)}, f32[3,8192]{1,0:T(4...) custom-call(f32[3,8192]{1,0:T(4,128)} %refs_0_.1, f32[3,8192]{1,0:T(4,128)} %refs_1_.1, ...), custom_call_target="tpu_custom_call" | custom-call | tf_op jit(solution)/shard_map/gather/pallas_call | solution.py:267
  2.1 11.3 %all_to_all.10.gathered = f32[8,16,128]{2,1,0:T(8,128)S(1)} all-to-all(f32[8,16,128]{2,1,0:T(8,128)S(1)} %get-tuple-element.12), channel_id=1, replica_groups={{7,6,5,4,3,2,1,0},{15,14,13,12,11,10,9,8},{23,22,21,20,19,18,17,16},{31..., dimensions={0} | all-to-all | bytes 131072 | tf_op jit(solution)/shard_map/all_to_all | solution.py:280
  13.5 6.4 %forces.1 = (f32[32,1,896]{2,1,0:T(1,128)S(1)}, f32[16,128]{1,0:T(8,128)S(1)}) custom-call(f32[8,16,128]{2,1,0:T(8,128)S(1)} %all_to_all.10.gathered, f32[3,8192]{1,0:T(4,128)S(1)} %get-tuple-element.13.pos, f32[3,8192]{1,0:T(4,128)S(1)} %get-tuple-element.14.vel, f32[3,8192]{1,0:T(4,128)S(1)} %get-tuple-element.15.acc, ...), custom_call_target="tpu_custom_call" | custom-call | tf_op jit(solution)/shard_map/forces/pallas_call | solution.py:281
  19.9 12.7 %all_to_all.11.everyone = f32[32,1,896]{2,1,0:T(1,128)S(1)} all-to-all(f32[32,1,896]{2,1,0:T(1,128)S(1)} %get-tuple-element.20), channel_id=1, replica_groups=mesh['ia'=4,'ja'=8] {'ia','ja'}, dimensions={0} | all-to-all | bytes 229376 | tf_op jit(solution)/shard_map/all_to_all | solution.py:297
  32.6 1.5 %finish.1 = (f32[12,128]{1,0:T(8,128)}, f32[12,8192]{1,0:T(8,128)}) custom-call(f32[32,1,896]{2,1,0:T(1,128)S(1)} %all_to_all.11.everyone, f32[16,128]{1,0:T(8,128)S(1)} %get-tuple-element.21.old, f32[3,8192]{1,0:T(4,128)S(1)} %get-tuple-element.13.pos, f32[3,8192]{1,0:T(4,128)S(1)} %get-tuple-element.14.vel, f32[3,8192]{1,0:T(4,128)S(1)} %get-tuple-element.15.acc, ...), custom_call_target="tpu_custom_call" | custom-call | tf_op jit(solution)/shard_map/finish/pallas_call | solution.py:298

commit v8 on v7

--- a/solution.py
+++ b/solution.py
@@ -173,7 +173,7 @@
 
 
 def finish_kernel(
-    rows, columns, everyone, old, pos, vel, acc, jrk, levels, targets_out, stars_out,
+    rows, columns, same_core, other_core, old, pos, vel, acc, jrk, levels, targets_out, stars_out,
     targets_new, stars_new, rowed, sems
 ):
     groups = levels.shape[0]
@@ -184,14 +184,16 @@
     forces, where_hi, where_lo = ([], [], [])
     mine = jnp.zeros((8, ntarget), f32)
     for r in range(rows):
-        total = everyone[r * columns]
+        everyone = same_core if r < rows // 2 else other_core
+        first = r % (rows // 2) * columns
+        total = everyone[first]
         for c in range(1, columns):
-            total = total + everyone[r * columns + c]
+            total = total + everyone[first + c]
         for c in range(6):
             rowed[r, c : c + 1, :] = total[:, tile(c)]
         forces.append(rowed[r])
-        mine = jnp.where(me == r, forces[r], mine)
-        offset = everyone[r * columns][:, tile(6)].astype(jnp.int32) - base
+        mine = jnp.where(rows // 2 - 1 - (me >> 1) == r, forces[r], mine)
+        offset = everyone[first][:, tile(6)].astype(jnp.int32) - base
         where_hi.append(offset >> 7)
         where_lo.append(offset & (LANES - 1))
 
@@ -281,7 +283,7 @@
     packed, old = pl.pallas_call(
         force_kernel,
         out_shape=(
-            pltpu.VMEM((rows * columns, 1, NEW_ROWS * ntarget), f32),
+            pltpu.VMEM((rows // 2 * columns, 1, NEW_ROWS * ntarget), f32),
             pltpu.VMEM((16, ntarget), f32),
         ),
         in_specs=[VMEM] * 8,
@@ -294,14 +296,19 @@
         compiler_params=PARAMS,
         name="forces",
     )(gathered, *kept)
-    everyone = lax.all_to_all(packed, ("ia", "ja"), 0, 0)
+    backwards = [
+        [r * columns + c for r in range(rows - 2 + core, -1, -2) for c in range(columns - 1, -1, -1)]
+        for core in range(2)
+    ]
+    same_core = lax.all_to_all(packed, ("ia", "ja"), 0, 0, axis_index_groups=backwards)
+    other_core = lax.ppermute(same_core, "ia", [(r, r ^ 1) for r in range(rows)])
     return pl.pallas_call(
         functools.partial(finish_kernel, rows, columns),
         out_shape=(
             jax.ShapeDtypeStruct((12, ntarget), f32),
             jax.ShapeDtypeStruct((12, nlocal), f32),
         ),
-        in_specs=[VMEM] * 7,
+        in_specs=[VMEM] * 8,
         out_specs=(HBM, HBM),
         scratch_shapes=[
             pltpu.VMEM((12, ntarget), f32),
@@ -311,7 +318,7 @@
         ],
         compiler_params=PARAMS,
         name="finish",
-    )(everyone, old, *kept[:5])
+    )(same_core, other_core, old, *kept[:5])
 
 
 def solution(mesh):

time: 34.4 us -> 33 us (0.959)
  blocking collectives: 24 us -> 21.5 us
  waiting for transfers between devices: 0 us -> 1.24 us
    all_to_all x1, blocking collectives: 12.7 us -> 10.1 us  [local(): lax.all_to_all(packed, ('ia', 'ja'), 0, 0, axis_index_groups=backwards)]
    ppermute x0 -> x1, waiting for transfers between devices: none -> 1.24 us  [local(): lax.ppermute(same_core, 'ia', [(r, r ^ 1) for r in range(rows)])]
  transfers between devices with their start and end apart: 0 -> 1, of which waited for: 0 -> 1; matrix products, arithmetic and copies ran while one was open for 0% -> 0% of each run, Pallas kernels for 0% -> 0%
where the time goes in v8:
time: 33 us; the launch traced here: 32.8 us
  blocking collectives  21.5 us (65%)
  Pallas kernels  9.43 us (29%)
  waiting for transfers between devices  1.24 us (4%)
  between operations  0.65 us (2%)
    all_to_all x1, blocking collectives, local(): gathered = lax.all_to_all(mine, 'ja', 0, 0, axis_index_groups=backwards)  11.3 us
    all_to_all x1, blocking collectives, local(): lax.all_to_all(packed, ('ia', 'ja'), 0, 0, axis_index_groups=backwards)  10.1 us
    pallas_call x1, Pallas kernels, local(): pl.pallas_call(force_kernel, out_shape=(pltpu.VMEM((rows // 2 * columns,...  6.4 us
    pallas_call x1, Pallas kernels, local(): pl.pallas_call(functools.partial(finish_kernel, rows, columns), out_shape...  1.54 us
    pallas_call x1, Pallas kernels, local(): pl.pallas_call(gather_kernel, out_shape=(pltpu.VMEM((columns, 16, ntarget...  1.49 us
    ppermute x1, waiting for transfers between devices, local(): lax.ppermute(same_core, 'ia', [(r, r ^ 1) for r in range(rows)])  1.24 us
  transfers between devices with their start and end apart: 1, of which 1 were waited for; matrix products, arithmetic and copies ran while one was open for 0% of the time, Pallas kernels for 0%

profile of v8, /device:TPU:0, one launch (start us, length us, event | category | flops | bytes accessed | tf_op | source)
XLA Modules:
  0.0 32.8 jit_solution(10854765365203894015)
XLA Ops:
  0.6 1.5 %gather.1 = (f32[8,16,128]{2,1,0:T(8,128)S(1)}, f32[3,8192]{1,0:T(4,128)S(1)}, f32[3,8192]{1,0:T(4,128)S(1)}, f32[3,8192]{1,0:T(4,128)S(1)}, f32[3,8192]{1,0:T(4...) custom-call(f32[3,8192]{1,0:T(4,128)} %refs_0_.1, f32[3,8192]{1,0:T(4,128)} %refs_1_.1, ...), custom_call_target="tpu_custom_call" | custom-call | tf_op jit(solution)/shard_map/gather/pallas_call | solution.py:269
  2.1 11.3 %all_to_all.10.gathered = f32[8,16,128]{2,1,0:T(8,128)S(1)} all-to-all(f32[8,16,128]{2,1,0:T(8,128)S(1)} %get-tuple-element.12), channel_id=1, replica_groups={{7,6,5,4,3,2,1,0},{15,14,13,12,11,10,9,8},{23,22,21,20,19,18,17,16},{31..., dimensions={0} | all-to-all | bytes 131072 | tf_op jit(solution)/shard_map/all_to_all | solution.py:282
  13.5 6.4 %forces.1 = (f32[16,1,896]{2,1,0:T(1,128)S(1)}, f32[16,128]{1,0:T(8,128)S(1)}) custom-call(f32[8,16,128]{2,1,0:T(8,128)S(1)} %all_to_all.10.gathered, f32[3,8192]{1,0:T(4,128)S(1)} %get-tuple-element.13.pos, f32[3,8192]{1,0:T(4,128)S(1)} %get-tuple-element.14.vel, f32[3,8192]{1,0:T(4,128)S(1)} %get-tuple-element.15.acc, ...), custom_call_target="tpu_custom_call" | custom-call | tf_op jit(solution)/shard_map/forces/pallas_call | solution.py:283
  19.9 10.1 %all_to_all.11.same_core = f32[16,1,896]{2,1,0:T(1,128)S(1)} all-to-all(f32[16,1,896]{2,1,0:T(1,128)S(1)} %get-tuple-element.20), channel_id=1, replica_groups={{23,22,21,20,19,18,17,16,7,6,5,4,3,2,1,0},{31,30,29,28,27,26,25,24,15,1..., dimensions={0} | all-to-all | bytes 114688 | tf_op jit(solution)/shard_map/all_to_all | solution.py:303
  30.0 0.0 collective-permute-start
  30.0 1.2 %collective-permute-done.other_core = f32[16,1,896]{2,1,0:T(1,128)S(1)} collective-permute-done((f32[16,1,896]{2,1,0:T(1,128)S(1)}, f32[16,1,896]{2,1,0:T(1,128)S(1)}, u32[]{:S(2)}, u32[]{:S(2)}) %collective-permute-start) | collective-permute-done | bytes 57376 | tf_op jit(solution)/shard_map/ppermute | solution.py:304
  31.2 1.5 %finish.1 = (f32[12,128]{1,0:T(8,128)}, f32[12,8192]{1,0:T(8,128)}) custom-call(f32[16,1,896]{2,1,0:T(1,128)S(1)} %all_to_all.11.same_core, f32[16,1,896]{2,1,0:T(1,128)S(1)} %collective-permute-done.other_core, f32[16,128]{1,0:T(8,128)S(1)} %get-tuple-element.21.old, f32[3,8192]{1,0:T(4,128)S(1)} %get-tuple-element.13.pos, ...), custom_call_target="tpu_custom_call" | custom-call | tf_op jit(solution)/shard_map/finish/pallas_call | solution.py:305
Async XLA Ops:
  30.0 1.2 %collective-permute-start = (f32[16,1,896]{2,1,0:T(1,128)S(1)}, f32[16,1,896]{2,1,0:T(1,128)S(1)}, u32[]{:S(2)}, u32[]{:S(2)}) collective-permute-start(f32[16,1,896]{2,1,0:T(1,128)S(1)} %all_to_all.11.same_core), channel_id=1, source_target_pairs={{0,8},{8,0},{16,24},{24,16},{1,9},{9,1},{17,25},{25,17},{2,10},{10... | collective-permute-start | bytes 172040 | tf_op jit(solution)/shard_map/ppermute | solution.py:304

commit v9 on v8

--- a/solution.py
+++ b/solution.py
@@ -43,6 +43,16 @@
     v1 = v0 + half * (a0 + a1) + quad * (j0 - j1)
     x1 = x0 + half * (v0 + v1) + quad * (a0 - a1)
     return (x1, v1)
+
+
+def column_order(columns):
+    first = max(columns - 3, 0)
+    return [first, *(c for c in range(columns - 1, -1, -1) if c != first)]
+
+
+def pair_order(rows, columns):
+    late = [columns - 1, columns - 2]
+    return [(h, c) for c in (*late, *range(columns - 2)) for h in range(rows // 2)]
 
 
 def tile(t):
@@ -183,16 +193,17 @@
 
     forces, where_hi, where_lo = ([], [], [])
     mine = jnp.zeros((8, ntarget), f32)
+    order = pair_order(rows, columns)
     for r in range(rows):
         everyone = same_core if r < rows // 2 else other_core
-        first = r % (rows // 2) * columns
+        first, *others = [k for k, (h, _) in enumerate(order) if h == r % (rows // 2)]
         total = everyone[first]
-        for c in range(1, columns):
-            total = total + everyone[first + c]
+        for k in others:
+            total = total + everyone[k]
         for c in range(6):
             rowed[r, c : c + 1, :] = total[:, tile(c)]
         forces.append(rowed[r])
-        mine = jnp.where(rows // 2 - 1 - (me >> 1) == r, forces[r], mine)
+        mine = jnp.where((me >> 1) == r, forces[r], mine)
         offset = everyone[first][:, tile(6)].astype(jnp.int32) - base
         where_hi.append(offset >> 7)
         where_lo.append(offset & (LANES - 1))
@@ -278,8 +289,7 @@
         compiler_params=PARAMS,
         name="gather",
     )(*(pltpu.with_memory_space_constraint(x, pltpu.HBM) for x in given))
-    backwards = [list(range(columns - 1, -1, -1))]
-    gathered = lax.all_to_all(mine, "ja", 0, 0, axis_index_groups=backwards)
+    gathered = lax.all_to_all(mine, "ja", 0, 0, axis_index_groups=[column_order(columns)])
     packed, old = pl.pallas_call(
         force_kernel,
         out_shape=(
@@ -296,11 +306,9 @@
         compiler_params=PARAMS,
         name="forces",
     )(gathered, *kept)
-    backwards = [
-        [r * columns + c for r in range(rows - 2 + core, -1, -2) for c in range(columns - 1, -1, -1)]
-        for core in range(2)
-    ]
-    same_core = lax.all_to_all(packed, ("ia", "ja"), 0, 0, axis_index_groups=backwards)
+    order = pair_order(rows, columns)
+    lists = [[(2 * h + core) * columns + c for h, c in order] for core in range(2)]
+    same_core = lax.all_to_all(packed, ("ia", "ja"), 0, 0, axis_index_groups=lists)
     other_core = lax.ppermute(same_core, "ia", [(r, r ^ 1) for r in range(rows)])
     return pl.pallas_call(
         functools.partial(finish_kernel, rows, columns),

time: 33 us -> 33.4 us (1.012)
    all_to_all x2, blocking collectives: 21.5 us -> 21.8 us  [the longest x1 11.2 us: local(): lax.all_to_all(mine, 'ja', 0, 0, axis_index_groups=[column_order(columns)])]
where the time goes in v9:
time: 33.4 us; the launch traced here: 33.2 us
  blocking collectives  21.8 us (65%)
  Pallas kernels  9.43 us (28%)
  waiting for transfers between devices  1.24 us (4%)
  between operations  0.65 us (2%)
    all_to_all x1, blocking collectives, local(): lax.all_to_all(mine, 'ja', 0, 0, axis_index_groups=[column_order(columns)])  11.2 us
    all_to_all x1, blocking collectives, local(): lax.all_to_all(packed, ('ia', 'ja'), 0, 0, axis_index_groups=lists)  10.7 us
    pallas_call x1, Pallas kernels, local(): pl.pallas_call(force_kernel, out_shape=(pltpu.VMEM((rows // 2 * columns,...  6.4 us
    pallas_call x1, Pallas kernels, local(): pl.pallas_call(functools.partial(finish_kernel, rows, columns), out_shape...  1.54 us
    pallas_call x1, Pallas kernels, local(): pl.pallas_call(gather_kernel, out_shape=(pltpu.VMEM((columns, 16, ntarget...  1.49 us
    ppermute x1, waiting for transfers between devices, local(): lax.ppermute(same_core, 'ia', [(r, r ^ 1) for r in range(rows)])  1.24 us
  transfers between devices with their start and end apart: 1, of which 1 were waited for; matrix products, arithmetic and copies ran while one was open for 0% of the time, Pallas kernels for 0%

profile of v9, /device:TPU:0, one launch (start us, length us, event | category | flops | bytes accessed | tf_op | source)
XLA Modules:
  0.0 33.2 jit_solution(14106281020062442901)
XLA Ops:
  0.6 1.5 %gather.1 = (f32[8,16,128]{2,1,0:T(8,128)S(1)}, f32[3,8192]{1,0:T(4,128)S(1)}, f32[3,8192]{1,0:T(4,128)S(1)}, f32[3,8192]{1,0:T(4,128)S(1)}, f32[3,8192]{1,0:T(4...) custom-call(f32[3,8192]{1,0:T(4,128)} %refs_0_.1, f32[3,8192]{1,0:T(4,128)} %refs_1_.1, ...), custom_call_target="tpu_custom_call" | custom-call | tf_op jit(solution)/shard_map/gather/pallas_call | solution.py:280
  2.1 11.2 %all_to_all.10.gathered = f32[8,16,128]{2,1,0:T(8,128)S(1)} all-to-all(f32[8,16,128]{2,1,0:T(8,128)S(1)} %get-tuple-element.12), channel_id=1, replica_groups={{5,7,6,4,3,2,1,0},{13,15,14,12,11,10,9,8},{21,23,22,20,19,18,17,16},{29..., dimensions={0} | all-to-all | bytes 131072 | tf_op jit(solution)/shard_map/all_to_all | solution.py:292
  13.3 6.4 %forces.1 = (f32[16,1,896]{2,1,0:T(1,128)S(1)}, f32[16,128]{1,0:T(8,128)S(1)}) custom-call(f32[8,16,128]{2,1,0:T(8,128)S(1)} %all_to_all.10.gathered, f32[3,8192]{1,0:T(4,128)S(1)} %get-tuple-element.13.pos, f32[3,8192]{1,0:T(4,128)S(1)} %get-tuple-element.14.vel, f32[3,8192]{1,0:T(4,128)S(1)} %get-tuple-element.15.acc, ...), custom_call_target="tpu_custom_call" | custom-call | tf_op jit(solution)/shard_map/forces/pallas_call | solution.py:293
  19.7 10.7 %all_to_all.11.same_core = f32[16,1,896]{2,1,0:T(1,128)S(1)} all-to-all(f32[16,1,896]{2,1,0:T(1,128)S(1)} %get-tuple-element.20), channel_id=1, replica_groups={{7,23,6,22,0,16,1,17,2,18,3,19,4,20,5,21},{15,31,14,30,8,24,9,25,10,26,..., dimensions={0} | all-to-all | bytes 114688 | tf_op jit(solution)/shard_map/all_to_all | solution.py:311
  30.4 0.0 collective-permute-start
  30.4 1.2 %collective-permute-done.other_core = f32[16,1,896]{2,1,0:T(1,128)S(1)} collective-permute-done((f32[16,1,896]{2,1,0:T(1,128)S(1)}, f32[16,1,896]{2,1,0:T(1,128)S(1)}, u32[]{:S(2)}, u32[]{:S(2)}) %collective-permute-start) | collective-permute-done | bytes 57376 | tf_op jit(solution)/shard_map/ppermute | solution.py:312
  31.6 1.5 %finish.1 = (f32[12,128]{1,0:T(8,128)}, f32[12,8192]{1,0:T(8,128)}) custom-call(f32[16,1,896]{2,1,0:T(1,128)S(1)} %all_to_all.11.same_core, f32[16,1,896]{2,1,0:T(1,128)S(1)} %collective-permute-done.other_core, f32[16,128]{1,0:T(8,128)S(1)} %get-tuple-element.21.old, f32[3,8192]{1,0:T(4,128)S(1)} %get-tuple-element.13.pos, ...), custom_call_target="tpu_custom_call" | custom-call | tf_op jit(solution)/shard_map/finish/pallas_call | solution.py:313
Async XLA Ops:
  30.4 1.2 %collective-permute-start = (f32[16,1,896]{2,1,0:T(1,128)S(1)}, f32[16,1,896]{2,1,0:T(1,128)S(1)}, u32[]{:S(2)}, u32[]{:S(2)}) collective-permute-start(f32[16,1,896]{2,1,0:T(1,128)S(1)} %all_to_all.11.same_core), channel_id=1, source_target_pairs={{0,8},{8,0},{16,24},{24,16},{1,9},{9,1},{17,25},{25,17},{2,10},{10... | collective-permute-start | bytes 172040 | tf_op jit(solution)/shard_map/ppermute | solution.py:312

commit v10 on v9

--- a/solution.py
+++ b/solution.py
@@ -51,8 +51,8 @@
 
 
 def pair_order(rows, columns):
-    late = [columns - 1, columns - 2]
-    return [(h, c) for c in (*late, *range(columns - 2)) for h in range(rows // 2)]
+    natural = [(h, c) for h in range(rows // 2) for c in range(columns)]
+    return natural[-1:] + natural[:-1]
 
 
 def tile(t):

time: 33.4 us -> 32.5 us (0.973)
  blocking collectives: 21.8 us -> 21 us
    all_to_all x1, blocking collectives: 10.7 us -> 9.82 us  [local(): lax.all_to_all(packed, ('ia', 'ja'), 0, 0, axis_index_groups=lists)]
where the time goes in v10:
time: 32.5 us; the launch traced here: 32.3 us
  blocking collectives  21 us (65%)
  Pallas kernels  9.43 us (29%)
  waiting for transfers between devices  1.24 us (4%)
  between operations  0.65 us (2%)
    all_to_all x1, blocking collectives, local(): lax.all_to_all(mine, 'ja', 0, 0, axis_index_groups=[column_order(columns)])  11.2 us
    all_to_all x1, blocking collectives, local(): lax.all_to_all(packed, ('ia', 'ja'), 0, 0, axis_index_groups=lists)  9.82 us
    pallas_call x1, Pallas kernels, local(): pl.pallas_call(force_kernel, out_shape=(pltpu.VMEM((rows // 2 * columns,...  6.4 us
    pallas_call x1, Pallas kernels, local(): pl.pallas_call(functools.partial(finish_kernel, rows, columns), out_shape...  1.54 us
    pallas_call x1, Pallas kernels, local(): pl.pallas_call(gather_kernel, out_shape=(pltpu.VMEM((columns, 16, ntarget...  1.49 us
    ppermute x1, waiting for transfers between devices, local(): lax.ppermute(same_core, 'ia', [(r, r ^ 1) for r in range(rows)])  1.24 us
  transfers between devices with their start and end apart: 1, of which 1 were waited for; matrix products, arithmetic and copies ran while one was open for 0% of the time, Pallas kernels for 0%

profile of v10, /device:TPU:0, one launch (start us, length us, event | category | flops | bytes accessed | tf_op | source)
XLA Modules:
  0.0 32.3 jit_solution(12943629115929999177)
XLA Ops:
  0.6 1.5 %gather.1 = (f32[8,16,128]{2,1,0:T(8,128)S(1)}, f32[3,8192]{1,0:T(4,128)S(1)}, f32[3,8192]{1,0:T(4,128)S(1)}, f32[3,8192]{1,0:T(4,128)S(1)}, f32[3,8192]{1,0:T(4...) custom-call(f32[3,8192]{1,0:T(4,128)} %refs_0_.1, f32[3,8192]{1,0:T(4,128)} %refs_1_.1, ...), custom_call_target="tpu_custom_call" | custom-call | tf_op jit(solution)/shard_map/gather/pallas_call | solution.py:280
  2.1 11.2 %all_to_all.10.gathered = f32[8,16,128]{2,1,0:T(8,128)S(1)} all-to-all(f32[8,16,128]{2,1,0:T(8,128)S(1)} %get-tuple-element.12), channel_id=1, replica_groups={{5,7,6,4,3,2,1,0},{13,15,14,12,11,10,9,8},{21,23,22,20,19,18,17,16},{29..., dimensions={0} | all-to-all | bytes 131072 | tf_op jit(solution)/shard_map/all_to_all | solution.py:292
  13.3 6.4 %forces.1 = (f32[16,1,896]{2,1,0:T(1,128)S(1)}, f32[16,128]{1,0:T(8,128)S(1)}) custom-call(f32[8,16,128]{2,1,0:T(8,128)S(1)} %all_to_all.10.gathered, f32[3,8192]{1,0:T(4,128)S(1)} %get-tuple-element.13.pos, f32[3,8192]{1,0:T(4,128)S(1)} %get-tuple-element.14.vel, f32[3,8192]{1,0:T(4,128)S(1)} %get-tuple-element.15.acc, ...), custom_call_target="tpu_custom_call" | custom-call | tf_op jit(solution)/shard_map/forces/pallas_call | solution.py:293
  19.7 9.8 %all_to_all.11.same_core = f32[16,1,896]{2,1,0:T(1,128)S(1)} all-to-all(f32[16,1,896]{2,1,0:T(1,128)S(1)} %get-tuple-element.20), channel_id=1, replica_groups={{23,0,1,2,3,4,5,6,7,16,17,18,19,20,21,22},{31,8,9,10,11,12,13,14,15,24,..., dimensions={0} | all-to-all | bytes 114688 | tf_op jit(solution)/shard_map/all_to_all | solution.py:311
  29.5 0.0 collective-permute-start
  29.5 1.2 %collective-permute-done.other_core = f32[16,1,896]{2,1,0:T(1,128)S(1)} collective-permute-done((f32[16,1,896]{2,1,0:T(1,128)S(1)}, f32[16,1,896]{2,1,0:T(1,128)S(1)}, u32[]{:S(2)}, u32[]{:S(2)}) %collective-permute-start) | collective-permute-done | bytes 57376 | tf_op jit(solution)/shard_map/ppermute | solution.py:312
  30.8 1.5 %finish.1 = (f32[12,128]{1,0:T(8,128)}, f32[12,8192]{1,0:T(8,128)}) custom-call(f32[16,1,896]{2,1,0:T(1,128)S(1)} %all_to_all.11.same_core, f32[16,1,896]{2,1,0:T(1,128)S(1)} %collective-permute-done.other_core, f32[16,128]{1,0:T(8,128)S(1)} %get-tuple-element.21.old, f32[3,8192]{1,0:T(4,128)S(1)} %get-tuple-element.13.pos, ...), custom_call_target="tpu_custom_call" | custom-call | tf_op jit(solution)/shard_map/finish/pallas_call | solution.py:313
Async XLA Ops:
  29.5 1.2 %collective-permute-start = (f32[16,1,896]{2,1,0:T(1,128)S(1)}, f32[16,1,896]{2,1,0:T(1,128)S(1)}, u32[]{:S(2)}, u32[]{:S(2)}) collective-permute-start(f32[16,1,896]{2,1,0:T(1,128)S(1)} %all_to_all.11.same_core), channel_id=1, source_target_pairs={{0,8},{8,0},{16,24},{24,16},{1,9},{9,1},{17,25},{25,17},{2,10},{10... | collective-permute-start | bytes 172040 | tf_op jit(solution)/shard_map/ppermute | solution.py:312

commit v11 on v10

--- a/solution.py
+++ b/solution.py
@@ -11,7 +11,7 @@
 base_step = 0.0625
 LANES = 128
 PIECES = 8
-NEW_ROWS = 7
+NEW_ROWS = 9
 f32 = jnp.float32
 VMEM = pl.BlockSpec(memory_space=pltpu.VMEM)
 HBM = pl.BlockSpec(memory_space=pltpu.HBM)
@@ -108,33 +108,46 @@
     late.wait()
 
 
-def force_kernel(
-    gathered, pos, vel, acc, jrk, levels, masses, active, packed, old, sources, targets, sums
-):
-    groups = levels.shape[0]
-    ntarget = active.shape[1]
-    state = gathered[0]
-    for k in range(1, gathered.shape[0]):
-        state = state + gathered[k]
-    old[...] = state
-    tpos, tvel = predict(
-        state[0:3], state[3:6], state[6:9], state[9:12], step_factors(state[12:13])
-    )
-    columns = jnp.transpose(
-        jnp.concatenate([tpos, tvel, jnp.zeros((LANES - 6, ntarget), f32)], axis=0)
-    )
+def pack(values):
+    quarter = lax.broadcasted_iota(jnp.int32, (1, LANES), 1) // (LANES // 4)
+    rows = []
+    for part in (values[:4], values[4:]):
+        row = jnp.zeros((1, LANES), f32)
+        for n, value in enumerate(part):
+            turned = pltpu.roll(value, (n + 1) * (LANES // 4) % LANES, 1)
+            row = jnp.where(quarter == n, turned, row)
+        rows.append(row)
+    return rows
+
+
+def unpack(rows):
+    last = lax.broadcasted_iota(jnp.int32, (1, LANES), 1) >= LANES - LANES // 4
+    values = []
     for c in range(6):
-        targets[c] = jnp.broadcast_to(columns[:, c : c + 1], (ntarget, LANES))
-    factors = step_factors(elapsed_of(levels[...]))
-    for t in range(groups):
-        spos, svel = predict(
-            *(x[:, tile(t)] for x in (pos, vel, acc, jrk)), [f[t : t + 1] for f in factors]
-        )
-        for c in range(3):
-            sources[t, c] = jnp.broadcast_to(spos[c : c + 1], (8, LANES))
-            sources[t, 3 + c] = jnp.broadcast_to(svel[c : c + 1], (8, LANES))
-        sources[t, 6] = jnp.broadcast_to(masses[t : t + 1, :], (8, LANES))
-
+        turned = pltpu.roll(rows[c // 4], (3 - c % 4) * (LANES // 4), 1)
+        values.append(jnp.where(last, turned, 0.0))
+    return values
+
+
+def spread(values, targets, rows):
+    fill = jnp.zeros((LANES - 6, LANES), f32)
+    columns = jnp.transpose(jnp.concatenate([*values, fill], axis=0))
+    for c in range(6):
+        targets[c] = jnp.broadcast_to(columns[rows, c : c + 1], targets.shape[1:])
+
+
+def predicted(state):
+    return predict(*(state[n : n + 3] for n in (0, 3, 6, 9)), step_factors(state[12:13]))
+
+
+def summed(blocks):
+    total = blocks[0]
+    for k in range(1, blocks.shape[0]):
+        total = total + blocks[k]
+    return total
+
+
+def pair_sums(sources, targets, sums, count):
     def one_group(g, unused):
         rows = pl.ds(pl.multiple_of(g * 8, 8), 8)
         tx, ty, tz, tu, tv, tw = (targets[c, rows, :] for c in range(6))
@@ -163,28 +176,78 @@
 
         zero = jnp.zeros((8, LANES), f32)
         ax, ay, az, jx, jy, jz, kx, ky, kz = lax.fori_loop(
-            0, groups, one_tile, (zero,) * 9, unroll=32
+            0, sources.shape[0], one_tile, (zero,) * 9, unroll=32
         )
         for c, value in enumerate((ax, ay, az, jx - 3.0 * kx, jy - 3.0 * ky, jz - 3.0 * kz)):
             sums[c, rows, :] = value
         return unused
 
-    lax.fori_loop(0, ntarget // 8, one_group, 0)
-    lane = lax.broadcasted_iota(jnp.int32, (ntarget, LANES), 1)
-    table = jnp.zeros((ntarget, LANES), f32)
+    lax.fori_loop(0, count, one_group, 0)
+
+
+def as_rows(sums):
+    count = sums.shape[1]
+    lane = lax.broadcasted_iota(jnp.int32, (count, LANES), 1)
+    table = jnp.zeros((count, LANES), f32)
     for c in range(6):
         table = jnp.where(lane == c, jnp.sum(sums[c], axis=1, keepdims=True), table)
-    table = jnp.transpose(table)[0:8]
+    if count < LANES:
+        table = jnp.concatenate([jnp.zeros((LANES - count, LANES), f32), table], axis=0)
+    return jnp.transpose(table)[0:8]
+
+
+def force_kernel(
+    gathered, pos, vel, acc, jrk, levels, masses, active, own, old, sources, targets, sums
+):
+    groups = levels.shape[0]
+    ntarget = active.shape[1]
+    state = summed(gathered)
+    old[...] = state
+    tpos, tvel = predicted(state)
+    spread([tpos, tvel], targets, slice(0, ntarget))
+    factors = step_factors(elapsed_of(levels[...]))
+    for t in range(groups):
+        spos, svel = predict(
+            *(x[:, tile(t)] for x in (pos, vel, acc, jrk)), [f[t : t + 1] for f in factors]
+        )
+        for c in range(3):
+            sources[t, c] = jnp.broadcast_to(spos[c : c + 1], (8, LANES))
+            sources[t, 3 + c] = jnp.broadcast_to(svel[c : c + 1], (8, LANES))
+        sources[t, 6] = jnp.broadcast_to(masses[t : t + 1, :], (8, LANES))
+    given = ntarget // 4
+    for c in range(6):
+        sums[c, ntarget - given :] = jnp.zeros((given, LANES), f32)
+    mine = (ntarget - given) // 8 + given // 8 * (lax.axis_index("ia") % 2)
+    pair_sums(sources, targets, sums, mine)
     row = lax.broadcasted_iota(jnp.int32, (8, ntarget), 0)
-    table = jnp.where(row == 6, active[...].astype(f32), table)
+    own[...] = jnp.where(row == 6, active[...].astype(f32), as_rows(sums))
+
+
+def taken_kernel(handed, sources, own, packed, taken, targets, sums):
+    given = targets.shape[1]
+    taken[...] = jnp.zeros(taken.shape, f32)
+
+    @pl.when(lax.axis_index("ia") % 2 == 1)
+    def _():
+        tpos, tvel = predicted(summed(handed))
+        spread([tpos, tvel], targets, slice(LANES - given, LANES))
+        pair_sums(sources, targets, sums, given // 8)
+        for n, value in enumerate(pack([row for row in split_rows(as_rows(sums), 6)])):
+            taken[n : n + 1, :] = value
+
+    rows = [*split_rows(own[...], 7), *split_rows(taken[...], 2)]
     for k in range(packed.shape[0]):
-        for c in range(NEW_ROWS):
-            packed[k, :, tile(c)] = table[c : c + 1]
+        for c, value in enumerate(rows):
+            packed[k, :, tile(c)] = value
+
+
+def split_rows(x, count):
+    return [x[c : c + 1] for c in range(count)]
 
 
 def finish_kernel(
     rows, columns, same_core, other_core, old, pos, vel, acc, jrk, levels, targets_out, stars_out,
-    targets_new, stars_new, rowed, sems
+    targets_new, stars_new, rowed, taken, sems
 ):
     groups = levels.shape[0]
     ntarget = old.shape[1]
@@ -194,19 +257,23 @@
     forces, where_hi, where_lo = ([], [], [])
     mine = jnp.zeros((8, ntarget), f32)
     order = pair_order(rows, columns)
+    half = rows // 2
     for r in range(rows):
-        everyone = same_core if r < rows // 2 else other_core
-        first, *others = [k for k, (h, _) in enumerate(order) if h == r % (rows // 2)]
+        everyone, other = (same_core, r + half) if r < half else (other_core, r - half)
+        first, *others = [k for k, (h, _) in enumerate(order) if h == r % half]
         total = everyone[first]
         for k in others:
             total = total + everyone[k]
         for c in range(6):
             rowed[r, c : c + 1, :] = total[:, tile(c)]
-        forces.append(rowed[r])
-        mine = jnp.where((me >> 1) == r, forces[r], mine)
+        for c, value in enumerate(unpack([total[:, tile(7)], total[:, tile(8)]])):
+            taken[other, c : c + 1, :] = value
         offset = everyone[first][:, tile(6)].astype(jnp.int32) - base
         where_hi.append(offset >> 7)
         where_lo.append(offset & (LANES - 1))
+    for r in range(rows):
+        forces.append(rowed[r] + taken[r])
+        mine = jnp.where((me >> 1) == r, forces[r], mine)
 
     o = old[...]
     factors = correction_factors(o[12:13])
@@ -290,22 +357,38 @@
         name="gather",
     )(*(pltpu.with_memory_space_constraint(x, pltpu.HBM) for x in given))
     gathered = lax.all_to_all(mine, "ja", 0, 0, axis_index_groups=[column_order(columns)])
-    packed, old = pl.pallas_call(
+    handed = lax.ppermute(gathered, "ia", [(r, r + 1) for r in range(0, rows, 2)])
+    own, old, sources = pl.pallas_call(
         force_kernel,
         out_shape=(
-            pltpu.VMEM((rows // 2 * columns, 1, NEW_ROWS * ntarget), f32),
+            pltpu.VMEM((8, ntarget), f32),
             pltpu.VMEM((16, ntarget), f32),
+            pltpu.VMEM((groups, 7, 8, LANES), f32),
         ),
         in_specs=[VMEM] * 8,
-        out_specs=(VMEM, VMEM),
+        out_specs=(VMEM,) * 3,
+        scratch_shapes=[pltpu.VMEM((6, ntarget, LANES), f32)] * 2,
+        compiler_params=PARAMS,
+        cost_estimate=pl.CostEstimate(
+            flops=40 * nlocal * ntarget,
+            bytes_accessed=4 * 80 * nlocal,
+            transcendentals=nlocal * ntarget,
+        ),
+        name="forces",
+    )(gathered, *kept)
+    packed = pl.pallas_call(
+        taken_kernel,
+        out_shape=pltpu.VMEM((rows // 2 * columns, 1, NEW_ROWS * ntarget), f32),
+        in_specs=[VMEM] * 3,
+        out_specs=VMEM,
         scratch_shapes=[
-            pltpu.VMEM((groups, 7, 8, LANES), f32),
-            pltpu.VMEM((6, ntarget, LANES), f32),
-            pltpu.VMEM((6, ntarget, LANES), f32),
+            pltpu.VMEM((2, ntarget), f32),
+            pltpu.VMEM((6, ntarget // 4, LANES), f32),
+            pltpu.VMEM((6, ntarget // 4, LANES), f32),
         ],
         compiler_params=PARAMS,
-        name="forces",
-    )(gathered, *kept)
+        name="taken",
+    )(handed, sources, own)
     order = pair_order(rows, columns)
     lists = [[(2 * h + core) * columns + c for h, c in order] for core in range(2)]
     same_core = lax.all_to_all(packed, ("ia", "ja"), 0, 0, axis_index_groups=lists)
@@ -322,6 +405,7 @@
             pltpu.VMEM((12, ntarget), f32),
             pltpu.VMEM((12, nlocal), f32),
             pltpu.VMEM((rows, 8, ntarget), f32),
+            pltpu.VMEM((rows, 8, ntarget), f32),
             pltpu.SemaphoreType.DMA((1 + PIECES,)),
         ],
         compiler_params=PARAMS,

time: 32.5 us -> 33.3 us (1.025)
  starting transfers between devices: 0.01 us -> 1.4 us
  Pallas kernels: 9.43 us -> 8.1 us
  blocking collectives: 21 us -> 21.7 us
    pallas_call x1 -> x2, Pallas kernels: 6.4 us -> 5.07 us  [the longest x1 5.02 us: local(): pl.pallas_call(force_kernel, out_shape=(pltpu.VMEM((8, ntarget), f32), pl...]
    ppermute x0 -> x1, starting transfers between devices: none -> 1.28 us  [local(): lax.ppermute(gathered, 'ia', [(r, r + 1) for r in range(0, rows, 2)])]
    all_to_all x1, blocking collectives: 9.82 us -> 10.5 us  [local(): lax.all_to_all(packed, ('ia', 'ja'), 0, 0, axis_index_groups=lists)]
  transfers between devices with their start and end apart: 1 -> 2, of which waited for: 1 -> 1; matrix products, arithmetic and copies ran while one was open for 0% -> 0% of each run, Pallas kernels for 0% -> 15%
where the time goes in v11:
time: 33.3 us; the launch traced here: 33 us
  blocking collectives  21.7 us (65%)
  Pallas kernels  8.1 us (24%)
  starting transfers between devices  1.4 us (4%)
  waiting for transfers between devices  1.15 us (3%)
  between operations  0.66 us (2%)
    all_to_all x1, blocking collectives, local(): lax.all_to_all(mine, 'ja', 0, 0, axis_index_groups=[column_order(columns)])  11.2 us
    all_to_all x1, blocking collectives, local(): lax.all_to_all(packed, ('ia', 'ja'), 0, 0, axis_index_groups=lists)  10.5 us
    pallas_call x1, Pallas kernels, local(): pl.pallas_call(force_kernel, out_shape=(pltpu.VMEM((8, ntarget), f32), pl...  5.02 us
    pallas_call x1, Pallas kernels, local(): pl.pallas_call(functools.partial(finish_kernel, rows, columns), out_shape...  1.54 us
    pallas_call x1, Pallas kernels, local(): pl.pallas_call(gather_kernel, out_shape=(pltpu.VMEM((columns, 16, ntarget...  1.49 us
    ppermute x1, starting transfers between devices, local(): lax.ppermute(gathered, 'ia', [(r, r + 1) for r in range(0, rows, 2)])  1.28 us
    ppermute x1, waiting for transfers between devices, local(): lax.ppermute(same_core, 'ia', [(r, r ^ 1) for r in range(rows)])  1.15 us
  transfers between devices with their start and end apart: 2, of which 1 were waited for; matrix products, arithmetic and copies ran while one was open for 0% of the time, Pallas kernels for 15%

profile of v11, /device:TPU:0, one launch (start us, length us, event | category | flops | bytes accessed | tf_op | source)
XLA Modules:
  0.0 33.0 jit_solution(1227092867334766192)
XLA Ops:
  0.6 1.5 %gather.1 = (f32[8,16,128]{2,1,0:T(8,128)S(1)}, f32[3,8192]{1,0:T(4,128)S(1)}, f32[3,8192]{1,0:T(4,128)S(1)}, f32[3,8192]{1,0:T(4,128)S(1)}, f32[3,8192]{1,0:T(4...) custom-call(f32[3,8192]{1,0:T(4,128)} %refs_0_.1, f32[3,8192]{1,0:T(4,128)} %refs_1_.1, ...), custom_call_target="tpu_custom_call" | custom-call | tf_op jit(solution)/shard_map/gather/pallas_call | solution.py:347
  2.1 11.2 %all_to_all.10.gathered = f32[8,16,128]{2,1,0:T(8,128)S(1)} all-to-all(f32[8,16,128]{2,1,0:T(8,128)S(1)} %get-tuple-element.13), channel_id=1, replica_groups={{5,7,6,4,3,2,1,0},{13,15,14,12,11,10,9,8},{21,23,22,20,19,18,17,16},{29..., dimensions={0} | all-to-all | bytes 131072 | tf_op jit(solution)/shard_map/all_to_all | solution.py:359
  13.3 1.3 %collective-permute-start = (f32[8,16,128]{2,1,0:T(8,128)S(1)}, f32[8,16,128]{2,1,0:T(8,128)S(1)}, u32[]{:S(2)}, u32[]{:S(2)}) collective-permute-start(f32[8,16,128]{2,1,0:T(8,128)S(1)} %all_to_all.10.gathered), channel_id=1, source_target_pairs={{0,8},{16,24},{1,9},{17,25},{2,10},{18,26},{3,11},{19,27},{4,12},{... | collective-permute-start | bytes 196616 | tf_op jit(solution)/shard_map/ppermute | solution.py:360
  14.6 5.0 %forces.1 = (f32[8,128]{1,0:T(8,128)S(1)}, f32[16,128]{1,0:T(8,128)S(1)}, f32[64,7,8,128]{3,2,1,0:T(8,128)S(1)}) custom-call(f32[8,16,128]{2,1,0:T(8,128)S(1)} %all_to_all.10.gathered, f32[3,8192]{1,0:T(4,128)S(1)} %get-tuple-element.14.pos, f32[3,8192]{1,0:T(4,128)S(1)} %get-tuple-element.15.vel, f32[3,8192]{1,0:T(4,128)S(1)} %get-tuple-element.16.acc, ...), custom_call_target="tpu_custom_call" | custom-call | flops 41943040 | bytes 2621440 | tf_op jit(solution)/shard_map/forces/pallas_call | solution.py:361
  19.6 0.0 collective-permute-done.handed
  19.7 10.5 %all_to_all.11.same_core = f32[16,1,1152]{2,1,0:T(1,128)S(1)} all-to-all(f32[16,1,1152]{2,1,0:T(1,128)S(1)} %taken.1), channel_id=1, replica_groups={{23,0,1,2,3,4,5,6,7,16,17,18,19,20,21,22},{31,8,9,10,11,12,13,14,15,24,..., dimensions={0} | all-to-all | bytes 147456 | tf_op jit(solution)/shard_map/all_to_all | solution.py:394
  30.2 0.1 collective-permute-start.1
  30.3 1.2 %collective-permute-done.1.other_core = f32[16,1,1152]{2,1,0:T(1,128)S(1)} collective-permute-done((f32[16,1,1152]{2,1,0:T(1,128)S(1)}, f32[16,1,1152]{2,1,0:T(1,128)S(1)}, u32[]{:S(2)}, u32[]{:S(2)}) %collective-permute-start.1) | collective-permute-done | bytes 73760 | tf_op jit(solution)/shard_map/ppermute | solution.py:395
  31.5 1.5 %finish.1 = (f32[12,128]{1,0:T(8,128)}, f32[12,8192]{1,0:T(8,128)}) custom-call(f32[16,1,1152]{2,1,0:T(1,128)S(1)} %all_to_all.11.same_core, f32[16,1,1152]{2,1,0:T(1,128)S(1)} %collective-permute-done.1.other_core, f32[16,128]{1,0:T(8,128)S(1)} %get-tuple-element.23.old, f32[3,8192]{1,0:T(4,128)S(1)} %get-tuple-element.14.pos, ...), custom_call_target="tpu_custom_call" | custom-call | tf_op jit(solution)/shard_map/finish/pallas_call | solution.py:396
  (1 shorter events, 0.0 us)
Async XLA Ops:
  13.3 6.3 %collective-permute-start = (f32[8,16,128]{2,1,0:T(8,128)S(1)}, f32[8,16,128]{2,1,0:T(8,128)S(1)}, u32[]{:S(2)}, u32[]{:S(2)}) collective-permute-start(f32[8,16,128]{2,1,0:T(8,128)S(1)} %all_to_all.10.gathered), channel_id=1, source_target_pairs={{0,8},{16,24},{1,9},{17,25},{2,10},{18,26},{3,11},{19,27},{4,12},{... | collective-permute-start | bytes 196616 | tf_op jit(solution)/shard_map/ppermute | solution.py:360
  30.2 1.3 %collective-permute-start.1 = (f32[16,1,1152]{2,1,0:T(1,128)S(1)}, f32[16,1,1152]{2,1,0:T(1,128)S(1)}, u32[]{:S(2)}, u32[]{:S(2)}) collective-permute-start(f32[16,1,1152]{2,1,0:T(1,128)S(1)} %all_to_all.11.same_core), channel_id=1, source_target_pairs={{0,8},{8,0},{16,24},{24,16},{1,9},{9,1},{17,25},{25,17},{2,10},{10... | collective-permute-start | bytes 221192 | tf_op jit(solution)/shard_map/ppermute | solution.py:395

commit v12 on v10

--- a/solution.py
+++ b/solution.py
@@ -182,50 +182,28 @@
             packed[k, :, tile(c)] = table[c : c + 1]
 
 
-def finish_kernel(
-    rows, columns, same_core, other_core, old, pos, vel, acc, jrk, levels, targets_out, stars_out,
-    targets_new, stars_new, rowed, sems
-):
-    groups = levels.shape[0]
-    ntarget = old.shape[1]
-    me = lax.axis_index("ia")
+def laid_out(rows, columns, everyone, rowed, groups, before):
+    ntarget = rowed.shape[2]
     base = lax.axis_index("ja") * (groups * LANES)
-
-    forces, where_hi, where_lo = ([], [], [])
-    mine = jnp.zeros((8, ntarget), f32)
     order = pair_order(rows, columns)
-    for r in range(rows):
-        everyone = same_core if r < rows // 2 else other_core
-        first, *others = [k for k, (h, _) in enumerate(order) if h == r % (rows // 2)]
+    group = lax.broadcasted_iota(jnp.int32, (groups, ntarget), 0)
+    lane = lax.broadcasted_iota(jnp.int32, (LANES, ntarget), 0)
+    number = lax.broadcasted_iota(jnp.int32, (groups, ntarget), 1).astype(f32) + 1.0
+    spot = jnp.zeros((groups, LANES), f32)
+    part = jnp.full((groups, LANES), -1.0, f32)
+    forces = []
+    for r in range(rows // 2):
+        first, *others = [k for k, (h, _) in enumerate(order) if h == r]
         total = everyone[first]
         for k in others:
             total = total + everyone[k]
         for c in range(6):
             rowed[r, c : c + 1, :] = total[:, tile(c)]
+        rowed[r, 6:8, :] = jnp.ones((2, ntarget), f32)
         forces.append(rowed[r])
-        mine = jnp.where((me >> 1) == r, forces[r], mine)
         offset = everyone[first][:, tile(6)].astype(jnp.int32) - base
-        where_hi.append(offset >> 7)
-        where_lo.append(offset & (LANES - 1))
-
-    o = old[...]
-    factors = correction_factors(o[12:13])
-    x1, v1 = correct(o[0:3], o[3:6], o[6:9], o[9:12], factors, mine[0:3], mine[3:6])
-    targets_new[0:3, :] = x1
-    targets_new[3:6, :] = v1
-    targets_new[6:12, :] = mine[0:6]
-    copies = [pltpu.make_async_copy(targets_new, targets_out, sems.at[0])]
-    copies[0].start()
-    piece = groups // PIECES
-
-    group = lax.broadcasted_iota(jnp.int32, (groups, ntarget), 0)
-    lane = lax.broadcasted_iota(jnp.int32, (LANES, ntarget), 0)
-    number = lax.broadcasted_iota(jnp.int32, (groups, ntarget), 1).astype(f32) + 1.0
-    spot = jnp.zeros((groups, LANES), f32)
-    part = jnp.zeros((groups, LANES), f32)
-    for r in range(rows):
-        hit = group == where_hi[r]
-        side = (lane == where_lo[r]).astype(jnp.bfloat16)
+        hit = group == offset >> 7
+        side = (lane == (offset & (LANES - 1))).astype(jnp.bfloat16)
         found = lax.dot_general(
             jnp.where(hit, number, 0.0).astype(jnp.bfloat16),
             side,
@@ -234,17 +212,43 @@
         )
         part = jnp.where(found > 0.5, float(r), part)
         spot = spot + found
-    present = spot > 0.5
-    slot = jnp.where(present, spot - 1.0, 0.0).astype(jnp.int32)
-    part = jnp.where(present, part, -1.0)
-    factors = correction_factors(elapsed_of(levels[...]))
+    slot = jnp.maximum(spot - 1.0, 0.0).astype(jnp.int32)
     for t in range(groups):
         lanes = jnp.broadcast_to(slot[t : t + 1], (8, LANES))
         holder = jnp.broadcast_to(part[t : t + 1], (8, LANES))
-        new = jnp.zeros((8, LANES), f32)
-        for r in range(rows):
+        new = before(t)
+        for r in range(rows // 2):
             new = jnp.where(holder == float(r), jnp.take_along_axis(forces[r], lanes, axis=1), new)
-        there = holder[0:3] > -0.5
+        yield new
+
+
+def same_kernel(rows, columns, same_core, old, targets_new, placed, rowed):
+    zero = jnp.zeros((8, LANES), f32)
+    tiles = laid_out(rows, columns, same_core, rowed, placed.shape[0], lambda t: zero)
+    for t, new in enumerate(tiles):
+        placed[t] = new
+    me = lax.axis_index("ia") >> 1
+    mine = rowed[0]
+    for r in range(1, rows // 2):
+        mine = jnp.where(me == r, rowed[r], mine)
+    o = old[...]
+    factors = correction_factors(o[12:13])
+    x1, v1 = correct(o[0:3], o[3:6], o[6:9], o[9:12], factors, mine[0:3], mine[3:6])
+    targets_new[0:3, :] = x1
+    targets_new[3:6, :] = v1
+    targets_new[6:12, :] = mine[0:6]
+
+
+def finish_kernel(
+    rows, columns, other_core, placed, pos, vel, acc, jrk, levels, stars_out, stars_new, rowed, sems
+):
+    groups = levels.shape[0]
+    piece = groups // PIECES
+    copies = []
+    factors = correction_factors(elapsed_of(levels[...]))
+    tiles = laid_out(rows, columns, other_core, rowed, groups, lambda t: placed[t])
+    for t, new in enumerate(tiles):
+        there = jnp.broadcast_to(new[7:8], (3, LANES)) > 0.5
         x0, v0, a0, j0 = (pos[:, tile(t)], vel[:, tile(t)], acc[:, tile(t)], jrk[:, tile(t)])
         a1, j1 = (new[0:3], new[3:6])
         x1, v1 = correct(x0, v0, a0, j0, [f[t : t + 1] for f in factors], a1, j1)
@@ -310,23 +314,35 @@
     lists = [[(2 * h + core) * columns + c for h, c in order] for core in range(2)]
     same_core = lax.all_to_all(packed, ("ia", "ja"), 0, 0, axis_index_groups=lists)
     other_core = lax.ppermute(same_core, "ia", [(r, r ^ 1) for r in range(rows)])
-    return pl.pallas_call(
-        functools.partial(finish_kernel, rows, columns),
+    targets_new, placed = pl.pallas_call(
+        functools.partial(same_kernel, rows, columns),
         out_shape=(
             jax.ShapeDtypeStruct((12, ntarget), f32),
-            jax.ShapeDtypeStruct((12, nlocal), f32),
-        ),
-        in_specs=[VMEM] * 8,
-        out_specs=(HBM, HBM),
+            pltpu.VMEM((groups, 8, LANES), f32),
+        ),
+        in_specs=[VMEM] * 2,
+        out_specs=(VMEM, VMEM),
+        scratch_shapes=[pltpu.VMEM((rows // 2, 8, ntarget), f32)],
+        compiler_params=PARAMS,
+        cost_estimate=pl.CostEstimate(
+            flops=200 * nlocal, bytes_accessed=4 * 64 * nlocal, transcendentals=0
+        ),
+        name="same",
+    )(same_core, old)
+    stars_new = pl.pallas_call(
+        functools.partial(finish_kernel, rows, columns),
+        out_shape=jax.ShapeDtypeStruct((12, nlocal), f32),
+        in_specs=[VMEM] * 7,
+        out_specs=HBM,
         scratch_shapes=[
-            pltpu.VMEM((12, ntarget), f32),
             pltpu.VMEM((12, nlocal), f32),
-            pltpu.VMEM((rows, 8, ntarget), f32),
-            pltpu.SemaphoreType.DMA((1 + PIECES,)),
+            pltpu.VMEM((rows // 2, 8, ntarget), f32),
+            pltpu.SemaphoreType.DMA((PIECES,)),
         ],
         compiler_params=PARAMS,
         name="finish",
-    )(same_core, other_core, old, *kept[:5])
+    )(other_core, placed, *kept[:5])
+    return (targets_new, stars_new)
 
 
 def solution(mesh):

time: 32.5 us -> 32.4 us (level)
  waiting for transfers between devices: 1.24 us -> 0.15 us
  Pallas kernels: 9.43 us -> 10.3 us
    ppermute x1, waiting for transfers between devices: 1.24 us -> 0.15 us  [local(): lax.ppermute(same_core, 'ia', [(r, r ^ 1) for r in range(rows)])]
    pallas_call x0 -> x1, Pallas kernels: none -> 1.09 us  [local(): pl.pallas_call(functools.partial(same_kernel, rows, columns), out_shape=(...]
  transfers between devices with their start and end apart: 1 -> 1, of which waited for: 1 -> 1; matrix products, arithmetic and copies ran while one was open for 0% -> 0% of each run, Pallas kernels for 0% -> 3%
where the time goes in v12:
time: 32.4 us; the launch traced here: 32.1 us
  blocking collectives  21 us (65%)
  Pallas kernels  10.3 us (32%)
  between operations  0.65 us (2%)
    all_to_all x1, blocking collectives, local(): lax.all_to_all(mine, 'ja', 0, 0, axis_index_groups=[column_order(columns)])  11.2 us
    all_to_all x1, blocking collectives, local(): lax.all_to_all(packed, ('ia', 'ja'), 0, 0, axis_index_groups=lists)  9.82 us
    pallas_call x1, Pallas kernels, local(): pl.pallas_call(force_kernel, out_shape=(pltpu.VMEM((rows // 2 * columns,...  6.4 us
    pallas_call x1, Pallas kernels, local(): pl.pallas_call(gather_kernel, out_shape=(pltpu.VMEM((columns, 16, ntarget...  1.49 us
    pallas_call x1, Pallas kernels, local(): pl.pallas_call(functools.partial(finish_kernel, rows, columns), out_shape...  1.36 us
    pallas_call x1, Pallas kernels, local(): pl.pallas_call(functools.partial(same_kernel, rows, columns), out_shape=(...  1.09 us
  transfers between devices with their start and end apart: 1, of which 1 were waited for; matrix products, arithmetic and copies ran while one was open for 0% of the time, Pallas kernels for 3%

profile of v12, /device:TPU:0, one launch (start us, length us, event | category | flops | bytes accessed | tf_op | source)
XLA Modules:
  0.0 32.1 jit_solution(14053862279633256934)
XLA Ops:
  0.6 1.5 %gather.1 = (f32[8,16,128]{2,1,0:T(8,128)S(1)}, f32[3,8192]{1,0:T(4,128)S(1)}, f32[3,8192]{1,0:T(4,128)S(1)}, f32[3,8192]{1,0:T(4,128)S(1)}, f32[3,8192]{1,0:T(4...) custom-call(f32[3,8192]{1,0:T(4,128)} %refs_0_.1, f32[3,8192]{1,0:T(4,128)} %refs_1_.1, ...), custom_call_target="tpu_custom_call" | custom-call | tf_op jit(solution)/shard_map/gather/pallas_call | solution.py:284
  2.1 11.2 %all_to_all.10.gathered = f32[8,16,128]{2,1,0:T(8,128)S(1)} all-to-all(f32[8,16,128]{2,1,0:T(8,128)S(1)} %get-tuple-element.14), channel_id=1, replica_groups={{5,7,6,4,3,2,1,0},{13,15,14,12,11,10,9,8},{21,23,22,20,19,18,17,16},{29..., dimensions={0} | all-to-all | bytes 131072 | tf_op jit(solution)/shard_map/all_to_all | solution.py:296
  13.3 6.4 %forces.1 = (f32[16,1,896]{2,1,0:T(1,128)S(1)}, f32[16,128]{1,0:T(8,128)S(1)}) custom-call(f32[8,16,128]{2,1,0:T(8,128)S(1)} %all_to_all.10.gathered, f32[3,8192]{1,0:T(4,128)S(1)} %get-tuple-element.15.pos, f32[3,8192]{1,0:T(4,128)S(1)} %get-tuple-element.16.vel, f32[3,8192]{1,0:T(4,128)S(1)} %get-tuple-element.17.acc, ...), custom_call_target="tpu_custom_call" | custom-call | tf_op jit(solution)/shard_map/forces/pallas_call | solution.py:297
  19.7 9.8 %all_to_all.11.same_core = f32[16,1,896]{2,1,0:T(1,128)S(1)} all-to-all(f32[16,1,896]{2,1,0:T(1,128)S(1)} %get-tuple-element.22), channel_id=1, replica_groups={{23,0,1,2,3,4,5,6,7,16,17,18,19,20,21,22},{31,8,9,10,11,12,13,14,15,24,..., dimensions={0} | all-to-all | bytes 114688 | tf_op jit(solution)/shard_map/all_to_all | solution.py:315
  29.5 0.0 collective-permute-start
  29.5 1.1 %same.1 = (f32[12,128]{1,0:T(8,128)}, f32[64,8,128]{2,1,0:T(8,128)S(1)}) custom-call(f32[16,1,896]{2,1,0:T(1,128)S(1)} %all_to_all.11.same_core, f32[16,128]{1,0:T(8,128)S(1)} %get-tuple-element.23.old), custom_call_target="tpu_custom_call" | custom-call | flops 1638400 | bytes 2097152 | tf_op jit(solution)/shard_map/same/pallas_call | solution.py:317
  30.6 0.1 collective-permute-done.other_core
  30.8 1.4 %finish.1 = f32[12,8192]{1,0:T(8,128)} custom-call(f32[16,1,896]{2,1,0:T(1,128)S(1)} %collective-permute-done.other_core, f32[64,8,128]{2,1,0:T(8,128)S(1)} %get-tuple-element.25.placed, f32[3,8192]{1,0:T(4,128)S(1)} %get-tuple-element.15.pos, f32[3,8192]{1,0:T(4,128)S(1)} %get-tuple-element.16.vel, f32[3,8192]{1,0:T(4,128)S(1)} %get-tuple-element.17.acc, ...), custom_call_target="tpu_custom_call" | custom-call | tf_op jit(solution)/shard_map/finish/pallas_call | solution.py:332
Async XLA Ops:
  29.5 1.2 %collective-permute-start = (f32[16,1,896]{2,1,0:T(1,128)S(1)}, f32[16,1,896]{2,1,0:T(1,128)S(1)}, u32[]{:S(2)}, u32[]{:S(2)}) collective-permute-start(f32[16,1,896]{2,1,0:T(1,128)S(1)} %all_to_all.11.same_core), channel_id=1, source_target_pairs={{0,8},{8,0},{16,24},{24,16},{1,9},{9,1},{17,25},{25,17},{2,10},{10... | collective-permute-start | bytes 172040 | tf_op jit(solution)/shard_map/ppermute | solution.py:316

commit v13 on v12

--- a/solution.py
+++ b/solution.py
@@ -47,12 +47,11 @@
 
 def column_order(columns):
     first = max(columns - 3, 0)
-    return [first, *(c for c in range(columns - 1, -1, -1) if c != first)]
+    return [*range(first, columns), *range(first)]
 
 
 def pair_order(rows, columns):
-    natural = [(h, c) for h in range(rows // 2) for c in range(columns)]
-    return natural[-1:] + natural[:-1]
+    return [(h, c) for h in range(rows // 2 - 1, -1, -1) for c in range(columns - 1, -1, -1)]
 
 
 def tile(t):

time: 32.4 us -> 32.2 us (level)
  no operation moved by 1% of the time
where the time goes in v13:
time: 32.2 us; the launch traced here: 32 us
  blocking collectives  20.8 us (65%)
  Pallas kernels  10.3 us (32%)
  between operations  0.65 us (2%)
    all_to_all x1, blocking collectives, local(): lax.all_to_all(mine, 'ja', 0, 0, axis_index_groups=[column_order(columns)])  11.3 us
    all_to_all x1, blocking collectives, local(): lax.all_to_all(packed, ('ia', 'ja'), 0, 0, axis_index_groups=lists)  9.57 us
    pallas_call x1, Pallas kernels, local(): pl.pallas_call(force_kernel, out_shape=(pltpu.VMEM((rows // 2 * columns,...  6.4 us
    pallas_call x1, Pallas kernels, local(): pl.pallas_call(gather_kernel, out_shape=(pltpu.VMEM((columns, 16, ntarget...  1.49 us
    pallas_call x1, Pallas kernels, local(): pl.pallas_call(functools.partial(finish_kernel, rows, columns), out_shape...  1.36 us
    pallas_call x1, Pallas kernels, local(): pl.pallas_call(functools.partial(same_kernel, rows, columns), out_shape=(...  1.09 us
  transfers between devices with their start and end apart: 1, of which 1 were waited for; matrix products, arithmetic and copies ran while one was open for 0% of the time, Pallas kernels for 3%

profile of v13, /device:TPU:0, one launch (start us, length us, event | category | flops | bytes accessed | tf_op | source)
XLA Modules:
  0.0 32.0 jit_solution(15331903512600262688)
XLA Ops:
  0.6 1.5 %gather.1 = (f32[8,16,128]{2,1,0:T(8,128)S(1)}, f32[3,8192]{1,0:T(4,128)S(1)}, f32[3,8192]{1,0:T(4,128)S(1)}, f32[3,8192]{1,0:T(4,128)S(1)}, f32[3,8192]{1,0:T(4...) custom-call(f32[3,8192]{1,0:T(4,128)} %refs_0_.1, f32[3,8192]{1,0:T(4,128)} %refs_1_.1, ...), custom_call_target="tpu_custom_call" | custom-call | tf_op jit(solution)/shard_map/gather/pallas_call | solution.py:283
  2.1 11.3 %all_to_all.10.gathered = f32[8,16,128]{2,1,0:T(8,128)S(1)} all-to-all(f32[8,16,128]{2,1,0:T(8,128)S(1)} %get-tuple-element.14), channel_id=1, replica_groups={{5,6,7,0,1,2,3,4},{13,14,15,8,9,10,11,12},{21,22,23,16,17,18,19,20},{29..., dimensions={0} | all-to-all | bytes 131072 | tf_op jit(solution)/shard_map/all_to_all | solution.py:295
  13.4 6.4 %forces.1 = (f32[16,1,896]{2,1,0:T(1,128)S(1)}, f32[16,128]{1,0:T(8,128)S(1)}) custom-call(f32[8,16,128]{2,1,0:T(8,128)S(1)} %all_to_all.10.gathered, f32[3,8192]{1,0:T(4,128)S(1)} %get-tuple-element.15.pos, f32[3,8192]{1,0:T(4,128)S(1)} %get-tuple-element.16.vel, f32[3,8192]{1,0:T(4,128)S(1)} %get-tuple-element.17.acc, ...), custom_call_target="tpu_custom_call" | custom-call | tf_op jit(solution)/shard_map/forces/pallas_call | solution.py:296
  19.8 9.6 %all_to_all.11.same_core = f32[16,1,896]{2,1,0:T(1,128)S(1)} all-to-all(f32[16,1,896]{2,1,0:T(1,128)S(1)} %get-tuple-element.22), channel_id=1, replica_groups={{23,22,21,20,19,18,17,16,7,6,5,4,3,2,1,0},{31,30,29,28,27,26,25,24,15,1..., dimensions={0} | all-to-all | bytes 114688 | tf_op jit(solution)/shard_map/all_to_all | solution.py:314
  29.4 0.0 collective-permute-start
  29.4 1.1 %same.1 = (f32[12,128]{1,0:T(8,128)}, f32[64,8,128]{2,1,0:T(8,128)S(1)}) custom-call(f32[16,1,896]{2,1,0:T(1,128)S(1)} %all_to_all.11.same_core, f32[16,128]{1,0:T(8,128)S(1)} %get-tuple-element.23.old), custom_call_target="tpu_custom_call" | custom-call | flops 1638400 | bytes 2097152 | tf_op jit(solution)/shard_map/same/pallas_call | solution.py:316
  30.4 0.1 collective-permute-done.other_core
  30.6 1.4 %finish.1 = f32[12,8192]{1,0:T(8,128)} custom-call(f32[16,1,896]{2,1,0:T(1,128)S(1)} %collective-permute-done.other_core, f32[64,8,128]{2,1,0:T(8,128)S(1)} %get-tuple-element.25.placed, f32[3,8192]{1,0:T(4,128)S(1)} %get-tuple-element.15.pos, f32[3,8192]{1,0:T(4,128)S(1)} %get-tuple-element.16.vel, f32[3,8192]{1,0:T(4,128)S(1)} %get-tuple-element.17.acc, ...), custom_call_target="tpu_custom_call" | custom-call | tf_op jit(solution)/shard_map/finish/pallas_call | solution.py:331
Async XLA Ops:
  29.4 1.2 %collective-permute-start = (f32[16,1,896]{2,1,0:T(1,128)S(1)}, f32[16,1,896]{2,1,0:T(1,128)S(1)}, u32[]{:S(2)}, u32[]{:S(2)}) collective-permute-start(f32[16,1,896]{2,1,0:T(1,128)S(1)} %all_to_all.11.same_core), channel_id=1, source_target_pairs={{0,8},{8,0},{16,24},{24,16},{1,9},{9,1},{17,25},{25,17},{2,10},{10... | collective-permute-start | bytes 172040 | tf_op jit(solution)/shard_map/ppermute | solution.py:315

commit v14 on v13

--- a/solution.py
+++ b/solution.py
@@ -60,23 +60,18 @@
 
 def gather_kernel(*refs):
     given, out, kept, sems = (refs[:7], refs[7], refs[8:15], refs[15])
-    pos, vel, acc, jrk, levels, masses, active = kept
+    levels, masses, active = kept[4:]
     groups = levels.shape[0]
-    half = groups // 2
-
-    def copy_of(n, sem, columns=None):
-        if columns is None:
-            return pltpu.make_async_copy(given[n], kept[n], sems.at[sem])
-        part = (slice(None), columns)
-        return pltpu.make_async_copy(given[n].at[part], kept[n].at[part], sems.at[sem])
-
-    small = [copy_of(6, 0), copy_of(4, 1)]
-    parts = [
-        [copy_of(n, 2 + 4 * h + n, slice(h * half * LANES, (h + 1) * half * LANES)) for n in range(4)]
-        for h in range(2)
+    small = [pltpu.make_async_copy(given[n], kept[n], sems.at[n]) for n in (6, 4)]
+    planes = [
+        [
+            pltpu.make_async_copy(given[n].at[:, c, :], kept[n].at[c], sems.at[7 + 3 * n + c])
+            for c in range(3)
+        ]
+        for n in range(4)
     ]
-    late = copy_of(5, 10)
-    for copy in (*small, *parts[0], *parts[1], late):
+    late = pltpu.make_async_copy(given[5], kept[5], sems.at[5])
+    for copy in (*small, *sum(planes, []), late):
         copy.start()
     for copy in small:
         copy.wait()
@@ -84,26 +79,24 @@
     group = jnp.broadcast_to(offset >> 7, (8, LANES))
     lane = jnp.broadcast_to(offset & (LANES - 1), (8, LANES))
     row = lax.broadcasted_iota(jnp.int32, (8, LANES), 0)
-    elapsed = elapsed_of(levels[...])
-    steps = jnp.zeros((8, LANES), f32)
-    for t in range(0, groups, 8):
-        here = group == row + t
-        steps = jnp.where(here, jnp.take_along_axis(elapsed[t : t + 8], lane, axis=1), steps)
-    found = [jnp.zeros((3, LANES), f32)] * 4
-    for h in range(2):
-        for copy in parts[h]:
-            copy.wait()
-        for t in range(h * half, (h + 1) * half):
-            here = group[0:3] == t
-            found = [
-                jnp.where(here, jnp.take_along_axis(x[:, tile(t)], lane[0:3], axis=1), old)
-                for x, old in zip((pos, vel, acc, jrk), found)
-            ]
-    steps = jnp.broadcast_to(jnp.sum(steps, axis=0, keepdims=True), (4, LANES))
+    here = [group == row + t for t in range(0, groups, 8)]
+
+    def picked(plane):
+        value = jnp.zeros((8, LANES), f32)
+        for n, mask in enumerate(here):
+            part = jnp.take_along_axis(plane[8 * n : 8 * n + 8], lane, axis=1)
+            value = jnp.where(mask, part, value)
+        return jnp.sum(value, axis=0, keepdims=True)
+
+    found = [picked(elapsed_of(levels[...]))]
+    for n in range(4):
+        for c in range(3):
+            planes[n][c].wait()
+            found.insert(3 * n + c, picked(kept[n].at[c]))
     for k in range(out.shape[0]):
         for n, value in enumerate(found):
-            out[k, 3 * n : 3 * n + 3, :] = value
-        out[k, 12:16, :] = steps
+            out[k, n : n + 1, :] = value
+        out[k, 13:16, :] = jnp.zeros((3, LANES), f32)
     late.wait()
 
 
@@ -125,13 +118,12 @@
     for c in range(6):
         targets[c] = jnp.broadcast_to(columns[:, c : c + 1], (ntarget, LANES))
     factors = step_factors(elapsed_of(levels[...]))
+    for c in range(3):
+        spos, svel = predict(pos[c], vel[c], acc[c], jrk[c], factors)
+        for t in range(groups):
+            sources[t, c] = jnp.broadcast_to(spos[t : t + 1], (8, LANES))
+            sources[t, 3 + c] = jnp.broadcast_to(svel[t : t + 1], (8, LANES))
     for t in range(groups):
-        spos, svel = predict(
-            *(x[:, tile(t)] for x in (pos, vel, acc, jrk)), [f[t : t + 1] for f in factors]
-        )
-        for c in range(3):
-            sources[t, c] = jnp.broadcast_to(spos[c : c + 1], (8, LANES))
-            sources[t, 3 + c] = jnp.broadcast_to(svel[c : c + 1], (8, LANES))
         sources[t, 6] = jnp.broadcast_to(masses[t : t + 1, :], (8, LANES))
 
     def one_group(g, unused):
@@ -221,7 +213,11 @@
         yield new
 
 
-def same_kernel(rows, columns, same_core, old, targets_new, placed, rowed):
+def same_kernel(rows, columns, same_core, old, *refs):
+    given, targets_new, placed, kept, rowed, sems = (refs[:4], *refs[4:6], refs[6:10], *refs[10:])
+    copies = [pltpu.make_async_copy(a, b, sems.at[n]) for n, (a, b) in enumerate(zip(given, kept))]
+    for copy in copies:
+        copy.start()
     zero = jnp.zeros((8, LANES), f32)
     tiles = laid_out(rows, columns, same_core, rowed, placed.shape[0], lambda t: zero)
     for t, new in enumerate(tiles):
@@ -236,6 +232,8 @@
     targets_new[0:3, :] = x1
     targets_new[3:6, :] = v1
     targets_new[6:12, :] = mine[0:6]
+    for copy in copies:
+        copy.wait()
 
 
 def finish_kernel(
@@ -271,11 +269,9 @@
     nlocal = positions.shape[1]
     ntarget = active.shape[0]
     groups = nlocal // LANES
+    state = (positions, velocities, accels, jerks)
     given = (
-        positions,
-        velocities,
-        accels,
-        jerks,
+        *(jnp.swapaxes(x.reshape(3, groups, LANES), 0, 1) for x in state),
         levels.reshape(groups, LANES),
         masses.reshape(groups, LANES),
         active.reshape(1, ntarget),
@@ -284,11 +280,12 @@
         gather_kernel,
         out_shape=(
             pltpu.VMEM((columns, 16, ntarget), f32),
-            *(pltpu.VMEM(x.shape, x.dtype) for x in given),
+            *(pltpu.VMEM((3, groups, LANES), f32) for _ in state),
+            *(pltpu.VMEM(x.shape, x.dtype) for x in given[4:]),
         ),
         in_specs=[HBM] * 7,
         out_specs=(VMEM,) * 8,
-        scratch_shapes=[pltpu.SemaphoreType.DMA((11,))],
+        scratch_shapes=[pltpu.SemaphoreType.DMA((19,))],
         compiler_params=PARAMS,
         name="gather",
     )(*(pltpu.with_memory_space_constraint(x, pltpu.HBM) for x in given))
@@ -313,21 +310,25 @@
     lists = [[(2 * h + core) * columns + c for h, c in order] for core in range(2)]
     same_core = lax.all_to_all(packed, ("ia", "ja"), 0, 0, axis_index_groups=lists)
     other_core = lax.ppermute(same_core, "ia", [(r, r ^ 1) for r in range(rows)])
-    targets_new, placed = pl.pallas_call(
+    targets_new, placed, *tiles = pl.pallas_call(
         functools.partial(same_kernel, rows, columns),
         out_shape=(
             jax.ShapeDtypeStruct((12, ntarget), f32),
             pltpu.VMEM((groups, 8, LANES), f32),
-        ),
-        in_specs=[VMEM] * 2,
-        out_specs=(VMEM, VMEM),
-        scratch_shapes=[pltpu.VMEM((rows // 2, 8, ntarget), f32)],
+            *(pltpu.VMEM(x.shape, f32) for x in state),
+        ),
+        in_specs=[VMEM] * 2 + [HBM] * 4,
+        out_specs=(VMEM,) * 6,
+        scratch_shapes=[
+            pltpu.VMEM((rows // 2, 8, ntarget), f32),
+            pltpu.SemaphoreType.DMA((4,)),
+        ],
         compiler_params=PARAMS,
         cost_estimate=pl.CostEstimate(
             flops=200 * nlocal, bytes_accessed=4 * 64 * nlocal, transcendentals=0
         ),
         name="same",
-    )(same_core, old)
+    )(same_core, old, *(pltpu.with_memory_space_constraint(x, pltpu.HBM) for x in state))
     stars_new = pl.pallas_call(
         functools.partial(finish_kernel, rows, columns),
         out_shape=jax.ShapeDtypeStruct((12, nlocal), f32),
@@ -340,7 +341,7 @@
         ],
         compiler_params=PARAMS,
         name="finish",
-    )(other_core, placed, *kept[:5])
+    )(other_core, placed, *tiles, kept[4])
     return (targets_new, stars_new)
 
 

time: 32.2 us -> 33.3 us (1.034)
  Pallas kernels: 10.3 us -> 11.5 us
    pallas_call x1, Pallas kernels: 1.09 us -> 1.74 us  [local(): pl.pallas_call(functools.partial(same_kernel, rows, columns), out_shape=(...]
    pallas_call x1, Pallas kernels: 1.49 us -> 2.07 us  [local(): pl.pallas_call(gather_kernel, out_shape=(pltpu.VMEM((columns, 16, ntarget...]
  transfers between devices with their start and end apart: 1 -> 1, of which waited for: 1 -> 0; matrix products, arithmetic and copies ran while one was open for 0% -> 0% of each run, Pallas kernels for 3% -> 5%
where the time goes in v14:
time: 33.3 us; the launch traced here: 33 us
  blocking collectives  20.8 us (62%)
  Pallas kernels  11.5 us (35%)
  between operations  0.66 us (2%)
    all_to_all x1, blocking collectives, local(): lax.all_to_all(mine, 'ja', 0, 0, axis_index_groups=[column_order(columns)])  11.3 us
    all_to_all x1, blocking collectives, local(): lax.all_to_all(packed, ('ia', 'ja'), 0, 0, axis_index_groups=lists)  9.57 us
    pallas_call x1, Pallas kernels, local(): pl.pallas_call(force_kernel, out_shape=(pltpu.VMEM((rows // 2 * columns,...  6.35 us
    pallas_call x1, Pallas kernels, local(): pl.pallas_call(gather_kernel, out_shape=(pltpu.VMEM((columns, 16, ntarget...  2.07 us
    pallas_call x1, Pallas kernels, local(): pl.pallas_call(functools.partial(same_kernel, rows, columns), out_shape=(...  1.74 us
    pallas_call x1, Pallas kernels, local(): pl.pallas_call(functools.partial(finish_kernel, rows, columns), out_shape...  1.36 us
  transfers between devices with their start and end apart: 1, of which 0 were waited for; matrix products, arithmetic and copies ran while one was open for 0% of the time, Pallas kernels for 5%

profile of v14, /device:TPU:0, one launch (start us, length us, event | category | flops | bytes accessed | tf_op | source)
XLA Modules:
  0.0 33.0 jit_solution(2318163599027603457)
XLA Ops:
  0.6 2.1 %gather.1 = (f32[8,16,128]{2,1,0:T(8,128)S(1)}, f32[3,64,128]{2,1,0:T(8,128)S(1)}, f32[3,64,128]{2,1,0:T(8,128)S(1)}, f32[3,64,128]{2,1,0:T(8,128)S(1)}, f32[3,6...) custom-call(f32[64,3,128]{2,1,0:T(4,128)} %bitcast.15, ...), custom_call_target="tpu_custom_call" | custom-call | tf_op jit(solution)/shard_map/gather/pallas_call | solution.py:279
  2.7 11.3 %all_to_all.10.gathered = f32[8,16,128]{2,1,0:T(8,128)S(1)} all-to-all(f32[8,16,128]{2,1,0:T(8,128)S(1)} %get-tuple-element.18), channel_id=1, replica_groups={{5,6,7,0,1,2,3,4},{13,14,15,8,9,10,11,12},{21,22,23,16,17,18,19,20},{29..., dimensions={0} | all-to-all | bytes 131072 | tf_op jit(solution)/shard_map/all_to_all | solution.py:292
  14.0 6.3 %forces.1 = (f32[16,1,896]{2,1,0:T(1,128)S(1)}, f32[16,128]{1,0:T(8,128)S(1)}) custom-call(f32[8,16,128]{2,1,0:T(8,128)S(1)} %all_to_all.10.gathered, f32[3,64,128]{2,1,0:T(8,128)S(1)} %get-tuple-element.19.pos, f32[3,64,128]{2,1,0:T(8,128)S(1)} %get-tuple-element.20.vel, f32[3,64,128]{2,1,0:T(8,128)S(1)} %get-tuple-element.21.acc, ...), custom_call_target="tpu_custom_call" | custom-call | tf_op jit(solution)/shard_map/forces/pallas_call | solution.py:293
  20.3 9.6 %all_to_all.11.same_core = f32[16,1,896]{2,1,0:T(1,128)S(1)} all-to-all(f32[16,1,896]{2,1,0:T(1,128)S(1)} %get-tuple-element.26), channel_id=1, replica_groups={{23,22,21,20,19,18,17,16,7,6,5,4,3,2,1,0},{31,30,29,28,27,26,25,24,15,1..., dimensions={0} | all-to-all | bytes 114688 | tf_op jit(solution)/shard_map/all_to_all | solution.py:311
  29.9 0.0 collective-permute-start
  29.9 1.7 %same.1 = (f32[12,128]{1,0:T(8,128)}, f32[64,8,128]{2,1,0:T(8,128)S(1)}, f32[3,8192]{1,0:T(4,128)S(1)}, f32[3,8192]{1,0:T(4,128)S(1)}, f32[3,8192]{1,0:T(4,128)S(1)}, /*index=5*/f32[3,8192]{1,0:T(4,128)S(1)}) custom-call(f32[16,1,896]{2,1,0:T(1,128)S(1)} %all_to_all.11.same_core, f32[16,128]{1,0:T(8,128)S(1)} %get-tuple-element.27.old, f32[3,8192]{1,0:T(4,128)} %refs_0_.1, ...), custom_call_target="tpu_custom_call" | custom-call | flops 1638400 | bytes 2097152 | tf_op jit(solution)/shard_map/same/pallas_call | solution.py:313
  31.6 0.0 collective-permute-done.other_core
  31.6 1.4 %finish.1 = f32[12,8192]{1,0:T(8,128)} custom-call(f32[16,1,896]{2,1,0:T(1,128)S(1)} %collective-permute-done.other_core, f32[64,8,128]{2,1,0:T(8,128)S(1)} %get-tuple-element.29.placed, f32[3,8192]{1,0:T(4,128)S(1)} %get-tuple-element.30.pos, f32[3,8192]{1,0:T(4,128)S(1)} %get-tuple-element.31.vel, f32[3,8192]{1,0:T(4,128)S(1)} %get-tuple-element.32.acc, ...), custom_call_target="tpu_custom_call" | custom-call | tf_op jit(solution)/shard_map/finish/pallas_call | solution.py:332
Async XLA Ops:
  29.9 1.8 %collective-permute-start = (f32[16,1,896]{2,1,0:T(1,128)S(1)}, f32[16,1,896]{2,1,0:T(1,128)S(1)}, u32[]{:S(2)}, u32[]{:S(2)}) collective-permute-start(f32[16,1,896]{2,1,0:T(1,128)S(1)} %all_to_all.11.same_core), channel_id=1, source_target_pairs={{0,8},{8,0},{16,24},{24,16},{1,9},{9,1},{17,25},{25,17},{2,10},{10... | collective-permute-start | bytes 172040 | tf_op jit(solution)/shard_map/ppermute | solution.py:312

commit v15 on v13

--- a/solution.py
+++ b/solution.py
@@ -140,12 +140,12 @@
 
         def one_tile(t, carry):
             dx, dy, dz = (sources[t, 0] - tx, sources[t, 1] - ty, sources[t, 2] - tz)
+            inv = lax.rsqrt(dx * dx + dy * dy + (dz * dz + softening_length))
             du, dv, dw = (sources[t, 3] - tu, sources[t, 4] - tv, sources[t, 5] - tw)
-            r2 = dx * dx + dy * dy + dz * dz + softening_length
-            inv = lax.rsqrt(r2)
+            dot = dx * du + dy * dv + dz * dw
             inv_sq = inv * inv
-            weight = sources[t, 6] * inv * inv_sq
-            radial = (dx * du + dy * dv + dz * dw) * inv_sq
+            weight = (sources[t, 6] * inv) * inv_sq
+            radial = dot * inv_sq
             px, py, pz = (weight * dx, weight * dy, weight * dz)
             ax, ay, az, jx, jy, jz, kx, ky, kz = carry
             return (
@@ -162,7 +162,7 @@
 
         zero = jnp.zeros((8, LANES), f32)
         ax, ay, az, jx, jy, jz, kx, ky, kz = lax.fori_loop(
-            0, groups, one_tile, (zero,) * 9, unroll=32
+            0, groups, one_tile, (zero,) * 9, unroll=16
         )
         for c, value in enumerate((ax, ay, az, jx - 3.0 * kx, jy - 3.0 * ky, jz - 3.0 * kz)):
             sums[c, rows, :] = value

time: 32.2 us -> 32.4 us (level)
  no operation moved by 1% of the time
where the time goes in v15:
time: 32.4 us; the launch traced here: 32.1 us
  blocking collectives  20.8 us (64%)
  Pallas kernels  10.5 us (32%)
  between operations  0.65 us (2%)
    all_to_all x1, blocking collectives, local(): lax.all_to_all(mine, 'ja', 0, 0, axis_index_groups=[column_order(columns)])  11.3 us
    all_to_all x1, blocking collectives, local(): lax.all_to_all(packed, ('ia', 'ja'), 0, 0, axis_index_groups=lists)  9.57 us
    pallas_call x1, Pallas kernels, local(): pl.pallas_call(force_kernel, out_shape=(pltpu.VMEM((rows // 2 * columns,...  6.56 us
    pallas_call x1, Pallas kernels, local(): pl.pallas_call(gather_kernel, out_shape=(pltpu.VMEM((columns, 16, ntarget...  1.49 us
    pallas_call x1, Pallas kernels, local(): pl.pallas_call(functools.partial(finish_kernel, rows, columns), out_shape...  1.36 us
    pallas_call x1, Pallas kernels, local(): pl.pallas_call(functools.partial(same_kernel, rows, columns), out_shape=(...  1.09 us
  transfers between devices with their start and end apart: 1, of which 1 were waited for; matrix products, arithmetic and copies ran while one was open for 0% of the time, Pallas kernels for 3%

profile of v15, /device:TPU:0, one launch (start us, length us, event | category | flops | bytes accessed | tf_op | source)
XLA Modules:
  0.0 32.1 jit_solution(15202630266951700608)
XLA Ops:
  0.6 1.5 %gather.1 = (f32[8,16,128]{2,1,0:T(8,128)S(1)}, f32[3,8192]{1,0:T(4,128)S(1)}, f32[3,8192]{1,0:T(4,128)S(1)}, f32[3,8192]{1,0:T(4,128)S(1)}, f32[3,8192]{1,0:T(4...) custom-call(f32[3,8192]{1,0:T(4,128)} %refs_0_.1, f32[3,8192]{1,0:T(4,128)} %refs_1_.1, ...), custom_call_target="tpu_custom_call" | custom-call | tf_op jit(solution)/shard_map/gather/pallas_call | solution.py:283
  2.1 11.3 %all_to_all.10.gathered = f32[8,16,128]{2,1,0:T(8,128)S(1)} all-to-all(f32[8,16,128]{2,1,0:T(8,128)S(1)} %get-tuple-element.14), channel_id=1, replica_groups={{5,6,7,0,1,2,3,4},{13,14,15,8,9,10,11,12},{21,22,23,16,17,18,19,20},{29..., dimensions={0} | all-to-all | bytes 131072 | tf_op jit(solution)/shard_map/all_to_all | solution.py:295
  13.4 6.6 %forces.1 = (f32[16,1,896]{2,1,0:T(1,128)S(1)}, f32[16,128]{1,0:T(8,128)S(1)}) custom-call(f32[8,16,128]{2,1,0:T(8,128)S(1)} %all_to_all.10.gathered, f32[3,8192]{1,0:T(4,128)S(1)} %get-tuple-element.15.pos, f32[3,8192]{1,0:T(4,128)S(1)} %get-tuple-element.16.vel, f32[3,8192]{1,0:T(4,128)S(1)} %get-tuple-element.17.acc, ...), custom_call_target="tpu_custom_call" | custom-call | tf_op jit(solution)/shard_map/forces/pallas_call | solution.py:296
  19.9 9.6 %all_to_all.11.same_core = f32[16,1,896]{2,1,0:T(1,128)S(1)} all-to-all(f32[16,1,896]{2,1,0:T(1,128)S(1)} %get-tuple-element.22), channel_id=1, replica_groups={{23,22,21,20,19,18,17,16,7,6,5,4,3,2,1,0},{31,30,29,28,27,26,25,24,15,1..., dimensions={0} | all-to-all | bytes 114688 | tf_op jit(solution)/shard_map/all_to_all | solution.py:314
  29.5 0.0 collective-permute-start
  29.5 1.1 %same.1 = (f32[12,128]{1,0:T(8,128)}, f32[64,8,128]{2,1,0:T(8,128)S(1)}) custom-call(f32[16,1,896]{2,1,0:T(1,128)S(1)} %all_to_all.11.same_core, f32[16,128]{1,0:T(8,128)S(1)} %get-tuple-element.23.old), custom_call_target="tpu_custom_call" | custom-call | flops 1638400 | bytes 2097152 | tf_op jit(solution)/shard_map/same/pallas_call | solution.py:316
  30.6 0.1 collective-permute-done.other_core
  30.8 1.4 %finish.1 = f32[12,8192]{1,0:T(8,128)} custom-call(f32[16,1,896]{2,1,0:T(1,128)S(1)} %collective-permute-done.other_core, f32[64,8,128]{2,1,0:T(8,128)S(1)} %get-tuple-element.25.placed, f32[3,8192]{1,0:T(4,128)S(1)} %get-tuple-element.15.pos, f32[3,8192]{1,0:T(4,128)S(1)} %get-tuple-element.16.vel, f32[3,8192]{1,0:T(4,128)S(1)} %get-tuple-element.17.acc, ...), custom_call_target="tpu_custom_call" | custom-call | tf_op jit(solution)/shard_map/finish/pallas_call | solution.py:331
Async XLA Ops:
  29.5 1.2 %collective-permute-start = (f32[16,1,896]{2,1,0:T(1,128)S(1)}, f32[16,1,896]{2,1,0:T(1,128)S(1)}, u32[]{:S(2)}, u32[]{:S(2)}) collective-permute-start(f32[16,1,896]{2,1,0:T(1,128)S(1)} %all_to_all.11.same_core), channel_id=1, source_target_pairs={{0,8},{8,0},{16,24},{24,16},{1,9},{9,1},{17,25},{25,17},{2,10},{10... | collective-permute-start | bytes 172040 | tf_op jit(solution)/shard_map/ppermute | solution.py:315

commit v16 on v13

--- a/solution.py
+++ b/solution.py
@@ -129,22 +129,24 @@
         spos, svel = predict(
             *(x[:, tile(t)] for x in (pos, vel, acc, jrk)), [f[t : t + 1] for f in factors]
         )
-        for c in range(3):
-            sources[t, c] = jnp.broadcast_to(spos[c : c + 1], (8, LANES))
-            sources[t, 3 + c] = jnp.broadcast_to(svel[c : c + 1], (8, LANES))
-        sources[t, 6] = jnp.broadcast_to(masses[t : t + 1, :], (8, LANES))
+        sources[t, 0:3, :] = spos
+        sources[t, 3:6, :] = svel
+        sources[t, 6:7, :] = masses[t : t + 1, :]
 
     def one_group(g, unused):
         rows = pl.ds(pl.multiple_of(g * 8, 8), 8)
         tx, ty, tz, tu, tv, tw = (targets[c, rows, :] for c in range(6))
 
         def one_tile(t, carry):
-            dx, dy, dz = (sources[t, 0] - tx, sources[t, 1] - ty, sources[t, 2] - tz)
-            du, dv, dw = (sources[t, 3] - tu, sources[t, 4] - tv, sources[t, 5] - tw)
+            sx, sy, sz, su, sv, sw, mass = (
+                jnp.broadcast_to(sources[t, c : c + 1, :], (8, LANES)) for c in range(7)
+            )
+            dx, dy, dz = (sx - tx, sy - ty, sz - tz)
+            du, dv, dw = (su - tu, sv - tv, sw - tw)
             r2 = dx * dx + dy * dy + dz * dz + softening_length
             inv = lax.rsqrt(r2)
             inv_sq = inv * inv
-            weight = sources[t, 6] * inv * inv_sq
+            weight = mass * inv * inv_sq
             radial = (dx * du + dy * dv + dz * dw) * inv_sq
             px, py, pz = (weight * dx, weight * dy, weight * dz)
             ax, ay, az, jx, jy, jz, kx, ky, kz = carry
@@ -302,7 +304,7 @@
         in_specs=[VMEM] * 8,
         out_specs=(VMEM, VMEM),
         scratch_shapes=[
-            pltpu.VMEM((groups, 7, 8, LANES), f32),
+            pltpu.VMEM((groups, 8, LANES), f32),
             pltpu.VMEM((6, ntarget, LANES), f32),
             pltpu.VMEM((6, ntarget, LANES), f32),
         ],

time: 32.2 us -> 32.1 us (level)
  no operation moved by 1% of the time
where the time goes in v16:
time: 32.1 us; the launch traced here: 31.9 us
  blocking collectives  20.8 us (65%)
  Pallas kernels  10.3 us (32%)
  between operations  0.65 us (2%)
    all_to_all x1, blocking collectives, local(): lax.all_to_all(mine, 'ja', 0, 0, axis_index_groups=[column_order(columns)])  11.3 us
    all_to_all x1, blocking collectives, local(): lax.all_to_all(packed, ('ia', 'ja'), 0, 0, axis_index_groups=lists)  9.57 us
    pallas_call x1, Pallas kernels, local(): pl.pallas_call(force_kernel, out_shape=(pltpu.VMEM((rows // 2 * columns,...  6.34 us
    pallas_call x1, Pallas kernels, local(): pl.pallas_call(gather_kernel, out_shape=(pltpu.VMEM((columns, 16, ntarget...  1.49 us
    pallas_call x1, Pallas kernels, local(): pl.pallas_call(functools.partial(finish_kernel, rows, columns), out_shape...  1.36 us
    pallas_call x1, Pallas kernels, local(): pl.pallas_call(functools.partial(same_kernel, rows, columns), out_shape=(...  1.09 us
  transfers between devices with their start and end apart: 1, of which 1 were waited for; matrix products, arithmetic and copies ran while one was open for 0% of the time, Pallas kernels for 3%

profile of v16, /device:TPU:0, one launch (start us, length us, event | category | flops | bytes accessed | tf_op | source)
XLA Modules:
  0.0 31.9 jit_solution(13161648221163492292)
XLA Ops:
  0.6 1.5 %gather.1 = (f32[8,16,128]{2,1,0:T(8,128)S(1)}, f32[3,8192]{1,0:T(4,128)S(1)}, f32[3,8192]{1,0:T(4,128)S(1)}, f32[3,8192]{1,0:T(4,128)S(1)}, f32[3,8192]{1,0:T(4...) custom-call(f32[3,8192]{1,0:T(4,128)} %refs_0_.1, f32[3,8192]{1,0:T(4,128)} %refs_1_.1, ...), custom_call_target="tpu_custom_call" | custom-call | tf_op jit(solution)/shard_map/gather/pallas_call | solution.py:285
  2.1 11.3 %all_to_all.10.gathered = f32[8,16,128]{2,1,0:T(8,128)S(1)} all-to-all(f32[8,16,128]{2,1,0:T(8,128)S(1)} %get-tuple-element.14), channel_id=1, replica_groups={{5,6,7,0,1,2,3,4},{13,14,15,8,9,10,11,12},{21,22,23,16,17,18,19,20},{29..., dimensions={0} | all-to-all | bytes 131072 | tf_op jit(solution)/shard_map/all_to_all | solution.py:297
  13.4 6.3 %forces.1 = (f32[16,1,896]{2,1,0:T(1,128)S(1)}, f32[16,128]{1,0:T(8,128)S(1)}) custom-call(f32[8,16,128]{2,1,0:T(8,128)S(1)} %all_to_all.10.gathered, f32[3,8192]{1,0:T(4,128)S(1)} %get-tuple-element.15.pos, f32[3,8192]{1,0:T(4,128)S(1)} %get-tuple-element.16.vel, f32[3,8192]{1,0:T(4,128)S(1)} %get-tuple-element.17.acc, ...), custom_call_target="tpu_custom_call" | custom-call | tf_op jit(solution)/shard_map/forces/pallas_call | solution.py:298
  19.7 9.6 %all_to_all.11.same_core = f32[16,1,896]{2,1,0:T(1,128)S(1)} all-to-all(f32[16,1,896]{2,1,0:T(1,128)S(1)} %get-tuple-element.22), channel_id=1, replica_groups={{23,22,21,20,19,18,17,16,7,6,5,4,3,2,1,0},{31,30,29,28,27,26,25,24,15,1..., dimensions={0} | all-to-all | bytes 114688 | tf_op jit(solution)/shard_map/all_to_all | solution.py:316
  29.3 0.0 collective-permute-start
  29.3 1.1 %same.1 = (f32[12,128]{1,0:T(8,128)}, f32[64,8,128]{2,1,0:T(8,128)S(1)}) custom-call(f32[16,1,896]{2,1,0:T(1,128)S(1)} %all_to_all.11.same_core, f32[16,128]{1,0:T(8,128)S(1)} %get-tuple-element.23.old), custom_call_target="tpu_custom_call" | custom-call | flops 1638400 | bytes 2097152 | tf_op jit(solution)/shard_map/same/pallas_call | solution.py:318
  30.4 0.1 collective-permute-done.other_core
  30.5 1.4 %finish.1 = f32[12,8192]{1,0:T(8,128)} custom-call(f32[16,1,896]{2,1,0:T(1,128)S(1)} %collective-permute-done.other_core, f32[64,8,128]{2,1,0:T(8,128)S(1)} %get-tuple-element.25.placed, f32[3,8192]{1,0:T(4,128)S(1)} %get-tuple-element.15.pos, f32[3,8192]{1,0:T(4,128)S(1)} %get-tuple-element.16.vel, f32[3,8192]{1,0:T(4,128)S(1)} %get-tuple-element.17.acc, ...), custom_call_target="tpu_custom_call" | custom-call | tf_op jit(solution)/shard_map/finish/pallas_call | solution.py:333
Async XLA Ops:
  29.3 1.2 %collective-permute-start = (f32[16,1,896]{2,1,0:T(1,128)S(1)}, f32[16,1,896]{2,1,0:T(1,128)S(1)}, u32[]{:S(2)}, u32[]{:S(2)}) collective-permute-start(f32[16,1,896]{2,1,0:T(1,128)S(1)} %all_to_all.11.same_core), channel_id=1, source_target_pairs={{0,8},{8,0},{16,24},{24,16},{1,9},{9,1},{17,25},{25,17},{2,10},{10... | collective-permute-start | bytes 172040 | tf_op jit(solution)/shard_map/ppermute | solution.py:317

commit v17 on v16

--- a/solution.py
+++ b/solution.py
@@ -183,8 +183,9 @@
             packed[k, :, tile(c)] = table[c : c + 1]
 
 
-def laid_out(rows, columns, everyone, rowed, groups, before):
+def laid_out(rows, columns, everyone, rowed, slots, parts, before):
     ntarget = rowed.shape[2]
+    groups = slots.shape[0]
     base = lax.axis_index("ja") * (groups * LANES)
     order = pair_order(rows, columns)
     group = lax.broadcasted_iota(jnp.int32, (groups, ntarget), 0)
@@ -213,19 +214,20 @@
         )
         part = jnp.where(found > 0.5, float(r), part)
         spot = spot + found
-    slot = jnp.maximum(spot - 1.0, 0.0).astype(jnp.int32)
+    slots[...] = jnp.maximum(spot - 1.0, 0.0).astype(jnp.int32)
+    parts[...] = part
     for t in range(groups):
-        lanes = jnp.broadcast_to(slot[t : t + 1], (8, LANES))
-        holder = jnp.broadcast_to(part[t : t + 1], (8, LANES))
+        lanes = jnp.broadcast_to(slots[t : t + 1, :], (8, LANES))
+        holder = jnp.broadcast_to(parts[t : t + 1, :], (8, LANES))
         new = before(t)
         for r in range(rows // 2):
             new = jnp.where(holder == float(r), jnp.take_along_axis(forces[r], lanes, axis=1), new)
         yield new
 
 
-def same_kernel(rows, columns, same_core, old, targets_new, placed, rowed):
+def same_kernel(rows, columns, same_core, old, targets_new, placed, rowed, slots, parts):
     zero = jnp.zeros((8, LANES), f32)
-    tiles = laid_out(rows, columns, same_core, rowed, placed.shape[0], lambda t: zero)
+    tiles = laid_out(rows, columns, same_core, rowed, slots, parts, lambda t: zero)
     for t, new in enumerate(tiles):
         placed[t] = new
     me = lax.axis_index("ia") >> 1
@@ -241,18 +243,20 @@
 
 
 def finish_kernel(
-    rows, columns, other_core, placed, pos, vel, acc, jrk, levels, stars_out, stars_new, rowed, sems
+    rows, columns, other_core, placed, pos, vel, acc, jrk, levels, stars_out,
+    stars_new, rowed, slots, parts, steps, sems
 ):
     groups = levels.shape[0]
     piece = groups // PIECES
     copies = []
-    factors = correction_factors(elapsed_of(levels[...]))
-    tiles = laid_out(rows, columns, other_core, rowed, groups, lambda t: placed[t])
+    steps[0], steps[1] = correction_factors(elapsed_of(levels[...]))
+    tiles = laid_out(rows, columns, other_core, rowed, slots, parts, lambda t: placed[t])
     for t, new in enumerate(tiles):
         there = jnp.broadcast_to(new[7:8], (3, LANES)) > 0.5
         x0, v0, a0, j0 = (pos[:, tile(t)], vel[:, tile(t)], acc[:, tile(t)], jrk[:, tile(t)])
         a1, j1 = (new[0:3], new[3:6])
-        x1, v1 = correct(x0, v0, a0, j0, [f[t : t + 1] for f in factors], a1, j1)
+        factors = [jnp.broadcast_to(steps[n, t : t + 1, :], (3, LANES)) for n in range(2)]
+        x1, v1 = correct(x0, v0, a0, j0, factors, a1, j1)
         stars_new[0:3, tile(t)] = jnp.where(there, x1, x0)
         stars_new[3:6, tile(t)] = jnp.where(there, v1, v0)
         stars_new[6:9, tile(t)] = jnp.where(there, a1, a0)
@@ -323,7 +327,11 @@
         ),
         in_specs=[VMEM] * 2,
         out_specs=(VMEM, VMEM),
-        scratch_shapes=[pltpu.VMEM((rows // 2, 8, ntarget), f32)],
+        scratch_shapes=[
+            pltpu.VMEM((rows // 2, 8, ntarget), f32),
+            pltpu.VMEM((groups, LANES), jnp.int32),
+            pltpu.VMEM((groups, LANES), f32),
+        ],
         compiler_params=PARAMS,
         cost_estimate=pl.CostEstimate(
             flops=200 * nlocal, bytes_accessed=4 * 64 * nlocal, transcendentals=0
@@ -338,6 +346,9 @@
         scratch_shapes=[
             pltpu.VMEM((12, nlocal), f32),
             pltpu.VMEM((rows // 2, 8, ntarget), f32),
+            pltpu.VMEM((groups, LANES), jnp.int32),
+            pltpu.VMEM((groups, LANES), f32),
+            pltpu.VMEM((2, groups, LANES), f32),
             pltpu.SemaphoreType.DMA((PIECES,)),
         ],
         compiler_params=PARAMS,

time: 32.1 us -> 32.1 us (level)
  no operation moved by 1% of the time
where the time goes in v17:
time: 32.1 us; the launch traced here: 31.9 us
  blocking collectives  20.8 us (65%)
  Pallas kernels  10.2 us (32%)
  between operations  0.65 us (2%)
    all_to_all x1, blocking collectives, local(): lax.all_to_all(mine, 'ja', 0, 0, axis_index_groups=[column_order(columns)])  11.3 us
    all_to_all x1, blocking collectives, local(): lax.all_to_all(packed, ('ia', 'ja'), 0, 0, axis_index_groups=lists)  9.57 us
    pallas_call x1, Pallas kernels, local(): pl.pallas_call(force_kernel, out_shape=(pltpu.VMEM((rows // 2 * columns,...  6.34 us
    pallas_call x1, Pallas kernels, local(): pl.pallas_call(gather_kernel, out_shape=(pltpu.VMEM((columns, 16, ntarget...  1.49 us
    pallas_call x1, Pallas kernels, local(): pl.pallas_call(functools.partial(finish_kernel, rows, columns), out_shape...  1.34 us
    pallas_call x1, Pallas kernels, local(): pl.pallas_call(functools.partial(same_kernel, rows, columns), out_shape=(...  1.08 us
  transfers between devices with their start and end apart: 1, of which 1 were waited for; matrix products, arithmetic and copies ran while one was open for 0% of the time, Pallas kernels for 3%

profile of v17, /device:TPU:0, one launch (start us, length us, event | category | flops | bytes accessed | tf_op | source)
XLA Modules:
  0.0 31.9 jit_solution(13568646806465728239)
XLA Ops:
  0.6 1.5 %gather.1 = (f32[8,16,128]{2,1,0:T(8,128)S(1)}, f32[3,8192]{1,0:T(4,128)S(1)}, f32[3,8192]{1,0:T(4,128)S(1)}, f32[3,8192]{1,0:T(4,128)S(1)}, f32[3,8192]{1,0:T(4...) custom-call(f32[3,8192]{1,0:T(4,128)} %refs_0_.1, f32[3,8192]{1,0:T(4,128)} %refs_1_.1, ...), custom_call_target="tpu_custom_call" | custom-call | tf_op jit(solution)/shard_map/gather/pallas_call | solution.py:289
  2.1 11.3 %all_to_all.10.gathered = f32[8,16,128]{2,1,0:T(8,128)S(1)} all-to-all(f32[8,16,128]{2,1,0:T(8,128)S(1)} %get-tuple-element.14), channel_id=1, replica_groups={{5,6,7,0,1,2,3,4},{13,14,15,8,9,10,11,12},{21,22,23,16,17,18,19,20},{29..., dimensions={0} | all-to-all | bytes 131072 | tf_op jit(solution)/shard_map/all_to_all | solution.py:301
  13.4 6.3 %forces.1 = (f32[16,1,896]{2,1,0:T(1,128)S(1)}, f32[16,128]{1,0:T(8,128)S(1)}) custom-call(f32[8,16,128]{2,1,0:T(8,128)S(1)} %all_to_all.10.gathered, f32[3,8192]{1,0:T(4,128)S(1)} %get-tuple-element.15.pos, f32[3,8192]{1,0:T(4,128)S(1)} %get-tuple-element.16.vel, f32[3,8192]{1,0:T(4,128)S(1)} %get-tuple-element.17.acc, ...), custom_call_target="tpu_custom_call" | custom-call | tf_op jit(solution)/shard_map/forces/pallas_call | solution.py:302
  19.7 9.6 %all_to_all.11.same_core = f32[16,1,896]{2,1,0:T(1,128)S(1)} all-to-all(f32[16,1,896]{2,1,0:T(1,128)S(1)} %get-tuple-element.22), channel_id=1, replica_groups={{23,22,21,20,19,18,17,16,7,6,5,4,3,2,1,0},{31,30,29,28,27,26,25,24,15,1..., dimensions={0} | all-to-all | bytes 114688 | tf_op jit(solution)/shard_map/all_to_all | solution.py:320
  29.3 0.0 collective-permute-start
  29.3 1.1 %same.1 = (f32[12,128]{1,0:T(8,128)}, f32[64,8,128]{2,1,0:T(8,128)S(1)}) custom-call(f32[16,1,896]{2,1,0:T(1,128)S(1)} %all_to_all.11.same_core, f32[16,128]{1,0:T(8,128)S(1)} %get-tuple-element.23.old), custom_call_target="tpu_custom_call" | custom-call | flops 1638400 | bytes 2097152 | tf_op jit(solution)/shard_map/same/pallas_call | solution.py:322
  30.4 0.2 collective-permute-done.other_core
  30.5 1.3 %finish.1 = f32[12,8192]{1,0:T(8,128)} custom-call(f32[16,1,896]{2,1,0:T(1,128)S(1)} %collective-permute-done.other_core, f32[64,8,128]{2,1,0:T(8,128)S(1)} %get-tuple-element.25.placed, f32[3,8192]{1,0:T(4,128)S(1)} %get-tuple-element.15.pos, f32[3,8192]{1,0:T(4,128)S(1)} %get-tuple-element.16.vel, f32[3,8192]{1,0:T(4,128)S(1)} %get-tuple-element.17.acc, ...), custom_call_target="tpu_custom_call" | custom-call | tf_op jit(solution)/shard_map/finish/pallas_call | solution.py:341
Async XLA Ops:
  29.3 1.2 %collective-permute-start = (f32[16,1,896]{2,1,0:T(1,128)S(1)}, f32[16,1,896]{2,1,0:T(1,128)S(1)}, u32[]{:S(2)}, u32[]{:S(2)}) collective-permute-start(f32[16,1,896]{2,1,0:T(1,128)S(1)} %all_to_all.11.same_core), channel_id=1, source_target_pairs={{0,8},{8,0},{16,24},{24,16},{1,9},{9,1},{17,25},{25,17},{2,10},{10... | collective-permute-start | bytes 172040 | tf_op jit(solution)/shard_map/ppermute | solution.py:321

commit v18 on v16

--- a/solution.py
+++ b/solution.py
@@ -120,7 +120,7 @@
         state[0:3], state[3:6], state[6:9], state[9:12], step_factors(state[12:13])
     )
     columns = jnp.transpose(
-        jnp.concatenate([tpos, tvel, jnp.zeros((LANES - 6, ntarget), f32)], axis=0)
+        jnp.concatenate([tpos, tvel, tpos[0:2]], axis=0)
     )
     for c in range(6):
         targets[c] = jnp.broadcast_to(columns[:, c : c + 1], (ntarget, LANES))
@@ -171,11 +171,11 @@
         return unused
 
     lax.fori_loop(0, ntarget // 8, one_group, 0)
-    lane = lax.broadcasted_iota(jnp.int32, (ntarget, LANES), 1)
-    table = jnp.zeros((ntarget, LANES), f32)
+    lane = lax.broadcasted_iota(jnp.int32, (ntarget, 8), 1)
+    table = jnp.zeros((ntarget, 8), f32)
     for c in range(6):
         table = jnp.where(lane == c, jnp.sum(sums[c], axis=1, keepdims=True), table)
-    table = jnp.transpose(table)[0:8]
+    table = jnp.transpose(table)
     row = lax.broadcasted_iota(jnp.int32, (8, ntarget), 0)
     table = jnp.where(row == 6, active[...].astype(f32), table)
     for k in range(packed.shape[0]):

time: 32.1 us -> 32.1 us (level)
  no operation moved by 1% of the time
where the time goes in v18:
time: 32.1 us; the launch traced here: 31.9 us
  blocking collectives  20.8 us (65%)
  Pallas kernels  10.3 us (32%)
  between operations  0.65 us (2%)
    all_to_all x1, blocking collectives, local(): lax.all_to_all(mine, 'ja', 0, 0, axis_index_groups=[column_order(columns)])  11.3 us
    all_to_all x1, blocking collectives, local(): lax.all_to_all(packed, ('ia', 'ja'), 0, 0, axis_index_groups=lists)  9.57 us
    pallas_call x1, Pallas kernels, local(): pl.pallas_call(force_kernel, out_shape=(pltpu.VMEM((rows // 2 * columns,...  6.33 us
    pallas_call x1, Pallas kernels, local(): pl.pallas_call(gather_kernel, out_shape=(pltpu.VMEM((columns, 16, ntarget...  1.49 us
    pallas_call x1, Pallas kernels, local(): pl.pallas_call(functools.partial(finish_kernel, rows, columns), out_shape...  1.36 us
    pallas_call x1, Pallas kernels, local(): pl.pallas_call(functools.partial(same_kernel, rows, columns), out_shape=(...  1.09 us
  transfers between devices with their start and end apart: 1, of which 1 were waited for; matrix products, arithmetic and copies ran while one was open for 0% of the time, Pallas kernels for 3%

profile of v18, /device:TPU:0, one launch (start us, length us, event | category | flops | bytes accessed | tf_op | source)
XLA Modules:
  0.0 31.9 jit_solution(10737292118522287611)
XLA Ops:
  0.6 1.5 %gather.1 = (f32[8,16,128]{2,1,0:T(8,128)S(1)}, f32[3,8192]{1,0:T(4,128)S(1)}, f32[3,8192]{1,0:T(4,128)S(1)}, f32[3,8192]{1,0:T(4,128)S(1)}, f32[3,8192]{1,0:T(4...) custom-call(f32[3,8192]{1,0:T(4,128)} %refs_0_.1, f32[3,8192]{1,0:T(4,128)} %refs_1_.1, ...), custom_call_target="tpu_custom_call" | custom-call | tf_op jit(solution)/shard_map/gather/pallas_call | solution.py:285
  2.1 11.3 %all_to_all.10.gathered = f32[8,16,128]{2,1,0:T(8,128)S(1)} all-to-all(f32[8,16,128]{2,1,0:T(8,128)S(1)} %get-tuple-element.14), channel_id=1, replica_groups={{5,6,7,0,1,2,3,4},{13,14,15,8,9,10,11,12},{21,22,23,16,17,18,19,20},{29..., dimensions={0} | all-to-all | bytes 131072 | tf_op jit(solution)/shard_map/all_to_all | solution.py:297
  13.4 6.3 %forces.1 = (f32[16,1,896]{2,1,0:T(1,128)S(1)}, f32[16,128]{1,0:T(8,128)S(1)}) custom-call(f32[8,16,128]{2,1,0:T(8,128)S(1)} %all_to_all.10.gathered, f32[3,8192]{1,0:T(4,128)S(1)} %get-tuple-element.15.pos, f32[3,8192]{1,0:T(4,128)S(1)} %get-tuple-element.16.vel, f32[3,8192]{1,0:T(4,128)S(1)} %get-tuple-element.17.acc, ...), custom_call_target="tpu_custom_call" | custom-call | tf_op jit(solution)/shard_map/forces/pallas_call | solution.py:298
  19.7 9.6 %all_to_all.11.same_core = f32[16,1,896]{2,1,0:T(1,128)S(1)} all-to-all(f32[16,1,896]{2,1,0:T(1,128)S(1)} %get-tuple-element.22), channel_id=1, replica_groups={{23,22,21,20,19,18,17,16,7,6,5,4,3,2,1,0},{31,30,29,28,27,26,25,24,15,1..., dimensions={0} | all-to-all | bytes 114688 | tf_op jit(solution)/shard_map/all_to_all | solution.py:316
  29.3 0.0 collective-permute-start
  29.3 1.1 %same.1 = (f32[12,128]{1,0:T(8,128)}, f32[64,8,128]{2,1,0:T(8,128)S(1)}) custom-call(f32[16,1,896]{2,1,0:T(1,128)S(1)} %all_to_all.11.same_core, f32[16,128]{1,0:T(8,128)S(1)} %get-tuple-element.23.old), custom_call_target="tpu_custom_call" | custom-call | flops 1638400 | bytes 2097152 | tf_op jit(solution)/shard_map/same/pallas_call | solution.py:318
  30.4 0.1 collective-permute-done.other_core
  30.5 1.4 %finish.1 = f32[12,8192]{1,0:T(8,128)} custom-call(f32[16,1,896]{2,1,0:T(1,128)S(1)} %collective-permute-done.other_core, f32[64,8,128]{2,1,0:T(8,128)S(1)} %get-tuple-element.25.placed, f32[3,8192]{1,0:T(4,128)S(1)} %get-tuple-element.15.pos, f32[3,8192]{1,0:T(4,128)S(1)} %get-tuple-element.16.vel, f32[3,8192]{1,0:T(4,128)S(1)} %get-tuple-element.17.acc, ...), custom_call_target="tpu_custom_call" | custom-call | tf_op jit(solution)/shard_map/finish/pallas_call | solution.py:333
Async XLA Ops:
  29.3 1.2 %collective-permute-start = (f32[16,1,896]{2,1,0:T(1,128)S(1)}, f32[16,1,896]{2,1,0:T(1,128)S(1)}, u32[]{:S(2)}, u32[]{:S(2)}) collective-permute-start(f32[16,1,896]{2,1,0:T(1,128)S(1)} %all_to_all.11.same_core), channel_id=1, source_target_pairs={{0,8},{8,0},{16,24},{24,16},{1,9},{9,1},{17,25},{25,17},{2,10},{10... | collective-permute-start | bytes 172040 | tf_op jit(solution)/shard_map/ppermute | solution.py:317

commit v19 on v18

--- a/solution.py
+++ b/solution.py
@@ -51,7 +51,8 @@
 
 
 def pair_order(rows, columns):
-    return [(h, c) for h in range(rows // 2 - 1, -1, -1) for c in range(columns - 1, -1, -1)]
+    back = [(h, c) for h in range(rows // 2 - 1, -1, -1) for c in range(columns - 1, -1, -1)]
+    return back[1:] + back[:1]
 
 
 def tile(t):

time: 32.1 us -> 32.8 us (1.022)
  blocking collectives: 20.8 us -> 21.5 us
    all_to_all x1, blocking collectives: 9.57 us -> 10.3 us  [local(): lax.all_to_all(packed, ('ia', 'ja'), 0, 0, axis_index_groups=lists)]
where the time goes in v19:
time: 32.8 us; the launch traced here: 32.6 us
  blocking collectives  21.5 us (66%)
  Pallas kernels  10.3 us (31%)
  between operations  0.65 us (2%)
    all_to_all x1, blocking collectives, local(): lax.all_to_all(mine, 'ja', 0, 0, axis_index_groups=[column_order(columns)])  11.3 us
    all_to_all x1, blocking collectives, local(): lax.all_to_all(packed, ('ia', 'ja'), 0, 0, axis_index_groups=lists)  10.3 us
    pallas_call x1, Pallas kernels, local(): pl.pallas_call(force_kernel, out_shape=(pltpu.VMEM((rows // 2 * columns,...  6.33 us
    pallas_call x1, Pallas kernels, local(): pl.pallas_call(gather_kernel, out_shape=(pltpu.VMEM((columns, 16, ntarget...  1.49 us
    pallas_call x1, Pallas kernels, local(): pl.pallas_call(functools.partial(finish_kernel, rows, columns), out_shape...  1.36 us
    pallas_call x1, Pallas kernels, local(): pl.pallas_call(functools.partial(same_kernel, rows, columns), out_shape=(...  1.09 us
  transfers between devices with their start and end apart: 1, of which 1 were waited for; matrix products, arithmetic and copies ran while one was open for 0% of the time, Pallas kernels for 3%

profile of v19, /device:TPU:0, one launch (start us, length us, event | category | flops | bytes accessed | tf_op | source)
XLA Modules:
  0.0 32.6 jit_solution(3098619686101110821)
XLA Ops:
  0.6 1.5 %gather.1 = (f32[8,16,128]{2,1,0:T(8,128)S(1)}, f32[3,8192]{1,0:T(4,128)S(1)}, f32[3,8192]{1,0:T(4,128)S(1)}, f32[3,8192]{1,0:T(4,128)S(1)}, f32[3,8192]{1,0:T(4...) custom-call(f32[3,8192]{1,0:T(4,128)} %refs_0_.1, f32[3,8192]{1,0:T(4,128)} %refs_1_.1, ...), custom_call_target="tpu_custom_call" | custom-call | tf_op jit(solution)/shard_map/gather/pallas_call | solution.py:286
  2.1 11.3 %all_to_all.10.gathered = f32[8,16,128]{2,1,0:T(8,128)S(1)} all-to-all(f32[8,16,128]{2,1,0:T(8,128)S(1)} %get-tuple-element.14), channel_id=1, replica_groups={{5,6,7,0,1,2,3,4},{13,14,15,8,9,10,11,12},{21,22,23,16,17,18,19,20},{29..., dimensions={0} | all-to-all | bytes 131072 | tf_op jit(solution)/shard_map/all_to_all | solution.py:298
  13.4 6.3 %forces.1 = (f32[16,1,896]{2,1,0:T(1,128)S(1)}, f32[16,128]{1,0:T(8,128)S(1)}) custom-call(f32[8,16,128]{2,1,0:T(8,128)S(1)} %all_to_all.10.gathered, f32[3,8192]{1,0:T(4,128)S(1)} %get-tuple-element.15.pos, f32[3,8192]{1,0:T(4,128)S(1)} %get-tuple-element.16.vel, f32[3,8192]{1,0:T(4,128)S(1)} %get-tuple-element.17.acc, ...), custom_call_target="tpu_custom_call" | custom-call | tf_op jit(solution)/shard_map/forces/pallas_call | solution.py:299
  19.7 10.3 %all_to_all.11.same_core = f32[16,1,896]{2,1,0:T(1,128)S(1)} all-to-all(f32[16,1,896]{2,1,0:T(1,128)S(1)} %get-tuple-element.22), channel_id=1, replica_groups={{22,21,20,19,18,17,16,7,6,5,4,3,2,1,0,23},{30,29,28,27,26,25,24,15,14,1..., dimensions={0} | all-to-all | bytes 114688 | tf_op jit(solution)/shard_map/all_to_all | solution.py:317
  30.0 0.0 collective-permute-start
  30.0 1.1 %same.1 = (f32[12,128]{1,0:T(8,128)}, f32[64,8,128]{2,1,0:T(8,128)S(1)}) custom-call(f32[16,1,896]{2,1,0:T(1,128)S(1)} %all_to_all.11.same_core, f32[16,128]{1,0:T(8,128)S(1)} %get-tuple-element.23.old), custom_call_target="tpu_custom_call" | custom-call | flops 1638400 | bytes 2097152 | tf_op jit(solution)/shard_map/same/pallas_call | solution.py:319
  31.1 0.1 collective-permute-done.other_core
  31.2 1.4 %finish.1 = f32[12,8192]{1,0:T(8,128)} custom-call(f32[16,1,896]{2,1,0:T(1,128)S(1)} %collective-permute-done.other_core, f32[64,8,128]{2,1,0:T(8,128)S(1)} %get-tuple-element.25.placed, f32[3,8192]{1,0:T(4,128)S(1)} %get-tuple-element.15.pos, f32[3,8192]{1,0:T(4,128)S(1)} %get-tuple-element.16.vel, f32[3,8192]{1,0:T(4,128)S(1)} %get-tuple-element.17.acc, ...), custom_call_target="tpu_custom_call" | custom-call | tf_op jit(solution)/shard_map/finish/pallas_call | solution.py:334
Async XLA Ops:
  30.0 1.2 %collective-permute-start = (f32[16,1,896]{2,1,0:T(1,128)S(1)}, f32[16,1,896]{2,1,0:T(1,128)S(1)}, u32[]{:S(2)}, u32[]{:S(2)}) collective-permute-start(f32[16,1,896]{2,1,0:T(1,128)S(1)} %all_to_all.11.same_core), channel_id=1, source_target_pairs={{0,8},{8,0},{16,24},{24,16},{1,9},{9,1},{17,25},{25,17},{2,10},{10... | collective-permute-start | bytes 172040 | tf_op jit(solution)/shard_map/ppermute | solution.py:318

commit v20 on v18

--- a/solution.py
+++ b/solution.py
@@ -258,13 +258,14 @@
         stars_new[6:9, tile(t)] = jnp.where(there, a1, a0)
         stars_new[9:12, tile(t)] = jnp.where(there, j1, j0)
         if (t + 1) % piece == 0:
-            part_of = (slice(None), slice((t + 1 - piece) * LANES, (t + 1) * LANES))
-            copies.append(
-                pltpu.make_async_copy(
-                    stars_new.at[part_of], stars_out.at[part_of], sems.at[len(copies)]
+            lanes = slice((t + 1 - piece) * LANES, (t + 1) * LANES)
+            for part_of in ((slice(0, 8), lanes), (slice(8, 12), lanes)):
+                copies.append(
+                    pltpu.make_async_copy(
+                        stars_new.at[part_of], stars_out.at[part_of], sems.at[len(copies)]
+                    )
                 )
-            )
-            copies[-1].start()
+                copies[-1].start()
     for copy in copies:
         copy.wait()
 
@@ -338,7 +339,7 @@
         scratch_shapes=[
             pltpu.VMEM((12, nlocal), f32),
             pltpu.VMEM((rows // 2, 8, ntarget), f32),
-            pltpu.SemaphoreType.DMA((PIECES,)),
+            pltpu.SemaphoreType.DMA((2 * PIECES,)),
         ],
         compiler_params=PARAMS,
         name="finish",

time: 32.1 us -> 32.2 us (level)
  no operation moved by 1% of the time
where the time goes in v20:
time: 32.2 us; the launch traced here: 32 us
  blocking collectives  20.8 us (65%)
  Pallas kernels  10.3 us (32%)
  between operations  0.65 us (2%)
    all_to_all x1, blocking collectives, local(): lax.all_to_all(mine, 'ja', 0, 0, axis_index_groups=[column_order(columns)])  11.3 us
    all_to_all x1, blocking collectives, local(): lax.all_to_all(packed, ('ia', 'ja'), 0, 0, axis_index_groups=lists)  9.57 us
    pallas_call x1, Pallas kernels, local(): pl.pallas_call(force_kernel, out_shape=(pltpu.VMEM((rows // 2 * columns,...  6.33 us
    pallas_call x1, Pallas kernels, local(): pl.pallas_call(gather_kernel, out_shape=(pltpu.VMEM((columns, 16, ntarget...  1.49 us
    pallas_call x1, Pallas kernels, local(): pl.pallas_call(functools.partial(finish_kernel, rows, columns), out_shape...  1.43 us
    pallas_call x1, Pallas kernels, local(): pl.pallas_call(functools.partial(same_kernel, rows, columns), out_shape=(...  1.09 us
  transfers between devices with their start and end apart: 1, of which 1 were waited for; matrix products, arithmetic and copies ran while one was open for 0% of the time, Pallas kernels for 3%

profile of v20, /device:TPU:0, one launch (start us, length us, event | category | flops | bytes accessed | tf_op | source)
XLA Modules:
  0.0 32.0 jit_solution(7276310363199235715)
XLA Ops:
  0.6 1.5 %gather.1 = (f32[8,16,128]{2,1,0:T(8,128)S(1)}, f32[3,8192]{1,0:T(4,128)S(1)}, f32[3,8192]{1,0:T(4,128)S(1)}, f32[3,8192]{1,0:T(4,128)S(1)}, f32[3,8192]{1,0:T(4...) custom-call(f32[3,8192]{1,0:T(4,128)} %refs_0_.1, f32[3,8192]{1,0:T(4,128)} %refs_1_.1, ...), custom_call_target="tpu_custom_call" | custom-call | tf_op jit(solution)/shard_map/gather/pallas_call | solution.py:286
  2.1 11.3 %all_to_all.10.gathered = f32[8,16,128]{2,1,0:T(8,128)S(1)} all-to-all(f32[8,16,128]{2,1,0:T(8,128)S(1)} %get-tuple-element.14), channel_id=1, replica_groups={{5,6,7,0,1,2,3,4},{13,14,15,8,9,10,11,12},{21,22,23,16,17,18,19,20},{29..., dimensions={0} | all-to-all | bytes 131072 | tf_op jit(solution)/shard_map/all_to_all | solution.py:298
  13.4 6.3 %forces.1 = (f32[16,1,896]{2,1,0:T(1,128)S(1)}, f32[16,128]{1,0:T(8,128)S(1)}) custom-call(f32[8,16,128]{2,1,0:T(8,128)S(1)} %all_to_all.10.gathered, f32[3,8192]{1,0:T(4,128)S(1)} %get-tuple-element.15.pos, f32[3,8192]{1,0:T(4,128)S(1)} %get-tuple-element.16.vel, f32[3,8192]{1,0:T(4,128)S(1)} %get-tuple-element.17.acc, ...), custom_call_target="tpu_custom_call" | custom-call | tf_op jit(solution)/shard_map/forces/pallas_call | solution.py:299
  19.7 9.6 %all_to_all.11.same_core = f32[16,1,896]{2,1,0:T(1,128)S(1)} all-to-all(f32[16,1,896]{2,1,0:T(1,128)S(1)} %get-tuple-element.22), channel_id=1, replica_groups={{23,22,21,20,19,18,17,16,7,6,5,4,3,2,1,0},{31,30,29,28,27,26,25,24,15,1..., dimensions={0} | all-to-all | bytes 114688 | tf_op jit(solution)/shard_map/all_to_all | solution.py:317
  29.3 0.0 collective-permute-start
  29.3 1.1 %same.1 = (f32[12,128]{1,0:T(8,128)}, f32[64,8,128]{2,1,0:T(8,128)S(1)}) custom-call(f32[16,1,896]{2,1,0:T(1,128)S(1)} %all_to_all.11.same_core, f32[16,128]{1,0:T(8,128)S(1)} %get-tuple-element.23.old), custom_call_target="tpu_custom_call" | custom-call | flops 1638400 | bytes 2097152 | tf_op jit(solution)/shard_map/same/pallas_call | solution.py:319
  30.4 0.1 collective-permute-done.other_core
  30.5 1.4 %finish.1 = f32[12,8192]{1,0:T(8,128)} custom-call(f32[16,1,896]{2,1,0:T(1,128)S(1)} %collective-permute-done.other_core, f32[64,8,128]{2,1,0:T(8,128)S(1)} %get-tuple-element.25.placed, f32[3,8192]{1,0:T(4,128)S(1)} %get-tuple-element.15.pos, f32[3,8192]{1,0:T(4,128)S(1)} %get-tuple-element.16.vel, f32[3,8192]{1,0:T(4,128)S(1)} %get-tuple-element.17.acc, ...), custom_call_target="tpu_custom_call" | custom-call | tf_op jit(solution)/shard_map/finish/pallas_call | solution.py:334
Async XLA Ops:
  29.3 1.2 %collective-permute-start = (f32[16,1,896]{2,1,0:T(1,128)S(1)}, f32[16,1,896]{2,1,0:T(1,128)S(1)}, u32[]{:S(2)}, u32[]{:S(2)}) collective-permute-start(f32[16,1,896]{2,1,0:T(1,128)S(1)} %all_to_all.11.same_core), channel_id=1, source_target_pairs={{0,8},{8,0},{16,24},{24,16},{1,9},{9,1},{17,25},{25,17},{2,10},{10... | collective-permute-start | bytes 172040 | tf_op jit(solution)/shard_map/ppermute | solution.py:318
